TPU v7x, 32 devices: a whole 2x2x4 slice. The times are simulated.
32 devices in a mesh: groups: 2 (over x), qry: 16 (over z, y, core).
Axes of the slice: x: 2, y: 2, z: 4, core: 2. Of those that a mesh axis runs over, the one named last changes fastest.
Arguments:
- queries: bfloat16 [32768, 128], P(('groups', 'qry')), parts along dimension 0, may hold values from -1.5 to 1.5
- vectors: bfloat16 [4096, 128], P(('groups', 'qry')), parts along dimension 0, may hold values from -3 to 3
- decoded: bfloat16 [4096, 128], P(('groups', 'qry')), parts along dimension 0, may hold values from -3 to 3
- mask: int32 [128, 8], P(('groups', 'qry')), parts along dimension 0, may hold values from 0 to 1, as said below
Outputs:
- grad_queries: float32 [32768, 128], P(('groups', 'qry')), parts along dimension 0
- grad_vectors: float32 [4096, 128], P(('groups', 'qry')), parts along dimension 0
- grad_decoded: float32 [4096, 128], P(('groups', 'qry')), parts along dimension 0
There are 2 independent parts, one for each index of `groups`. A program takes and returns all parts, laid end to end along the dimension named above; each array names one. Nothing has to cross between parts.
Inputs may be any that keep to these rules, and one draw needn't show every extreme that they name: mask[b, k] is 1 where query block b and vector block k are a sampled pair; how many pairs a query block samples differs from block to block.
All inputs are finite; a program needn't handle non-finite values.
Results may differ from a plain program's by a relative error of at most 0.0012.
Values may be sent and summed in bfloat16 or wider, within the bound.
No kernel may reach another device: no remote copies, remote signals or barrier semaphores. Data moves between devices by JAX's collectives and lax.ppermute only.
A program may use at most 256 MiB of HBM per device.

v0:
```python
import math

import jax
import jax.numpy as jnp
from jax import lax
from jax.sharding import PartitionSpec as P

BLK = 256


def block_grads(query_rows, vec_rows, dec_rows, live, scale):
    score = jnp.dot(query_rows, vec_rows.T, preferred_element_type=jnp.float32)
    error = score - jnp.dot(query_rows, dec_rows.T, preferred_element_type=jnp.float32)
    sig = jax.nn.sigmoid(score)
    pos_weight = (scale * live * (sig * (1.0 - sig) * error * error + 2.0 * sig * error)).astype(
        jnp.bfloat16
    )
    neg_weight = (scale * live * 2.0 * sig * error).astype(jnp.bfloat16)
    grad_q = jnp.dot(pos_weight, vec_rows, preferred_element_type=jnp.float32) - jnp.dot(
        neg_weight, dec_rows, preferred_element_type=jnp.float32
    )
    grad_v = jnp.dot(pos_weight.T, query_rows, preferred_element_type=jnp.float32)
    grad_d = -jnp.dot(neg_weight.T, query_rows, preferred_element_type=jnp.float32)
    return (grad_q, grad_v, grad_d)


def guarded(query_rows, vec_rows, dec_rows, live, scale):
    return block_grads(query_rows, vec_rows, dec_rows, live, scale)


def body(queries, vectors, decoded, mask):
    local_v = vectors.shape[0]
    devices_qry = lax.axis_size("qry")
    total_v = local_v * devices_qry
    scale = 1.0 / math.sqrt(total_v)
    blocks_v = mask.shape[1]
    block_ids = jnp.arange(blocks_v, dtype=jnp.int32)
    row_mask = jnp.repeat(mask.astype(jnp.float32), BLK, axis=0)
    stacked = jnp.stack([vectors, decoded])
    piece = lax.all_gather(stacked, "qry", axis=1, tiled=True)
    count = piece.shape[1]
    columns = jnp.arange(count, dtype=jnp.int32) // BLK
    onehot = (block_ids[:, None] == columns[None, :]).astype(jnp.float32)
    live = jnp.dot(row_mask, onehot, preferred_element_type=jnp.float32)
    grad_q, grad_v, grad_d = guarded(queries, piece[0], piece[1], live, scale)
    terms = jnp.stack([grad_v, grad_d])
    grad_query, terms = (grad_q, terms)
    summed = lax.psum_scatter(terms, "qry", scatter_dimension=1, tiled=True)
    return (grad_query, summed[0], summed[1])


def solution(mesh):
    placed = (
        P(("groups", "qry"), None),
        P(("groups", "qry"), None),
        P(("groups", "qry"), None),
        P(("groups", "qry"), None),
    )
    return jax.shard_map(
        body,
        mesh=mesh,
        in_specs=placed,
        out_specs=(
            P(("groups", "qry"), None),
            P(("groups", "qry"), None),
            P(("groups", "qry"), None),
        ),
        check_vma=False,
    )
```

profile of v0, /device:TPU:0, one launch (start us, length us, event | category | flops | bytes accessed | tf_op | source)
XLA Modules:
  0.0 135.5 jit_solution(1522020767284501486)
XLA Ops:
  7.2 0.0 copy-start
  7.2 0.0 all-gather.2.cloned.1.call-start
  7.2 1.4 %pad_maximum_fusion.1 = bf16[2,128,128]{2,1,0:T(8,128)(2,1)} fusion(bf16[1,128,128]{2,1,0:T(8,128)(2,1)} %bitcast.48, bf16[1,128,128]{2,1,0:T(8,128)(2,1)} %bitcast.49), kind=kLoop, calls=%fused_computation.23 | loop fusion | flops 32768 | bytes 131072 | tf_op jit(solution)/shard_map/stack | solution.py:39
  8.7 0.0 all-gather.2.cloned.1.call-update
  8.7 0.0 reduce-scatter.2.cloned.1.call-start
  8.7 0.7 convert_element_type.10
  9.5 4.5 %fusion.11 = f32[2048,1024]{1,0:T(8,128)} fusion(bf16[1024,8]{1,0:T(8,128)(2,1)S(1)} %bitcast.47, s32[2048]{0:T(1024)S(1)} %add_select_fusion), kind=kOutput, calls=%fused_computation.26 | convolution fusion | flops 33587200 | bytes 8413184 | tf_op jit(solution)/shard_map/dot_general | solution.py:44
  14.0 37.5 %all-gather.2.cloned.1.call-done = bf16[2,2048,128]{2,1,0:T(8,128)(2,1)} async-done(((bf16[2,128,128]{2,1,0:T(8,128)(2,1)}), bf16[2,2048,128]{2,1,0:T(8,128)(2,1)}) %all-gather.2.cloned.1.call-update) | async-done | bytes 1048592 | tf_op jit(solution)/shard_map/all_gather | solution.py:40
  51.5 0.0 copy-done
  51.5 0.0 copy-start.2
  51.5 2.4 %fusion.9 = f32[2048,1024]{1,0:T(8,128)S(1)} fusion(bf16[1024,128]{1,0:T(8,128)(2,1)S(1)} %copy-done, bf16[2,2048,128]{2,1,0:T(8,128)(2,1)} %all-gather.2.cloned.1.call-done), kind=kOutput, calls=%fused_computation.20 | convolution fusion | flops 536870912 | bytes 9175040 | tf_op jit(solution)/shard_map/dot_general | solution.py:12
  53.9 1.1 copy-done.2
  55.0 6.7 %fusion.6 = (bf16[1024,2048]{0,1:T(8,128)(2,1)S(1)}, bf16[1024,2048]{0,1:T(8,128)(2,1)S(1)}) fusion(f32[2048,1024]{1,0:T(8,128)S(1)} %copy-done.2, f32[2048,1024]{1,0:T(8,128)S(1)} %fusion.9, bf16[1024,128]{1,0:T(8,128)(2,1)S(1)} %copy-done, bf16[2,2048,128]{2,1,0:T(8,128)(2,1)} %all-gather.2.cloned.1.call-done), kind=kOutput, calls=%fused_computation.8 | convolution fusion | flops 572522496 | bytes 25952256 | tf_op jit(solution)/shard_map/dot_general | solution.py:13
  61.7 0.0 copy-start.1
  61.7 0.0 copy-start.3
  61.7 0.0 copy-start.4
  61.7 1.2 convolution_bitcast_fusion
  63.0 0.7 copy-done.1
  63.7 1.3 fusion.7
  64.9 0.0 copy-done.3
  64.9 1.5 %pad_maximum_fusion = f32[2,2048,128]{2,1,0:T(8,128)} fusion(f32[1,2048,128]{2,1,0:T(8,128)S(1)} %fusion.7, f32[1,2048,128]{2,1,0:T(8,128)S(1)} %convolution_bitcast_fusion), kind=kLoop, calls=%fused_computation.15 | loop fusion | flops 524288 | bytes 4194304 | tf_op jit(solution)/shard_map/stack | solution.py:46
  66.4 0.0 reduce-scatter.2.cloned.1.call-update
  66.5 0.0 copy-done.4
  66.5 3.5 %fusion.8 = f32[1024,128]{1,0:T(8,128)S(1)} fusion(bf16[1024,2048]{0,1:T(8,128)(2,1)} %copy-done.3, bf16[2,2048,128]{2,1,0:T(8,128)(2,1)S(1)} %copy-done.4), kind=kOutput, calls=%fused_computation.19 | convolution fusion | flops 536870912 | bytes 5242880 | tf_op jit(solution)/shard_map/dot_general | solution.py:19
  69.9 4.4 %convolution_subtract_fusion.1 = f32[1024,128]{1,0:T(8,128)} fusion(f32[1024,128]{1,0:T(8,128)S(1)} %fusion.8, bf16[1024,2048]{0,1:T(8,128)(2,1)} %copy-done.1, bf16[2,2048,128]{2,1,0:T(8,128)(2,1)S(1)} %copy-done.4), kind=kOutput, calls=%fused_computation.16 | convolution fusion | flops 537001984 | bytes 5767168 | tf_op jit(solution)/shard_map/dot_general | solution.py:19
  74.3 52.8 %reduce-scatter.2.cloned.1.call-done = f32[2,128,128]{2,1,0:T(8,128)} async-done(((f32[2,2048,128]{2,1,0:T(8,128)}), f32[2,128,128]{2,1,0:T(8,128)}) %reduce-scatter.2.cloned.1.call-update) | async-done | bytes 131088 | tf_op jit(solution)/shard_map/reduce_scatter | solution.py:48
  127.1 1.5 %slice_bitcast_fusion.6 = (f32[128,128]{1,0:T(8,128)}, f32[128,128]{1,0:T(8,128)}) fusion(f32[2,128,128]{2,1,0:T(8,128)} %reduce-scatter.2.cloned.1.call-done), kind=kLoop, calls=%fused_computation.21 | loop fusion | bytes 262144 | tf_op jit(solution)/shard_map/squeeze | solution.py:49
  (2 shorter events, 0.0 us)
Async XLA Ops:
  7.2 44.3 %copy-start = (bf16[1024,128]{1,0:T(8,128)(2,1)S(1)}, bf16[1024,128]{1,0:T(8,128)(2,1)}, u32[]{:S(2)}) copy-start(bf16[1024,128]{1,0:T(8,128)(2,1)} %param.4) | copy-start | bytes 786436
  7.2 44.3 %all-gather.2.cloned.1.call-start = ((), (), s32[]{:S(2)}) async-start(), calls=%async_computation.1 | async-start | bytes 1114112 | tf_op jit(solution)/shard_map/all_gather | solution.py:40
  8.7 118.4 %reduce-scatter.2.cloned.1.call-start = ((), (), s32[]{:S(2)}) async-start(), calls=%async_computation.2 | async-start | bytes 2228224 | tf_op jit(solution)/shard_map/reduce_scatter | solution.py:48
  51.5 3.5 %copy-start.2 = (f32[2048,1024]{1,0:T(8,128)S(1)}, f32[2048,1024]{1,0:T(8,128)}, u32[]{:S(2)}) copy-start(f32[2048,1024]{1,0:T(8,128)} %fusion.11) | copy-start | bytes 25165828
  61.7 1.9 %copy-start.1 = (bf16[1024,2048]{0,1:T(8,128)(2,1)}, bf16[1024,2048]{0,1:T(8,128)(2,1)S(1)}, u32[]{:S(2)}) copy-start(bf16[1024,2048]{0,1:T(8,128)(2,1)S(1)} %get-tuple-element.3) | copy-start | bytes 12582916
  61.7 3.2 %copy-start.3 = (bf16[1024,2048]{0,1:T(8,128)(2,1)}, bf16[1024,2048]{0,1:T(8,128)(2,1)S(1)}, u32[]{:S(2)}) copy-start(bf16[1024,2048]{0,1:T(8,128)(2,1)S(1)} %get-tuple-element.4) | copy-start | bytes 12582916
  61.7 4.7 %copy-start.4 = (bf16[2,2048,128]{2,1,0:T(8,128)(2,1)S(1)}, bf16[2,2048,128]{2,1,0:T(8,128)(2,1)}, u32[]{:S(2)}) copy-start(bf16[2,2048,128]{2,1,0:T(8,128)(2,1)} %all-gather.2.cloned.1.call-done) | copy-start | bytes 3145732
Sparse Core Ops, SparseCore 0:
  10.8 40.6 all-gather.1
  66.6 60.4 reduce-scatter.1
where the time goes:
time: 136 us; the launch traced here: 135 us
  waiting for transfers between devices  90.3 us (66%)
  matrix products  24 us (18%)
  between operations  14.1 us (10%)
  other arithmetic  3.63 us (3%)
  local copies, waits for them, and re-layouts  3.35 us (2%)
    reduce_scatter x1, waiting for transfers between devices, body(): summed = lax.psum_scatter(terms, 'qry', scatter_dimension=1, tiled=True)  52.8 us
    all_gather x1, waiting for transfers between devices, body(): piece = lax.all_gather(stacked, 'qry', axis=1, tiled=True)  37.5 us
    dot_general x1, matrix products, block_grads(): jnp.dot(query_rows, dec_rows.T, preferred_element_type=jnp.float32)  6.7 us
    dot_general x1, matrix products, body(): live = jnp.dot(row_mask, onehot, preferred_element_type=jnp.float32)  4.52 us
    dot_general x1, matrix products, block_grads(): jnp.dot(neg_weight, dec_rows, preferred_element_type=jnp.float32)  4.36 us
    dot_general x1, matrix products, block_grads(): jnp.dot(pos_weight, vec_rows, preferred_element_type=jnp.float32)  3.46 us
  transfers between devices with their start and end apart: 2, of which 2 were waited for; matrix products, arithmetic and copies ran while one was open for 10% of the time, Pallas kernels for 0%

commit v1 on v0

v1 whole, which is shorter than its diff:
```python
import math

import jax
import jax.numpy as jnp
from jax import lax
from jax.experimental import pallas as pl
from jax.experimental.pallas import tpu as pltpu
from jax.sharding import PartitionSpec as P

BLK = 256
LOG2E = 1.4426950408889634
VMEM = pl.BlockSpec(memory_space=pltpu.VMEM)
F32 = jnp.float32


def params(mib):
    return pltpu.CompilerParams(vmem_limit_bytes=mib << 20)


def pack_kernel(q_ref, v_ref, d_ref, m_ref, qm_ref, vd_ref):
    rows = q_ref.shape[0]
    local_v = v_ref.shape[0]
    qm_ref[0:rows, :] = q_ref[...]
    tail = jnp.zeros((qm_ref.shape[0] - rows, q_ref.shape[1]), F32)
    blocks, cols = m_ref.shape
    padded = jnp.concatenate(
        [m_ref[...].astype(F32), jnp.zeros((blocks, q_ref.shape[1] - cols), F32)], axis=1
    )
    tail = jnp.concatenate([padded, tail[blocks:]], axis=0)
    qm_ref[rows:, :] = tail.astype(jnp.bfloat16)
    vd_ref[0:local_v, :] = v_ref[...]
    vd_ref[local_v:, :] = d_ref[...]


def grads_kernel(rows, blocks, chunks, local_v, scale, *refs):
    qm_refs, vd_refs = refs[:4], refs[4 : 4 + chunks]
    gq_refs, gv_ref = refs[4 + chunks : 8 + chunks], refs[8 + chunks]
    w_ref, live_ref = refs[9 + chunks :]
    me = lax.axis_index("qry")
    wide = 2 * local_v
    group = min(chunks, 4)
    for s in range(chunks):
        w_ref[s * wide : (s + 1) * wide, :] = vd_refs[s][...]
    pad = qm_refs[0].shape[0] - rows
    lanes = lax.broadcasted_iota(jnp.int32, (pad, 128), 1)
    for t in range(4):
        flags = qm_refs[t][rows:, :].astype(F32)
        for s in range(chunks):
            col = (jnp.bitwise_xor(me, 4 * s) * local_v) // BLK
            flag = jnp.sum(jnp.where(lanes == col, flags, 0.0), axis=1, keepdims=True)
            live_ref[s, t * pad : (t + 1) * pad, :] = jnp.broadcast_to(
                flag * (-2.0 * scale), (pad, 128)
            )
    gv_ref[...] = jnp.zeros_like(gv_ref)

    def tile(t, r0, height, g):
        q = qm_refs[t][pl.ds(r0, height), :]
        w = w_ref[pl.ds(g * group * wide, group * wide), :]
        both = lax.dot_general(q, w, (((1,), (1,)), ((), ())), preferred_element_type=F32)
        row_blocks = []
        for b in range(height // BLK):
            weights = []
            for c in range(group):
                score = both[b * BLK : (b + 1) * BLK, c * wide : c * wide + local_v]
                error = score - both[b * BLK : (b + 1) * BLK, c * wide + local_v : (c + 1) * wide]
                m = live_ref[g * group + c, pl.ds(t * pad + r0 // BLK + b, 1), :]
                sig = 1.0 / (1.0 + jnp.exp2(score * (-LOG2E)))
                neg = (error * m) * sig
                pos = neg * (error * (0.5 * sig - 0.5) - 1.0)
                weights += [pos.astype(jnp.bfloat16), neg.astype(jnp.bfloat16)]
            row_blocks.append(jnp.concatenate(weights, axis=1))
        weights = jnp.concatenate(row_blocks, axis=0)
        part = jnp.dot(weights, w, preferred_element_type=F32)
        if chunks == group:
            gq_refs[t][pl.ds(r0, height), :] = part
        else:
            gq_refs[t][pl.ds(r0, height), :] = part + jnp.where(
                g == 0, 0.0, gq_refs[t][pl.ds(r0, height), :]
            )
        gv_ref[g] += jnp.dot(q.T, weights, preferred_element_type=F32)

    height = 2 * BLK if rows % (2 * BLK) == 0 else BLK
    for t in range(4):
        if chunks == group:
            for i in range(rows // height):
                tile(t, i * height, height, 0)
        else:

            def step(n, carry, t=t):
                g = n // (rows // height)
                r0 = pl.multiple_of((n % (rows // height)) * height, height)
                tile(t, r0, height, g)
                return carry

            lax.fori_loop(0, (chunks // group) * (rows // height), step, 0)


def core_sum_kernel(own_ref, y_ref, got_ref, own_out, y_out):
    rows = own_ref.shape[0]
    own_out[...] = own_ref[...] + got_ref[0:rows, :]
    y_out[...] = y_ref[...] + got_ref[rows:, :]


def finish_kernel(n, *refs):
    own_ref, got_ref = refs[:2]
    terms = refs[2 : 2 + n]
    gq_out, gv_out, gd_out = refs[2 + n :]
    gq_out[...] = own_ref[...] + got_ref[...]
    total = terms[0][...]
    for term in terms[1:]:
        total = total + term[...]
    local_v = gv_out.shape[0]
    gv_out[...] = total[:, :local_v].T
    gd_out[...] = total[:, local_v:].T


def body(queries, vectors, decoded, mask):
    rows, dim = queries.shape
    local_v = vectors.shape[0]
    blocks, blocks_v = mask.shape
    n = lax.axis_size("qry")
    chunks = n // 4
    wide = 2 * local_v
    scale = 1.0 / math.sqrt(local_v * n)
    pad = -(-blocks // 16) * 16
    bf = jnp.bfloat16

    def swap(x, bit):
        return lax.ppermute(x, "qry", [(i, i ^ bit) for i in range(n)])

    qm, vd = pl.pallas_call(
        pack_kernel,
        out_shape=(
            jax.ShapeDtypeStruct((rows + pad, dim), bf),
            jax.ShapeDtypeStruct((wide, dim), bf),
        ),
        in_specs=[VMEM] * 4,
        out_specs=(VMEM, VMEM),
        compiler_params=params(8),
        name="pack",
    )(queries, vectors, decoded, mask)
    qm_y = swap(qm, 2)
    vds = [vd] + [swap(vd, 4 * s) for s in range(1, chunks)]
    qm_c = swap(qm, 1)
    qm_yc = swap(qm_y, 1)
    group = min(chunks, 4)
    row_out = jax.ShapeDtypeStruct((rows, dim), F32)
    gq_own, gq_c, gq_y, gq_yc, gv = pl.pallas_call(
        lambda *refs: grads_kernel(rows, blocks, chunks, local_v, scale, *refs),
        out_shape=(row_out,) * 4
        + (jax.ShapeDtypeStruct((chunks // group, dim, group * wide), F32),),
        in_specs=[VMEM] * (4 + chunks),
        out_specs=(VMEM,) * 5,
        scratch_shapes=[
            pltpu.VMEM((chunks * wide, dim), bf),
            pltpu.VMEM((chunks, 4 * pad, 128), F32),
        ],
        compiler_params=params(40),
        name="grads",
    )(qm, qm_c, qm_y, qm_yc, *vds)
    terms = [
        gv[s // group, :, (s % group) * wide : (s % group + 1) * wide] for s in range(chunks)
    ]
    got_c = swap(jnp.concatenate([gq_c, gq_yc], axis=0), 1)
    gq_own, gq_y = pl.pallas_call(
        core_sum_kernel,
        out_shape=(row_out,) * 2,
        in_specs=[VMEM] * 3,
        out_specs=(VMEM,) * 2,
        compiler_params=params(16),
        name="core_sum",
    )(gq_own, gq_y, got_c)
    got_y = swap(gq_y, 2)
    terms = [terms[0]] + [swap(terms[s], 4 * s) for s in range(1, chunks)]
    vec_out = jax.ShapeDtypeStruct((local_v, dim), F32)
    return pl.pallas_call(
        lambda *refs: finish_kernel(chunks, *refs),
        out_shape=(row_out, vec_out, vec_out),
        in_specs=[VMEM] * (2 + chunks),
        out_specs=(VMEM,) * 3,
        compiler_params=params(16),
        name="finish",
    )(gq_own, got_y, *terms)


def solution(mesh):
    placed = P(("groups", "qry"), None)
    return jax.shard_map(
        body,
        mesh=mesh,
        in_specs=(placed,) * 4,
        out_specs=(placed,) * 3,
        check_vma=False,
    )
```

time: 136 us -> 49.4 us (0.36)
  waiting for transfers between devices: 90.3 us -> 24.6 us
  matrix products: 24 us -> 0 us
  starting transfers between devices: 0.08 us -> 13.5 us
  between operations: 14.1 us -> 0.69 us
  Pallas kernels: 0 us -> 7.03 us
  other arithmetic: 3.63 us -> 0.07 us
    reduce_scatter x1 -> x0, waiting for transfers between devices: 52.8 us -> none  [body(): summed = lax.psum_scatter(terms, 'qry', scatter_dimension=1, tiled=True)]
    all_gather x1 -> x0, waiting for transfers between devices: 37.5 us -> none  [body(): piece = lax.all_gather(stacked, 'qry', axis=1, tiled=True)]
    ppermute x0 -> x11, waiting for transfers between devices: none -> 24.6 us  [swap(): return lax.ppermute(x, 'qry', [(i, i ^ bit) for i in range(n)])]
    dot_general x7 -> x0, matrix products: 24 us -> none  [the longest x1 6.7 us: block_grads(): jnp.dot(query_rows, dec_rows.T, preferred_element_type=jnp.float32)]
    ppermute x0 -> x11, starting transfers between devices: none -> 13.5 us  [swap(): return lax.ppermute(x, 'qry', [(i, i ^ bit) for i in range(n)])]
    pallas_call x0 -> x4, Pallas kernels: none -> 7.03 us  [the longest x1 5.99 us: body(): pl.pallas_call(lambda *refs: grads_kernel(rows, blocks, chunks, local_v,...]
    another operation x2 -> x0, other arithmetic: 2.94 us -> none  [the longest x1 1.49 us: body(): terms = jnp.stack([grad_v, grad_d])]
    squeeze x1, local copies, waits for them, and re-layouts: 1.53 us -> 0.03 us  [body(): gv[s // group, :, s % group * wide:(s % group + 1) * wide]]
  transfers between devices with their start and end apart: 2 -> 11, of which waited for: 2 -> 6; matrix products, arithmetic and copies ran while one was open for 10% -> 0% of each run, Pallas kernels for 0% -> 0%
where the time goes in v1:
time: 49.4 us; the launch traced here: 49.1 us
  waiting for transfers between devices  24.6 us (50%)
  starting transfers between devices  13.5 us (27%)
  Pallas kernels  7.03 us (14%)
  local copies, waits for them, and re-layouts  3.17 us (6%)
  between operations  0.69 us (1%)
    ppermute x11, waiting for transfers between devices, swap(): return lax.ppermute(x, 'qry', [(i, i ^ bit) for i in range(n)])  24.6 us
    ppermute x11, starting transfers between devices, swap(): return lax.ppermute(x, 'qry', [(i, i ^ bit) for i in range(n)])  13.5 us
    pallas_call x1, Pallas kernels, body(): pl.pallas_call(lambda *refs: grads_kernel(rows, blocks, chunks, local_v,...  5.99 us
    unnamed x8, local copies, waits for them, and re-layouts  3.14 us
  transfers between devices with their start and end apart: 11, of which 6 were waited for; matrix products, arithmetic and copies ran while one was open for 0% of the time, Pallas kernels for 0%

profile of v1, /device:TPU:0, one launch (start us, length us, event | category | flops | bytes accessed | tf_op | source)
XLA Modules:
  0.0 49.1 jit_solution(4020102137754872892)
XLA Ops:
  0.6 0.0 copy-start
  0.6 0.9 %copy-done = bf16[1024,128]{1,0:T(8,128)(2,1)S(1)} copy-done((bf16[1024,128]{1,0:T(8,128)(2,1)S(1)}, bf16[1024,128]{1,0:T(8,128)(2,1)}, u32[]{:S(2)}) %copy-start) | copy-done | bytes 262168
  1.6 0.0 copy-start.1
  1.6 0.8 %copy-done.1 = bf16[128,128]{1,0:T(8,128)(2,1)S(1)} copy-done((bf16[128,128]{1,0:T(8,128)(2,1)S(1)}, bf16[128,128]{1,0:T(8,128)(2,1)}, u32[]{:S(2)}) %copy-start.1) | copy-done | bytes 32792
  2.3 0.0 copy-start.2
  2.3 0.8 %copy-done.2 = bf16[128,128]{1,0:T(8,128)(2,1)S(1)} copy-done((bf16[128,128]{1,0:T(8,128)(2,1)S(1)}, bf16[128,128]{1,0:T(8,128)(2,1)}, u32[]{:S(2)}) %copy-start.2) | copy-done | bytes 32792
  3.1 0.0 copy-start.3
  3.1 0.7 %copy-done.3 = s32[4,8]{1,0:T(4,128)S(1)} copy-done((s32[4,8]{1,0:T(4,128)S(1)}, s32[4,8]{1,0:T(4,128)}, u32[]{:S(2)}) %copy-start.3) | copy-done | bytes 152
  3.8 3.0 %collective-permute-start.1 = (bf16[1040,128]{1,0:T(8,128)(2,1)S(1)}, bf16[1040,128]{1,0:T(8,128)(2,1)S(1)}, u32[]{:S(2)}, u32[]{:S(2)}) collective-permute-start(bf16[1040,128]{1,0:T(8,128)(2,1)S(1)} %get-tuple-element.12.refs_0_), channel_id=1, source_target_pairs={{0,2},{1,3},{2,0},{3,1},{4,6},{5,7},{6,4},{7,5},{8,10},{9,11},{10,... | collective-permute-start | bytes 798728 | tf_op jit(solution)/shard_map/ppermute | solution.py:129
  6.8 0.0 collective-permute-start
  6.8 6.4 %collective-permute-done.1.refs_2_ = bf16[1040,128]{1,0:T(8,128)(2,1)S(1)} collective-permute-done((bf16[1040,128]{1,0:T(8,128)(2,1)S(1)}, bf16[1040,128]{1,0:T(8,128)(2,1)S(1)}, u32[]{:S(2)}, u32[]{:S(2)}) %collective-permute-start.1) | collective-permute-done | bytes 266272 | tf_op jit(solution)/shard_map/ppermute | solution.py:129
  13.2 0.0 collective-permute-start.2
  13.2 3.8 %collective-permute-start.5 = (bf16[256,128]{1,0:T(8,128)(2,1)S(1)}, bf16[256,128]{1,0:T(8,128)(2,1)S(1)}, u32[]{:S(2)}, u32[]{:S(2)}) collective-permute-start(bf16[256,128]{1,0:T(8,128)(2,1)S(1)} %get-tuple-element.13.refs_4_), channel_id=1, source_target_pairs={{0,12},{1,13},{2,14},{3,15},{4,8},{5,9},{6,10},{7,11},{8,4},{9,5},... | collective-permute-start | bytes 196616 | tf_op jit(solution)/shard_map/ppermute | solution.py:129
  17.1 0.0 collective-permute-start.4
  17.1 0.6 %collective-permute-start.3 = (bf16[256,128]{1,0:T(8,128)(2,1)S(1)}, bf16[256,128]{1,0:T(8,128)(2,1)S(1)}, u32[]{:S(2)}, u32[]{:S(2)}) collective-permute-start(bf16[256,128]{1,0:T(8,128)(2,1)S(1)} %get-tuple-element.13.refs_4_), channel_id=1, source_target_pairs={{0,4},{1,5},{2,6},{3,7},{4,0},{5,1},{6,2},{7,3},{8,12},{9,13},{10,... | collective-permute-start | bytes 196616 | tf_op jit(solution)/shard_map/ppermute | solution.py:129
  17.6 2.4 %collective-permute-done.5.refs_7_ = bf16[256,128]{1,0:T(8,128)(2,1)S(1)} collective-permute-done((bf16[256,128]{1,0:T(8,128)(2,1)S(1)}, bf16[256,128]{1,0:T(8,128)(2,1)S(1)}, u32[]{:S(2)}, u32[]{:S(2)}) %collective-permute-start.5) | collective-permute-done | bytes 65568 | tf_op jit(solution)/shard_map/ppermute | solution.py:129
  20.0 3.2 %collective-permute-done.4.refs_6_ = bf16[256,128]{1,0:T(8,128)(2,1)S(1)} collective-permute-done((bf16[256,128]{1,0:T(8,128)(2,1)S(1)}, bf16[256,128]{1,0:T(8,128)(2,1)S(1)}, u32[]{:S(2)}, u32[]{:S(2)}) %collective-permute-start.4) | collective-permute-done | bytes 65568 | tf_op jit(solution)/shard_map/ppermute | solution.py:129
  23.2 0.0 collective-permute-done.3.refs_5_
  23.2 0.0 collective-permute-done.refs_1_
  23.2 0.0 collective-permute-done.2.refs_3_
  23.2 6.0 %grads.1 = (f32[1024,128]{1,0:T(8,128)S(1)}, f32[1024,128]{1,0:T(8,128)S(1)}, f32[1024,128]{1,0:T(8,128)S(1)}, f32[1024,128]{1,0:T(8,128)S(1)}, f32[1,128,1024]{2,1,0:T(8,128)S(1)}) custom-call(bf16[1040,128]{1,0:T(8,128)(2,1)S(1)} %get-tuple-element.12.refs_0_, bf16[1040,128]{1,0:T(8,128)(2,1)S(1)} %collective-permute-done.refs_1_, ...), custom_call_target="tpu_custom_call" | custom-call | tf_op jit(solution)/shard_map/grads/pallas_call | solution.py:148
  29.2 0.1 pad_maximum_fusion
  29.3 0.1 collective-permute-start.6
  29.4 2.6 %collective-permute-done.6.got_ref = f32[2048,128]{1,0:T(8,128)S(1)} collective-permute-done((f32[2048,128]{1,0:T(8,128)S(1)}, f32[2048,128]{1,0:T(8,128)S(1)}, u32[]{:S(2)}, u32[]{:S(2)}) %collective-permute-start.6) | collective-permute-done | bytes 1048608 | tf_op jit(solution)/shard_map/ppermute | solution.py:129
  32.0 0.1 core_sum.1
  32.1 1.6 %collective-permute-start.7 = (f32[1024,128]{1,0:T(8,128)S(1)}, f32[1024,128]{1,0:T(8,128)S(1)}, u32[]{:S(2)}, u32[]{:S(2)}) collective-permute-start(f32[1024,128]{1,0:T(8,128)S(1)} %get-tuple-element.19), channel_id=1, source_target_pairs={{0,2},{1,3},{2,0},{3,1},{4,6},{5,7},{6,4},{7,5},{8,10},{9,11},{10,... | collective-permute-start | bytes 1572872 | tf_op jit(solution)/shard_map/ppermute | solution.py:129
  33.7 2.5 %collective-permute-start.10 = (f32[128,256]{1,0:T(8,128)S(1)}, f32[128,256]{1,0:T(8,128)S(1)}, u32[]{:S(2)}, u32[]{:S(2)}) collective-permute-start(f32[128,256]{1,0:T(8,128)S(1)} %get-tuple-element.21), channel_id=1, source_target_pairs={{0,12},{1,13},{2,14},{3,15},{4,8},{5,9},{6,10},{7,11},{8,4},{9,5},... | collective-permute-start | bytes 393224 | tf_op jit(solution)/shard_map/ppermute | solution.py:129
  36.3 0.2 collective-permute-start.9
  36.5 1.7 %collective-permute-start.8 = (f32[128,256]{1,0:T(8,128)S(1)}, f32[128,256]{1,0:T(8,128)S(1)}, u32[]{:S(2)}, u32[]{:S(2)}) collective-permute-start(f32[128,256]{1,0:T(8,128)S(1)} %get-tuple-element.23), channel_id=1, source_target_pairs={{0,4},{1,5},{2,6},{3,7},{4,0},{5,1},{6,2},{7,3},{8,12},{9,13},{10,... | collective-permute-start | bytes 393224 | tf_op jit(solution)/shard_map/ppermute | solution.py:129
  38.2 3.8 %collective-permute-done.10.refs_5_ = f32[128,256]{1,0:T(8,128)S(1)} collective-permute-done((f32[128,256]{1,0:T(8,128)S(1)}, f32[128,256]{1,0:T(8,128)S(1)}, u32[]{:S(2)}, u32[]{:S(2)}) %collective-permute-start.10) | collective-permute-done | bytes 131104 | tf_op jit(solution)/shard_map/ppermute | solution.py:129
  42.0 6.1 %collective-permute-done.9.refs_4_ = f32[128,256]{1,0:T(8,128)S(1)} collective-permute-done((f32[128,256]{1,0:T(8,128)S(1)}, f32[128,256]{1,0:T(8,128)S(1)}, u32[]{:S(2)}, u32[]{:S(2)}) %collective-permute-start.9) | collective-permute-done | bytes 131104 | tf_op jit(solution)/shard_map/ppermute | solution.py:129
  48.2 0.0 collective-permute-done.8.refs_3_
  48.2 0.0 collective-permute-done.7.refs_1_
  48.2 0.9 %finish.1 = (f32[1024,128]{1,0:T(8,128)}, f32[128,128]{1,0:T(8,128)}, f32[128,128]{1,0:T(8,128)}) custom-call(f32[1024,128]{1,0:T(8,128)S(1)} %get-tuple-element.18.refs_0_, f32[1024,128]{1,0:T(8,128)S(1)} %collective-permute-done.7.refs_1_, f32[128,256]{1,0:T(8,128)S(1)} %get-tuple-element.24.refs_2_, f32[128,256]{1,0:T(8,128)S(1)} %collective-permute-done.8.refs_3_, ...), custom_call_target="tpu_custom_call" | custom-call | tf_op jit(solution)/shard_map/finish/pallas_call | solution.py:176
  (2 shorter events, 0.1 us)
Async XLA Ops:
  0.6 1.0 %copy-start = (bf16[1024,128]{1,0:T(8,128)(2,1)S(1)}, bf16[1024,128]{1,0:T(8,128)(2,1)}, u32[]{:S(2)}) copy-start(bf16[1024,128]{1,0:T(8,128)(2,1)} %q_ref.1) | copy-start | bytes 786436
  1.6 0.8 %copy-start.1 = (bf16[128,128]{1,0:T(8,128)(2,1)S(1)}, bf16[128,128]{1,0:T(8,128)(2,1)}, u32[]{:S(2)}) copy-start(bf16[128,128]{1,0:T(8,128)(2,1)} %v_ref.1) | copy-start | bytes 98308
  2.3 0.8 %copy-start.2 = (bf16[128,128]{1,0:T(8,128)(2,1)S(1)}, bf16[128,128]{1,0:T(8,128)(2,1)}, u32[]{:S(2)}) copy-start(bf16[128,128]{1,0:T(8,128)(2,1)} %d_ref.1) | copy-start | bytes 98308
  3.1 0.7 %copy-start.3 = (s32[4,8]{1,0:T(4,128)S(1)}, s32[4,8]{1,0:T(4,128)}, u32[]{:S(2)}) copy-start(s32[4,8]{1,0:T(4,128)} %m_ref.1) | copy-start | bytes 388
  3.8 9.4 %collective-permute-start.1 = (bf16[1040,128]{1,0:T(8,128)(2,1)S(1)}, bf16[1040,128]{1,0:T(8,128)(2,1)S(1)}, u32[]{:S(2)}, u32[]{:S(2)}) collective-permute-start(bf16[1040,128]{1,0:T(8,128)(2,1)S(1)} %get-tuple-element.12.refs_0_), channel_id=1, source_target_pairs={{0,2},{1,3},{2,0},{3,1},{4,6},{5,7},{6,4},{7,5},{8,10},{9,11},{10,... | collective-permute-start | bytes 798728 | tf_op jit(solution)/shard_map/ppermute | solution.py:129
  6.8 16.4 %collective-permute-start = (bf16[1040,128]{1,0:T(8,128)(2,1)S(1)}, bf16[1040,128]{1,0:T(8,128)(2,1)S(1)}, u32[]{:S(2)}, u32[]{:S(2)}) collective-permute-start(bf16[1040,128]{1,0:T(8,128)(2,1)S(1)} %get-tuple-element.12.refs_0_), channel_id=1, source_target_pairs={{0,1},{1,0},{2,3},{3,2},{4,5},{5,4},{6,7},{7,6},{8,9},{9,8},{10,11... | collective-permute-start | bytes 798728 | tf_op jit(solution)/shard_map/ppermute | solution.py:129
  13.2 10.0 %collective-permute-start.2 = (bf16[1040,128]{1,0:T(8,128)(2,1)S(1)}, bf16[1040,128]{1,0:T(8,128)(2,1)S(1)}, u32[]{:S(2)}, u32[]{:S(2)}) collective-permute-start(bf16[1040,128]{1,0:T(8,128)(2,1)S(1)} %collective-permute-done.1.refs_2_), channel_id=1, source_target_pairs={{0,1},{1,0},{2,3},{3,2},{4,5},{5,4},{6,7},{7,6},{8,9},{9,8},{10,11... | collective-permute-start | bytes 798728 | tf_op jit(solution)/shard_map/ppermute | solution.py:129
  13.2 6.8 %collective-permute-start.5 = (bf16[256,128]{1,0:T(8,128)(2,1)S(1)}, bf16[256,128]{1,0:T(8,128)(2,1)S(1)}, u32[]{:S(2)}, u32[]{:S(2)}) collective-permute-start(bf16[256,128]{1,0:T(8,128)(2,1)S(1)} %get-tuple-element.13.refs_4_), channel_id=1, source_target_pairs={{0,12},{1,13},{2,14},{3,15},{4,8},{5,9},{6,10},{7,11},{8,4},{9,5},... | collective-permute-start | bytes 196616 | tf_op jit(solution)/shard_map/ppermute | solution.py:129
  17.1 6.1 %collective-permute-start.4 = (bf16[256,128]{1,0:T(8,128)(2,1)S(1)}, bf16[256,128]{1,0:T(8,128)(2,1)S(1)}, u32[]{:S(2)}, u32[]{:S(2)}) collective-permute-start(bf16[256,128]{1,0:T(8,128)(2,1)S(1)} %get-tuple-element.13.refs_4_), channel_id=1, source_target_pairs={{0,8},{1,9},{2,10},{3,11},{4,12},{5,13},{6,14},{7,15},{8,0},{9,1},... | collective-permute-start | bytes 196616 | tf_op jit(solution)/shard_map/ppermute | solution.py:129
  17.1 6.1 %collective-permute-start.3 = (bf16[256,128]{1,0:T(8,128)(2,1)S(1)}, bf16[256,128]{1,0:T(8,128)(2,1)S(1)}, u32[]{:S(2)}, u32[]{:S(2)}) collective-permute-start(bf16[256,128]{1,0:T(8,128)(2,1)S(1)} %get-tuple-element.13.refs_4_), channel_id=1, source_target_pairs={{0,4},{1,5},{2,6},{3,7},{4,0},{5,1},{6,2},{7,3},{8,12},{9,13},{10,... | collective-permute-start | bytes 196616 | tf_op jit(solution)/shard_map/ppermute | solution.py:129
  29.3 2.7 %collective-permute-start.6 = (f32[2048,128]{1,0:T(8,128)S(1)}, f32[2048,128]{1,0:T(8,128)S(1)}, u32[]{:S(2)}, u32[]{:S(2)}) collective-permute-start(f32[2048,128]{1,0:T(8,128)S(1)} %pad_maximum_fusion), channel_id=1, source_target_pairs={{0,1},{1,0},{2,3},{3,2},{4,5},{5,4},{6,7},{7,6},{8,9},{9,8},{10,11... | collective-permute-start | bytes 3145736 | tf_op jit(solution)/shard_map/ppermute | solution.py:129
  32.1 16.0 %collective-permute-start.7 = (f32[1024,128]{1,0:T(8,128)S(1)}, f32[1024,128]{1,0:T(8,128)S(1)}, u32[]{:S(2)}, u32[]{:S(2)}) collective-permute-start(f32[1024,128]{1,0:T(8,128)S(1)} %get-tuple-element.19), channel_id=1, source_target_pairs={{0,2},{1,3},{2,0},{3,1},{4,6},{5,7},{6,4},{7,5},{8,10},{9,11},{10,... | collective-permute-start | bytes 1572872 | tf_op jit(solution)/shard_map/ppermute | solution.py:129
  33.7 8.3 %collective-permute-start.10 = (f32[128,256]{1,0:T(8,128)S(1)}, f32[128,256]{1,0:T(8,128)S(1)}, u32[]{:S(2)}, u32[]{:S(2)}) collective-permute-start(f32[128,256]{1,0:T(8,128)S(1)} %get-tuple-element.21), channel_id=1, source_target_pairs={{0,12},{1,13},{2,14},{3,15},{4,8},{5,9},{6,10},{7,11},{8,4},{9,5},... | collective-permute-start | bytes 393224 | tf_op jit(solution)/shard_map/ppermute | solution.py:129
  36.3 11.9 %collective-permute-start.9 = (f32[128,256]{1,0:T(8,128)S(1)}, f32[128,256]{1,0:T(8,128)S(1)}, u32[]{:S(2)}, u32[]{:S(2)}) collective-permute-start(f32[128,256]{1,0:T(8,128)S(1)} %get-tuple-element.22), channel_id=1, source_target_pairs={{0,8},{1,9},{2,10},{3,11},{4,12},{5,13},{6,14},{7,15},{8,0},{9,1},... | collective-permute-start | bytes 393224 | tf_op jit(solution)/shard_map/ppermute | solution.py:129
  36.5 11.7 %collective-permute-start.8 = (f32[128,256]{1,0:T(8,128)S(1)}, f32[128,256]{1,0:T(8,128)S(1)}, u32[]{:S(2)}, u32[]{:S(2)}) collective-permute-start(f32[128,256]{1,0:T(8,128)S(1)} %get-tuple-element.23), channel_id=1, source_target_pairs={{0,4},{1,5},{2,6},{3,7},{4,0},{5,1},{6,2},{7,3},{8,12},{9,13},{10,... | collective-permute-start | bytes 393224 | tf_op jit(solution)/shard_map/ppermute | solution.py:129

commit v2 on v1

v2 whole, which is shorter than its diff:
```python
import math

import jax
import jax.numpy as jnp
from jax import lax
from jax.experimental import pallas as pl
from jax.experimental.pallas import tpu as pltpu
from jax.sharding import PartitionSpec as P

BLK = 256
LOG2E = 1.4426950408889634
LEVELS = 32000.0
TAIL = 16
VMEM = pl.BlockSpec(memory_space=pltpu.VMEM)
HBM = pl.BlockSpec(memory_space=pltpu.HBM)
F32 = jnp.float32
BF16 = jnp.bfloat16
I16 = jnp.int16


def params(mib):
    return pltpu.CompilerParams(vmem_limit_bytes=mib << 20)


def cost(flops, nbytes):
    return pl.CostEstimate(flops=flops, bytes_accessed=nbytes, transcendentals=0)


def encode(x):
    top = jnp.max(jnp.abs(x), axis=0, keepdims=True)
    exponent = jnp.ceil(jnp.log2(jnp.maximum(top, 1e-30)))
    scaled = jnp.round(x * (jnp.exp2(-exponent) * LEVELS))
    return scaled.astype(jnp.int32).astype(I16), exponent


def decode(x, exponent):
    return x.astype(jnp.int32).astype(F32) * (jnp.exp2(exponent) * (1.0 / LEVELS))


def tail_of(exponents):
    rows = jnp.concatenate(exponents, axis=0)
    rest = jnp.zeros((TAIL - rows.shape[0], rows.shape[1]), F32)
    return jnp.concatenate([rows, rest], axis=0).astype(jnp.int32).astype(I16)


def pack_kernel(q_hbm, v_hbm, d_hbm, m_hbm, qm_ref, vd_ref, m_ref, sems):
    rows = q_hbm.shape[0]
    local_v = v_hbm.shape[0]
    copies = [
        pltpu.make_async_copy(m_hbm, m_ref, sems.at[0]),
        pltpu.make_async_copy(v_hbm, vd_ref.at[pl.ds(0, local_v)], sems.at[1]),
        pltpu.make_async_copy(d_hbm, vd_ref.at[pl.ds(local_v, local_v)], sems.at[2]),
        pltpu.make_async_copy(q_hbm, qm_ref.at[pl.ds(0, rows)], sems.at[3]),
    ]
    for copy in copies:
        copy.start()
    copies[0].wait()
    blocks, cols = m_ref.shape
    pad, lanes = qm_ref.shape[0] - rows, qm_ref.shape[1]
    flags = jnp.concatenate([m_ref[...].astype(F32), jnp.zeros((blocks, lanes - cols), F32)], axis=1)
    flags = jnp.concatenate([flags, jnp.zeros((pad - blocks, lanes), F32)], axis=0)
    qm_ref[rows:, :] = flags.astype(BF16)
    for copy in copies[1:]:
        copy.wait()


def tiles(rows, chunks, local_v, scale, qm_refs, vd_refs, gq_refs, gv_ref, w_ref, live_ref):
    me = lax.axis_index("qry")
    wide = 2 * local_v
    group = min(chunks, 4)
    for s in range(chunks):
        w_ref[s * wide : (s + 1) * wide, :] = vd_refs[s][...]
    pad = qm_refs[0].shape[0] - rows
    lanes = lax.broadcasted_iota(jnp.int32, (pad, 128), 1)
    for t, qm_ref in enumerate(qm_refs):
        flags = qm_ref[rows:, :].astype(F32)
        for s in range(chunks):
            col = (jnp.bitwise_xor(me, 4 * s) * local_v) // BLK
            flag = jnp.sum(jnp.where(lanes == col, flags, 0.0), axis=1, keepdims=True)
            live_ref[s, t * pad : (t + 1) * pad, :] = jnp.broadcast_to(
                flag * (-2.0 * scale), (pad, 128)
            )

    def tile(t, r0, height, g):
        q = qm_refs[t][pl.ds(r0, height), :]
        w = w_ref[pl.ds(g * group * wide, group * wide), :]
        both = lax.dot_general(q, w, (((1,), (1,)), ((), ())), preferred_element_type=F32)
        row_blocks = []
        for b in range(height // BLK):
            weights = []
            for c in range(group):
                score = both[b * BLK : (b + 1) * BLK, c * wide : c * wide + local_v]
                error = score - both[b * BLK : (b + 1) * BLK, c * wide + local_v : (c + 1) * wide]
                m = live_ref[g * group + c, pl.ds(t * pad + r0 // BLK + b, 1), :]
                sig = 1.0 / (1.0 + jnp.exp2(score * (-LOG2E)))
                neg = (error * m) * sig
                pos = neg * (error * (0.5 * sig - 0.5) - 1.0)
                weights += [pos.astype(BF16), neg.astype(BF16)]
            row_blocks.append(jnp.concatenate(weights, axis=1))
        weights = jnp.concatenate(row_blocks, axis=0)
        part = jnp.dot(weights, w, preferred_element_type=F32)
        if chunks == group:
            gq_refs[t][pl.ds(r0, height), :] = part
        else:
            gq_refs[t][pl.ds(r0, height), :] = part + jnp.where(
                g == 0, 0.0, gq_refs[t][pl.ds(r0, height), :]
            )
        gv_ref[g] += jnp.dot(q.T, weights, preferred_element_type=F32)

    height = 2 * BLK if rows % (2 * BLK) == 0 else BLK
    for t in range(len(qm_refs)):
        if chunks == group:
            for i in range(rows // height):
                tile(t, i * height, height, 0)
        else:

            def step(n, carry, t=t):
                g = n // (rows // height)
                r0 = pl.multiple_of((n % (rows // height)) * height, height)
                tile(t, r0, height, g)
                return carry

            lax.fori_loop(0, (chunks // group) * (rows // height), step, 0)


def core_sum_kernel(own_ref, got_own_ref, y_ref, got_y_ref, own_out, y_out):
    rows = own_ref.shape[0]
    own_out[...] = own_ref[...] + got_own_ref[...]
    exponents = []
    for r in range(0, rows, BLK):
        code, exponent = encode(y_ref[r : r + BLK, :] + got_y_ref[r : r + BLK, :])
        y_out[r : r + BLK, :] = code
        exponents.append(exponent)
    y_out[rows:, :] = tail_of(exponents)


def finish_kernel(chunks, own_ref, got_ref, term_ref, *refs):
    got_terms, (gq_out, gv_out, gd_out) = refs[: chunks - 1], refs[chunks - 1 :]
    rows = own_ref.shape[0]
    tail = got_ref[rows:, :].astype(jnp.int32).astype(F32)
    for b in range(rows // BLK):
        at = slice(b * BLK, (b + 1) * BLK)
        gq_out[at, :] = own_ref[at, :] + decode(got_ref[at, :], tail[b : b + 1, :])
    total = term_ref[...]
    dim = total.shape[0]
    for got in got_terms:
        tail = got[dim:, :].astype(jnp.int32).astype(F32)
        total = total + decode(got[0:dim, :], tail[0:1, :])
    local_v = gv_out.shape[0]
    gv_out[...] = total[:, :local_v].T
    gd_out[...] = total[:, local_v:].T


def body(queries, vectors, decoded, mask):
    rows, dim = queries.shape
    local_v = vectors.shape[0]
    blocks = mask.shape[0]
    n = lax.axis_size("qry")
    chunks = n // 4
    group = min(chunks, 4)
    wide = 2 * local_v
    scale = 1.0 / math.sqrt(local_v * n)
    pad = -(-blocks // 16) * 16

    def swap(x, bit):
        return lax.ppermute(x, "qry", [(i, i ^ bit) for i in range(n)])

    qm, vd = pl.pallas_call(
        pack_kernel,
        out_shape=(
            jax.ShapeDtypeStruct((rows + pad, dim), BF16),
            jax.ShapeDtypeStruct((wide, dim), BF16),
        ),
        in_specs=[HBM] * 4,
        out_specs=(VMEM, VMEM),
        scratch_shapes=[pltpu.VMEM(mask.shape, mask.dtype), pltpu.SemaphoreType.DMA((4,))],
        compiler_params=params(8),
        name="pack",
    )(queries, vectors, decoded, mask)
    row_out = jax.ShapeDtypeStruct((rows, dim), F32)
    gv_out = jax.ShapeDtypeStruct((chunks // group, dim, group * wide), F32)
    message = jax.ShapeDtypeStruct((dim + TAIL, wide), I16)
    scratch = [
        pltpu.VMEM((chunks * wide, dim), BF16),
        pltpu.VMEM((chunks, 4 * pad, 128), F32),
    ]

    def grads(sets, vds, gv, last, name):
        k = len(sets)

        def kernel(*refs):
            qm_refs, refs = refs[:k], refs[k:]
            vd_refs, refs = refs[:chunks], refs[chunks:]
            gv_in = None
            if gv is not None:
                gv_in, refs = refs[0], refs[1:]
            gq_refs, refs = refs[:k], refs[k:]
            if last:
                outs, (gv_ref, w_ref, live_ref) = refs[:chunks], refs[chunks:]
            else:
                gv_ref, w_ref, live_ref = refs
            gv_ref[...] = jnp.zeros_like(gv_ref) if gv_in is None else gv_in[...]
            tiles(rows, chunks, local_v, scale, qm_refs, vd_refs, gq_refs, gv_ref, w_ref, live_ref)
            if last:
                for s in range(chunks):
                    at = (s % group) * wide
                    term = gv_ref[s // group, :, at : at + wide]
                    if s == 0:
                        outs[0][...] = term
                    else:
                        code, exponent = encode(term)
                        outs[s][0:dim, :] = code
                        outs[s][dim:, :] = tail_of([exponent])

        ends = (
            (jax.ShapeDtypeStruct((dim, wide), F32),) + (message,) * (chunks - 1)
            if last
            else (gv_out,)
        )
        operands = [*sets, *vds] + ([] if gv is None else [gv])
        return pl.pallas_call(
            kernel,
            out_shape=(row_out,) * k + ends,
            in_specs=[VMEM] * len(operands),
            out_specs=(VMEM,) * (k + len(ends)),
            scratch_shapes=([pltpu.VMEM(gv_out.shape, F32)] if last else []) + scratch,
            compiler_params=params(36),
            cost_estimate=cost(12 * k * rows * chunks * wide * dim, 4 << 20),
            name=name,
        )(*operands)

    qm_y = swap(qm, 2)
    qm_c = swap(qm, 1)
    vds = [vd] + [swap(vd, 4 * s) for s in range(1, chunks)]
    qm_y, *vds = lax.optimization_barrier((qm_y, *vds))
    qm_yc = swap(qm_y, 1)
    gq_own, gq_c, gv = grads([qm, qm_c], vds, None, False, "grads_own")
    got_own = swap(gq_c, 1)
    gq_yc, gv = grads([qm_yc], vds, gv, False, "grads_far")
    got_y = swap(gq_yc, 1)
    gq_y, term, *messages = grads([qm_y], vds, gv, True, "grads_y")
    gq_own, gq_message = pl.pallas_call(
        core_sum_kernel,
        out_shape=(row_out, jax.ShapeDtypeStruct((rows + TAIL, dim), I16)),
        in_specs=[VMEM] * 4,
        out_specs=(VMEM,) * 2,
        compiler_params=params(16),
        name="core_sum",
    )(gq_own, got_own, gq_y, got_y)
    got_message = swap(gq_message, 2)
    got_terms = [swap(messages[s - 1], 4 * s) for s in range(1, chunks)]
    vec_out = jax.ShapeDtypeStruct((local_v, dim), F32)
    return pl.pallas_call(
        lambda *refs: finish_kernel(chunks, *refs),
        out_shape=(row_out, vec_out, vec_out),
        in_specs=[VMEM] * (2 + chunks),
        out_specs=(VMEM,) * 3,
        compiler_params=params(16),
        name="finish",
    )(gq_own, got_message, term, *got_terms)


def solution(mesh):
    placed = P(("groups", "qry"), None)
    return jax.shard_map(
        body,
        mesh=mesh,
        in_specs=(placed,) * 4,
        out_specs=(placed,) * 3,
        check_vma=False,
    )
```

time: 49.4 us -> 35.8 us (0.72)
  waiting for transfers between devices: 24.6 us -> 10.9 us
  Pallas kernels: 7.03 us -> 7.73 us
  starting transfers between devices: 13.5 us -> 13 us
    ppermute x11 -> x12, waiting for transfers between devices: 24.6 us -> 10.9 us  [swap(): return lax.ppermute(x, 'qry', [(i, i ^ bit) for i in range(n)])]
    pallas_call x2 -> x4, Pallas kernels: 6.1 us -> 6.63 us  [the longest x3 6.43 us: grads(): pl.pallas_call(kernel, out_shape=(row_out,) * k + ends, in_specs=[VMEM] *...]
    ppermute x11 -> x12, starting transfers between devices: 13.5 us -> 13 us  [swap(): return lax.ppermute(x, 'qry', [(i, i ^ bit) for i in range(n)])]
  transfers between devices with their start and end apart: 11 -> 12, of which waited for: 6 -> 4; matrix products, arithmetic and copies ran while one was open for 0% -> 0% of each run, Pallas kernels for 0% -> 18%
where the time goes in v2:
time: 35.8 us; the launch traced here: 35.5 us
  starting transfers between devices  13 us (36%)
  waiting for transfers between devices  10.9 us (30%)
  Pallas kernels  7.73 us (22%)
  local copies, waits for them, and re-layouts  3.14 us (9%)
  between operations  0.71 us (2%)
    ppermute x12, starting transfers between devices, swap(): return lax.ppermute(x, 'qry', [(i, i ^ bit) for i in range(n)])  13 us
    ppermute x12, waiting for transfers between devices, swap(): return lax.ppermute(x, 'qry', [(i, i ^ bit) for i in range(n)])  10.9 us
    pallas_call x3, Pallas kernels, grads(): pl.pallas_call(kernel, out_shape=(row_out,) * k + ends, in_specs=[VMEM] *...  6.43 us
    unnamed x8, local copies, waits for them, and re-layouts  3.14 us
    pallas_call x1, Pallas kernels, body(): pl.pallas_call(lambda *refs: finish_kernel(chunks, *refs), out_shape=(row...  0.97 us
  transfers between devices with their start and end apart: 12, of which 4 were waited for; matrix products, arithmetic and copies ran while one was open for 0% of the time, Pallas kernels for 18%

profile of v2, /device:TPU:0, one launch (start us, length us, event | category | flops | bytes accessed | tf_op | source)
XLA Modules:
  0.0 35.5 jit_solution(12355026864029792337)
XLA Ops:
  0.6 0.0 copy-start
  0.6 0.9 %copy-done = bf16[1024,128]{1,0:T(8,128)(2,1)S(1)} copy-done((bf16[1024,128]{1,0:T(8,128)(2,1)S(1)}, bf16[1024,128]{1,0:T(8,128)(2,1)}, u32[]{:S(2)}) %copy-start) | copy-done | bytes 262168
  1.6 0.0 copy-start.1
  1.6 0.8 %copy-done.1 = bf16[128,128]{1,0:T(8,128)(2,1)S(1)} copy-done((bf16[128,128]{1,0:T(8,128)(2,1)S(1)}, bf16[128,128]{1,0:T(8,128)(2,1)}, u32[]{:S(2)}) %copy-start.1) | copy-done | bytes 32792
  2.3 0.0 copy-start.2
  2.3 0.8 %copy-done.2 = bf16[128,128]{1,0:T(8,128)(2,1)S(1)} copy-done((bf16[128,128]{1,0:T(8,128)(2,1)S(1)}, bf16[128,128]{1,0:T(8,128)(2,1)}, u32[]{:S(2)}) %copy-start.2) | copy-done | bytes 32792
  3.1 0.0 copy-start.3
  3.1 0.7 %copy-done.3 = s32[4,8]{1,0:T(4,128)S(1)} copy-done((s32[4,8]{1,0:T(4,128)S(1)}, s32[4,8]{1,0:T(4,128)}, u32[]{:S(2)}) %copy-start.3) | copy-done | bytes 152
  3.8 0.1 pack.1
  3.9 3.0 %collective-permute-start.1 = (bf16[1040,128]{1,0:T(8,128)(2,1)S(1)}, bf16[1040,128]{1,0:T(8,128)(2,1)S(1)}, u32[]{:S(2)}, u32[]{:S(2)}) collective-permute-start(bf16[1040,128]{1,0:T(8,128)(2,1)S(1)} %get-tuple-element.22.refs_0_), channel_id=1, source_target_pairs={{0,2},{1,3},{2,0},{3,1},{4,6},{5,7},{6,4},{7,5},{8,10},{9,11},{10,... | collective-permute-start | bytes 798728 | tf_op jit(solution)/shard_map/ppermute | solution.py:166
  6.9 0.0 collective-permute-start
  6.9 3.6 %collective-permute-start.4 = (bf16[256,128]{1,0:T(8,128)(2,1)S(1)}, bf16[256,128]{1,0:T(8,128)(2,1)S(1)}, u32[]{:S(2)}, u32[]{:S(2)}) collective-permute-start(bf16[256,128]{1,0:T(8,128)(2,1)S(1)} %get-tuple-element.24.refs_2_.refs_1_), channel_id=1, source_target_pairs={{0,12},{1,13},{2,14},{3,15},{4,8},{5,9},{6,10},{7,11},{8,4},{9,5},... | collective-permute-start | bytes 196616 | tf_op jit(solution)/shard_map/ppermute | solution.py:166
  10.6 0.0 collective-permute-start.3
  10.6 0.8 %collective-permute-start.2 = (bf16[256,128]{1,0:T(8,128)(2,1)S(1)}, bf16[256,128]{1,0:T(8,128)(2,1)S(1)}, u32[]{:S(2)}, u32[]{:S(2)}) collective-permute-start(bf16[256,128]{1,0:T(8,128)(2,1)S(1)} %get-tuple-element.24.refs_2_.refs_1_), channel_id=1, source_target_pairs={{0,4},{1,5},{2,6},{3,7},{4,0},{5,1},{6,2},{7,3},{8,12},{9,13},{10,... | collective-permute-start | bytes 196616 | tf_op jit(solution)/shard_map/ppermute | solution.py:166
  11.3 2.2 %collective-permute-done.4.refs_5_.refs_4_ = bf16[256,128]{1,0:T(8,128)(2,1)S(1)} collective-permute-done((bf16[256,128]{1,0:T(8,128)(2,1)S(1)}, bf16[256,128]{1,0:T(8,128)(2,1)S(1)}, u32[]{:S(2)}, u32[]{:S(2)}) %collective-permute-start.4) | collective-permute-done | bytes 65568 | tf_op jit(solution)/shard_map/ppermute | solution.py:166
  13.5 3.2 %collective-permute-done.3.refs_4_.refs_3_ = bf16[256,128]{1,0:T(8,128)(2,1)S(1)} collective-permute-done((bf16[256,128]{1,0:T(8,128)(2,1)S(1)}, bf16[256,128]{1,0:T(8,128)(2,1)S(1)}, u32[]{:S(2)}, u32[]{:S(2)}) %collective-permute-start.3) | collective-permute-done | bytes 65568 | tf_op jit(solution)/shard_map/ppermute | solution.py:166
  16.7 0.0 collective-permute-done.2.refs_3_.refs_2_
  16.7 0.0 collective-permute-done.1.refs_0_
  16.7 0.0 collective-permute-start.6
  16.7 0.0 collective-permute-done.refs_1_
  16.7 3.1 %grads_own.1 = (f32[1024,128]{1,0:T(8,128)S(1)}, f32[1024,128]{1,0:T(8,128)S(1)}, f32[1,128,1024]{2,1,0:T(8,128)S(1)}) custom-call(bf16[1040,128]{1,0:T(8,128)(2,1)S(1)} %get-tuple-element.22.refs_0_, bf16[1040,128]{1,0:T(8,128)(2,1)S(1)} %collective-permute-done.refs_1_, bf16[256,128]{1,0:T(8,128)(2,1)S(1)} %get-tuple-element.24.refs_2_.refs_1_, ...), custom_call_target="tpu_custom_call" | custom-call | flops 3221225472 | bytes 4194304 | tf_op jit(solution)/shard_map/grads_own/pallas_call | solution.py:221
  19.8 0.6 %collective-permute-start.5 = (f32[1024,128]{1,0:T(8,128)S(1)}, f32[1024,128]{1,0:T(8,128)S(1)}, u32[]{:S(2)}, u32[]{:S(2)}) collective-permute-start(f32[1024,128]{1,0:T(8,128)S(1)} %get-tuple-element.29), channel_id=1, source_target_pairs={{0,1},{1,0},{2,3},{3,2},{4,5},{5,4},{6,7},{7,6},{8,9},{9,8},{10,11... | collective-permute-start | bytes 1572872 | tf_op jit(solution)/shard_map/ppermute | solution.py:166
  20.4 0.0 collective-permute-done.6.refs_0_
  20.4 1.7 %grads_far.1 = (f32[1024,128]{1,0:T(8,128)S(1)}, f32[1,128,1024]{2,1,0:T(8,128)S(1)}) custom-call(bf16[1040,128]{1,0:T(8,128)(2,1)S(1)} %collective-permute-done.6.refs_0_, bf16[256,128]{1,0:T(8,128)(2,1)S(1)} %get-tuple-element.24.refs_2_.refs_1_, bf16[256,128]{1,0:T(8,128)(2,1)S(1)} %collective-permute-done.2.refs_3_.refs_2_, ...), custom_call_target="tpu_custom_call" | custom-call | flops 1610612736 | bytes 4194304 | tf_op jit(solution)/shard_map/grads_far/pallas_call | solution.py:221
  22.1 0.1 collective-permute-start.7
  22.1 1.7 %grads_y.1 = (f32[1024,128]{1,0:T(8,128)S(1)}, f32[128,256]{1,0:T(8,128)S(1)}, s16[144,256]{1,0:T(8,128)(2,1)S(1)}, s16[144,256]{1,0:T(8,128)(2,1)S(1)}, s16[144,256]{1,0:T(8,128)(2,1)S(1)}) custom-call(bf16[1040,128]{1,0:T(8,128)(2,1)S(1)} %collective-permute-done.1.refs_0_, bf16[256,128]{1,0:T(8,128)(2,1)S(1)} %get-tuple-element.24.refs_2_.refs_1_, ...), custom_call_target="tpu_custom_call" | custom-call | flops 1610612736 | bytes 4194304 | tf_op jit(solution)/shard_map/grads_y/pallas_call | solution.py:221
  23.8 0.0 collective-permute-done.5.got_own_ref
  23.8 0.2 collective-permute-done.7.got_y_ref
  24.0 0.2 core_sum.1
  24.2 0.6 %collective-permute-start.8 = (s16[1040,128]{1,0:T(8,128)(2,1)S(1)}, s16[1040,128]{1,0:T(8,128)(2,1)S(1)}, u32[]{:S(2)}, u32[]{:S(2)}) collective-permute-start(s16[1040,128]{1,0:T(8,128)(2,1)S(1)} %get-tuple-element.36), channel_id=1, source_target_pairs={{0,2},{1,3},{2,0},{3,1},{4,6},{5,7},{6,4},{7,5},{8,10},{9,11},{10,... | collective-permute-start | bytes 798728 | tf_op jit(solution)/shard_map/ppermute | solution.py:166
  24.8 1.2 %collective-permute-start.9 = (s16[144,256]{1,0:T(8,128)(2,1)S(1)}, s16[144,256]{1,0:T(8,128)(2,1)S(1)}, u32[]{:S(2)}, u32[]{:S(2)}) collective-permute-start(s16[144,256]{1,0:T(8,128)(2,1)S(1)} %get-tuple-element.38), channel_id=1, source_target_pairs={{0,4},{1,5},{2,6},{3,7},{4,0},{5,1},{6,2},{7,3},{8,12},{9,13},{10,... | collective-permute-start | bytes 221192 | tf_op jit(solution)/shard_map/ppermute | solution.py:166
  26.0 1.8 %collective-permute-start.10 = (s16[144,256]{1,0:T(8,128)(2,1)S(1)}, s16[144,256]{1,0:T(8,128)(2,1)S(1)}, u32[]{:S(2)}, u32[]{:S(2)}) collective-permute-start(s16[144,256]{1,0:T(8,128)(2,1)S(1)} %get-tuple-element.39), channel_id=1, source_target_pairs={{0,8},{1,9},{2,10},{3,11},{4,12},{5,13},{6,14},{7,15},{8,0},{9,1},... | collective-permute-start | bytes 221192 | tf_op jit(solution)/shard_map/ppermute | solution.py:166
  27.9 1.3 %collective-permute-start.11 = (s16[144,256]{1,0:T(8,128)(2,1)S(1)}, s16[144,256]{1,0:T(8,128)(2,1)S(1)}, u32[]{:S(2)}, u32[]{:S(2)}) collective-permute-start(s16[144,256]{1,0:T(8,128)(2,1)S(1)} %get-tuple-element.40), channel_id=1, source_target_pairs={{0,12},{1,13},{2,14},{3,15},{4,8},{5,9},{6,10},{7,11},{8,4},{9,5},... | collective-permute-start | bytes 221192 | tf_op jit(solution)/shard_map/ppermute | solution.py:166
  29.2 0.0 collective-permute-done.9.refs_3_
  29.2 5.3 %collective-permute-done.10.refs_4_ = s16[144,256]{1,0:T(8,128)(2,1)S(1)} collective-permute-done((s16[144,256]{1,0:T(8,128)(2,1)S(1)}, s16[144,256]{1,0:T(8,128)(2,1)S(1)}, u32[]{:S(2)}, u32[]{:S(2)}) %collective-permute-start.10) | collective-permute-done | bytes 73760 | tf_op jit(solution)/shard_map/ppermute | solution.py:166
  34.5 0.0 collective-permute-done.11.refs_5_
  34.5 0.0 collective-permute-done.8.refs_1_
  34.5 1.0 %finish.1 = (f32[1024,128]{1,0:T(8,128)}, f32[128,128]{1,0:T(8,128)}, f32[128,128]{1,0:T(8,128)}) custom-call(f32[1024,128]{1,0:T(8,128)S(1)} %get-tuple-element.35.refs_0_, s16[1040,128]{1,0:T(8,128)(2,1)S(1)} %collective-permute-done.8.refs_1_, f32[128,256]{1,0:T(8,128)S(1)} %get-tuple-element.37.refs_2_, ...), custom_call_target="tpu_custom_call" | custom-call | tf_op jit(solution)/shard_map/finish/pallas_call | solution.py:253
Async XLA Ops:
  0.6 1.0 %copy-start = (bf16[1024,128]{1,0:T(8,128)(2,1)S(1)}, bf16[1024,128]{1,0:T(8,128)(2,1)}, u32[]{:S(2)}) copy-start(bf16[1024,128]{1,0:T(8,128)(2,1)} %q_hbm.1) | copy-start | bytes 786436
  1.6 0.8 %copy-start.1 = (bf16[128,128]{1,0:T(8,128)(2,1)S(1)}, bf16[128,128]{1,0:T(8,128)(2,1)}, u32[]{:S(2)}) copy-start(bf16[128,128]{1,0:T(8,128)(2,1)} %v_hbm.1) | copy-start | bytes 98308
  2.3 0.8 %copy-start.2 = (bf16[128,128]{1,0:T(8,128)(2,1)S(1)}, bf16[128,128]{1,0:T(8,128)(2,1)}, u32[]{:S(2)}) copy-start(bf16[128,128]{1,0:T(8,128)(2,1)} %d_hbm.1) | copy-start | bytes 98308
  3.1 0.7 %copy-start.3 = (s32[4,8]{1,0:T(4,128)S(1)}, s32[4,8]{1,0:T(4,128)}, u32[]{:S(2)}) copy-start(s32[4,8]{1,0:T(4,128)} %m_hbm.1) | copy-start | bytes 388
  3.9 12.8 %collective-permute-start.1 = (bf16[1040,128]{1,0:T(8,128)(2,1)S(1)}, bf16[1040,128]{1,0:T(8,128)(2,1)S(1)}, u32[]{:S(2)}, u32[]{:S(2)}) collective-permute-start(bf16[1040,128]{1,0:T(8,128)(2,1)S(1)} %get-tuple-element.22.refs_0_), channel_id=1, source_target_pairs={{0,2},{1,3},{2,0},{3,1},{4,6},{5,7},{6,4},{7,5},{8,10},{9,11},{10,... | collective-permute-start | bytes 798728 | tf_op jit(solution)/shard_map/ppermute | solution.py:166
  6.9 9.8 %collective-permute-start = (bf16[1040,128]{1,0:T(8,128)(2,1)S(1)}, bf16[1040,128]{1,0:T(8,128)(2,1)S(1)}, u32[]{:S(2)}, u32[]{:S(2)}) collective-permute-start(bf16[1040,128]{1,0:T(8,128)(2,1)S(1)} %get-tuple-element.22.refs_0_), channel_id=1, source_target_pairs={{0,1},{1,0},{2,3},{3,2},{4,5},{5,4},{6,7},{7,6},{8,9},{9,8},{10,11... | collective-permute-start | bytes 798728 | tf_op jit(solution)/shard_map/ppermute | solution.py:166
  6.9 6.6 %collective-permute-start.4 = (bf16[256,128]{1,0:T(8,128)(2,1)S(1)}, bf16[256,128]{1,0:T(8,128)(2,1)S(1)}, u32[]{:S(2)}, u32[]{:S(2)}) collective-permute-start(bf16[256,128]{1,0:T(8,128)(2,1)S(1)} %get-tuple-element.24.refs_2_.refs_1_), channel_id=1, source_target_pairs={{0,12},{1,13},{2,14},{3,15},{4,8},{5,9},{6,10},{7,11},{8,4},{9,5},... | collective-permute-start | bytes 196616 | tf_op jit(solution)/shard_map/ppermute | solution.py:166
  10.6 6.1 %collective-permute-start.3 = (bf16[256,128]{1,0:T(8,128)(2,1)S(1)}, bf16[256,128]{1,0:T(8,128)(2,1)S(1)}, u32[]{:S(2)}, u32[]{:S(2)}) collective-permute-start(bf16[256,128]{1,0:T(8,128)(2,1)S(1)} %get-tuple-element.24.refs_2_.refs_1_), channel_id=1, source_target_pairs={{0,8},{1,9},{2,10},{3,11},{4,12},{5,13},{6,14},{7,15},{8,0},{9,1},... | collective-permute-start | bytes 196616 | tf_op jit(solution)/shard_map/ppermute | solution.py:166
  10.6 6.1 %collective-permute-start.2 = (bf16[256,128]{1,0:T(8,128)(2,1)S(1)}, bf16[256,128]{1,0:T(8,128)(2,1)S(1)}, u32[]{:S(2)}, u32[]{:S(2)}) collective-permute-start(bf16[256,128]{1,0:T(8,128)(2,1)S(1)} %get-tuple-element.24.refs_2_.refs_1_), channel_id=1, source_target_pairs={{0,4},{1,5},{2,6},{3,7},{4,0},{5,1},{6,2},{7,3},{8,12},{9,13},{10,... | collective-permute-start | bytes 196616 | tf_op jit(solution)/shard_map/ppermute | solution.py:166
  16.7 3.7 %collective-permute-start.6 = (bf16[1040,128]{1,0:T(8,128)(2,1)S(1)}, bf16[1040,128]{1,0:T(8,128)(2,1)S(1)}, u32[]{:S(2)}, u32[]{:S(2)}) collective-permute-start(bf16[1040,128]{1,0:T(8,128)(2,1)S(1)} %collective-permute-done.1.refs_0_), channel_id=1, source_target_pairs={{0,1},{1,0},{2,3},{3,2},{4,5},{5,4},{6,7},{7,6},{8,9},{9,8},{10,11... | collective-permute-start | bytes 798728 | tf_op jit(solution)/shard_map/ppermute | solution.py:166
  19.8 4.0 %collective-permute-start.5 = (f32[1024,128]{1,0:T(8,128)S(1)}, f32[1024,128]{1,0:T(8,128)S(1)}, u32[]{:S(2)}, u32[]{:S(2)}) collective-permute-start(f32[1024,128]{1,0:T(8,128)S(1)} %get-tuple-element.29), channel_id=1, source_target_pairs={{0,1},{1,0},{2,3},{3,2},{4,5},{5,4},{6,7},{7,6},{8,9},{9,8},{10,11... | collective-permute-start | bytes 1572872 | tf_op jit(solution)/shard_map/ppermute | solution.py:166
  22.1 2.0 %collective-permute-start.7 = (f32[1024,128]{1,0:T(8,128)S(1)}, f32[1024,128]{1,0:T(8,128)S(1)}, u32[]{:S(2)}, u32[]{:S(2)}) collective-permute-start(f32[1024,128]{1,0:T(8,128)S(1)} %get-tuple-element.34), channel_id=1, source_target_pairs={{0,1},{1,0},{2,3},{3,2},{4,5},{5,4},{6,7},{7,6},{8,9},{9,8},{10,11... | collective-permute-start | bytes 1572872 | tf_op jit(solution)/shard_map/ppermute | solution.py:166
  24.2 10.3 %collective-permute-start.8 = (s16[1040,128]{1,0:T(8,128)(2,1)S(1)}, s16[1040,128]{1,0:T(8,128)(2,1)S(1)}, u32[]{:S(2)}, u32[]{:S(2)}) collective-permute-start(s16[1040,128]{1,0:T(8,128)(2,1)S(1)} %get-tuple-element.36), channel_id=1, source_target_pairs={{0,2},{1,3},{2,0},{3,1},{4,6},{5,7},{6,4},{7,5},{8,10},{9,11},{10,... | collective-permute-start | bytes 798728 | tf_op jit(solution)/shard_map/ppermute | solution.py:166
  24.8 4.4 %collective-permute-start.9 = (s16[144,256]{1,0:T(8,128)(2,1)S(1)}, s16[144,256]{1,0:T(8,128)(2,1)S(1)}, u32[]{:S(2)}, u32[]{:S(2)}) collective-permute-start(s16[144,256]{1,0:T(8,128)(2,1)S(1)} %get-tuple-element.38), channel_id=1, source_target_pairs={{0,4},{1,5},{2,6},{3,7},{4,0},{5,1},{6,2},{7,3},{8,12},{9,13},{10,... | collective-permute-start | bytes 221192 | tf_op jit(solution)/shard_map/ppermute | solution.py:166
  26.0 8.5 %collective-permute-start.10 = (s16[144,256]{1,0:T(8,128)(2,1)S(1)}, s16[144,256]{1,0:T(8,128)(2,1)S(1)}, u32[]{:S(2)}, u32[]{:S(2)}) collective-permute-start(s16[144,256]{1,0:T(8,128)(2,1)S(1)} %get-tuple-element.39), channel_id=1, source_target_pairs={{0,8},{1,9},{2,10},{3,11},{4,12},{5,13},{6,14},{7,15},{8,0},{9,1},... | collective-permute-start | bytes 221192 | tf_op jit(solution)/shard_map/ppermute | solution.py:166
  27.9 6.6 %collective-permute-start.11 = (s16[144,256]{1,0:T(8,128)(2,1)S(1)}, s16[144,256]{1,0:T(8,128)(2,1)S(1)}, u32[]{:S(2)}, u32[]{:S(2)}) collective-permute-start(s16[144,256]{1,0:T(8,128)(2,1)S(1)} %get-tuple-element.40), channel_id=1, source_target_pairs={{0,12},{1,13},{2,14},{3,15},{4,8},{5,9},{6,10},{7,11},{8,4},{9,5},... | collective-permute-start | bytes 221192 | tf_op jit(solution)/shard_map/ppermute | solution.py:166

commit v3 on v2

v3 whole, which is shorter than its diff:
```python
import math

import jax
import jax.numpy as jnp
from jax import lax
from jax.experimental import pallas as pl
from jax.experimental.pallas import tpu as pltpu
from jax.sharding import PartitionSpec as P

BLK = 256
LOG2E = 1.4426950408889634
LEVELS = 32000.0
TAIL = 16
VMEM = pl.BlockSpec(memory_space=pltpu.VMEM)
HBM = pl.BlockSpec(memory_space=pltpu.HBM)
F32 = jnp.float32
BF16 = jnp.bfloat16
I16 = jnp.int16


def params(mib):
    return pltpu.CompilerParams(vmem_limit_bytes=mib << 20)


def cost(flops, nbytes):
    return pl.CostEstimate(flops=flops, bytes_accessed=nbytes, transcendentals=0)


def encode(x):
    top = jnp.max(jnp.abs(x), axis=0, keepdims=True)
    exponent = jnp.ceil(jnp.log2(jnp.maximum(top, 1e-30)))
    scaled = jnp.round(x * (jnp.exp2(-exponent) * LEVELS))
    return scaled.astype(jnp.int32).astype(I16), exponent


def decode(x, exponent):
    return x.astype(jnp.int32).astype(F32) * (jnp.exp2(exponent) * (1.0 / LEVELS))


def tail_of(exponents):
    rows = jnp.concatenate(exponents, axis=0)
    rest = jnp.zeros((TAIL - rows.shape[0], rows.shape[1]), F32)
    return jnp.concatenate([rows, rest], axis=0).astype(jnp.int32).astype(I16)


def pack_kernel(q_hbm, v_hbm, d_hbm, m_hbm, qm_ref, vd_ref, m_ref, sems):
    rows = q_hbm.shape[0]
    local_v = v_hbm.shape[0]
    copies = [
        pltpu.make_async_copy(m_hbm, m_ref, sems.at[0]),
        pltpu.make_async_copy(v_hbm, vd_ref.at[pl.ds(0, local_v)], sems.at[1]),
        pltpu.make_async_copy(d_hbm, vd_ref.at[pl.ds(local_v, local_v)], sems.at[2]),
        pltpu.make_async_copy(q_hbm, qm_ref.at[pl.ds(0, rows)], sems.at[3]),
    ]
    for copy in copies:
        copy.start()
    copies[0].wait()
    blocks, cols = m_ref.shape
    pad, lanes = qm_ref.shape[0] - rows, qm_ref.shape[1]
    flags = jnp.concatenate([m_ref[...].astype(F32), jnp.zeros((blocks, lanes - cols), F32)], axis=1)
    flags = jnp.concatenate([flags, jnp.zeros((pad - blocks, lanes), F32)], axis=0)
    qm_ref[rows:, :] = flags.astype(BF16)
    for copy in copies[1:]:
        copy.wait()


def tile_grads(q, w, live, chunks, local_v):
    wide = 2 * local_v
    both = lax.dot_general(q, w, (((1,), (1,)), ((), ())), preferred_element_type=F32)
    row_blocks = []
    for b in range(q.shape[0] // BLK):
        weights = []
        for c in range(chunks):
            score = both[b * BLK : (b + 1) * BLK, c * wide : c * wide + local_v]
            error = score - both[b * BLK : (b + 1) * BLK, c * wide + local_v : (c + 1) * wide]
            sig = 1.0 / (1.0 + jnp.exp2(score * (-LOG2E)))
            neg = (error * live(b, c)) * sig
            pos = neg * (error * (0.5 * sig - 0.5) - 1.0)
            weights += [pos.astype(BF16), neg.astype(BF16)]
        row_blocks.append(jnp.concatenate(weights, axis=1))
    weights = jnp.concatenate(row_blocks, axis=0)
    return (
        jnp.dot(weights, w, preferred_element_type=F32),
        jnp.dot(q.T, weights, preferred_element_type=F32),
    )


def grads(sets, vds, group, rows, local_v, scale, gqs, gvs, send, code_last, name):
    k, m = len(sets), len(vds)
    dim = sets[0].shape[1]
    pad = sets[0].shape[0] - rows
    wide = 2 * local_v
    part = min(m, 4)
    height = 2 * BLK if rows % (2 * BLK) == 0 else BLK

    def kernel(*refs):
        qm_refs, refs = refs[:k], refs[k:]
        vd_refs, refs = refs[:m], refs[m:]
        gq_ins, gv_ins = None, None
        if gqs is not None:
            gq_ins, refs = refs[:k], refs[k:]
        if gvs is not None:
            gv_ins, refs = refs[:m], refs[m:]
        gq_refs, refs = refs[:k], refs[k:]
        gv_outs, (gv_ref, w_ref, live_ref) = refs[:m], refs[m:]
        me = lax.axis_index("qry")
        lanes = lax.broadcasted_iota(jnp.int32, (pad, 128), 1)
        for s in range(m):
            w_ref[s * wide : (s + 1) * wide, :] = vd_refs[s][...]
            gv_ref[:, s * wide : (s + 1) * wide] = (
                jnp.zeros((dim, wide), F32) if gv_ins is None else gv_ins[s][...]
            )
        for t in range(k):
            flags = qm_refs[t][rows:, :].astype(F32)
            for s in range(m):
                col = (jnp.bitwise_xor(me, 4 * group[s]) * local_v) // BLK
                flag = jnp.sum(jnp.where(lanes == col, flags, 0.0), axis=1, keepdims=True)
                live_ref[s, t * pad : (t + 1) * pad, :] = jnp.broadcast_to(
                    flag * (-2.0 * scale), (pad, 128)
                )

        exponents = []

        def tile(t, r0, first):
            def live(b, c):
                return live_ref[first + c, pl.ds(t * pad + r0 // BLK + b, 1), :]

            at = slice(first * wide, (first + part) * wide)
            q = qm_refs[t][pl.ds(r0, height), :]
            gq, gv = tile_grads(q, w_ref[at, :], live, part, local_v)
            if first > 0:
                gq = gq + gq_refs[t][pl.ds(r0, height), :]
            elif gq_ins is not None:
                gq = gq + gq_ins[t][pl.ds(r0, height), :]
            if code_last and t == k - 1:
                for b in range(0, height, BLK):
                    code, exponent = encode(gq[b : b + BLK])
                    gq_refs[t][r0 + b : r0 + b + BLK, :] = code
                    exponents.append(exponent)
            else:
                gq_refs[t][pl.ds(r0, height), :] = gq
            gv_ref[:, at] += gv

        for t in range(k):
            for first in range(0, m, part):
                if m <= 4:
                    for i in range(rows // height):
                        tile(t, i * height, first)
                else:

                    def step(i, carry, t=t, first=first):
                        tile(t, pl.multiple_of(i * height, height), first)
                        return carry

                    lax.fori_loop(0, rows // height, step, 0)
        if code_last:
            gq_refs[k - 1][rows:, :] = tail_of(exponents)
        for s in range(m):
            term = gv_ref[:, s * wide : (s + 1) * wide]
            if group[s] in send:
                code, exponent = encode(term)
                gv_outs[s][0:dim, :] = code
                gv_outs[s][dim:, :] = tail_of([exponent])
            else:
                gv_outs[s][...] = term

    operands = [*sets, *vds, *(gqs or []), *(gvs or [])]
    outs = [jax.ShapeDtypeStruct((rows, dim), F32)] * k + [
        jax.ShapeDtypeStruct((dim + TAIL, wide), I16)
        if s in send
        else jax.ShapeDtypeStruct((dim, wide), F32)
        for s in group
    ]
    if code_last:
        outs[k - 1] = jax.ShapeDtypeStruct((rows + TAIL, dim), I16)
    res = pl.pallas_call(
        kernel,
        out_shape=tuple(outs),
        in_specs=[VMEM] * len(operands),
        out_specs=(VMEM,) * len(outs),
        scratch_shapes=[
            pltpu.VMEM((dim, m * wide), F32),
            pltpu.VMEM((m * wide, dim), BF16),
            pltpu.VMEM((m, k * pad, 128), F32),
        ],
        compiler_params=params(32),
        cost_estimate=cost(k * rows * m * wide, 1 << 10),
        name=name,
    )(*operands)
    return list(res[:k]), list(res[k:])


def core_sum_kernel(y_ref, got_y_ref, y_out):
    rows = y_ref.shape[0]
    exponents = []
    for r in range(0, rows, BLK):
        code, exponent = encode(y_ref[r : r + BLK, :] + got_y_ref[r : r + BLK, :])
        y_out[r : r + BLK, :] = code
        exponents.append(exponent)
    y_out[rows : rows + TAIL, :] = tail_of(exponents)
    y_out[rows + TAIL :, :] = jnp.zeros((y_out.shape[0] - rows - TAIL, y_out.shape[1]), I16)


def finish_kernel(chunks, own_ref, got_own_ref, got_ref, term_ref, *refs):
    got_terms, (gq_out, gv_out, gd_out) = refs[: chunks - 1], refs[chunks - 1 :]
    rows = own_ref.shape[0]
    tail = got_ref[rows:, :].astype(jnp.int32).astype(F32)
    own_tail = got_own_ref[rows:, :].astype(jnp.int32).astype(F32)
    for b in range(rows // BLK):
        at = slice(b * BLK, (b + 1) * BLK)
        own = own_ref[at, :] + decode(got_own_ref[at, :], own_tail[b : b + 1, :])
        gq_out[at, :] = own + decode(got_ref[at, :], tail[b : b + 1, :])
    total = term_ref[...]
    dim = total.shape[0]
    for got in got_terms:
        tail = got[dim:, :].astype(jnp.int32).astype(F32)
        total = total + decode(got[0:dim, :], tail[0:1, :])
    local_v = gv_out.shape[0]
    gv_out[...] = total[:, :local_v].T
    gd_out[...] = total[:, local_v:].T


def body(queries, vectors, decoded, mask):
    rows, dim = queries.shape
    local_v = vectors.shape[0]
    blocks = mask.shape[0]
    n = lax.axis_size("qry")
    chunks = n // 4
    wide = 2 * local_v
    scale = 1.0 / math.sqrt(local_v * n)
    pad = -(-blocks // 16) * 16

    def swap(x, bit):
        return lax.ppermute(x, "qry", [(i, i ^ bit) for i in range(n)])

    qm, vd = pl.pallas_call(
        pack_kernel,
        out_shape=(
            jax.ShapeDtypeStruct((rows + pad, dim), BF16),
            jax.ShapeDtypeStruct((wide, dim), BF16),
        ),
        in_specs=[HBM] * 4,
        out_specs=(VMEM, VMEM),
        scratch_shapes=[pltpu.VMEM(mask.shape, mask.dtype), pltpu.SemaphoreType.DMA((4,))],
        compiler_params=params(60),
        name="pack",
    )(queries, vectors, decoded, mask)
    row_out = jax.ShapeDtypeStruct((rows, dim), F32)
    quarter = chunks // 4
    groups = [tuple(range(g * quarter, (g + 1) * quarter)) for g in range(4)]
    done = {"yc": groups[0] + groups[1], "own_3": groups[3], "own_2": groups[2]}

    def add(sets, which, gqs, gvs, name):
        group = sum((groups[g] for g in which), ())
        ready = [s for s in group if s > 0 and s in done.get(name, ())]
        return grads(
            sets, [vds[s] for s in group], group, rows, local_v, scale, gqs, gvs, ready,
            name == "own_2", name,
        )

    qm_y = swap(qm, 2)
    qm_c = swap(qm, 1)
    vds = [vd] + [swap(vd, 4 * s) for s in range(1, chunks)]
    own, half = [qm, qm_c], 2 * quarter
    gq_o, gv0 = add(own, [0], None, None, "own_0")
    gq_o, gv1 = add(own, [1], gq_o, None, "own_1")
    gq_y, gv01 = add([qm_y], [0, 1], None, gv0 + gv1, "y_01")
    qm_y, gq_y, gv01, vds[half:] = lax.optimization_barrier((qm_y, gq_y, gv01, vds[half:]))
    qm_yc = swap(qm_y, 1)
    gq_y, gv23 = add([qm_y], [2, 3], gq_y, None, "y_23")
    gq_yc, gvs = add([qm_yc], [0, 1, 2, 3], None, gv01 + gv23, "yc")
    got_y = swap(gq_yc[0], 1)
    gq_o, gv3 = add(own, [3], gq_o, gvs[half + quarter :], "own_3")
    gq_message = pl.pallas_call(
        core_sum_kernel,
        out_shape=jax.ShapeDtypeStruct((rows + 2 * TAIL, dim), I16),
        in_specs=[VMEM] * 2,
        out_specs=VMEM,
        compiler_params=params(16),
        name="core_sum",
    )(gq_y[0], got_y)
    gq_o, gq_message = lax.optimization_barrier((gq_o, gq_message))
    gq_o, gv2 = add(own, [2], gq_o, gvs[half : half + quarter], "own_2")
    gq_own, gq_c = gq_o
    got_own = swap(gq_c, 1)
    term, *near = gvs[:half]
    near = [swap(x, 4 * s) for s, x in enumerate(near, 1)]
    got_terms = near + [swap(x, 4 * s) for s, x in enumerate(gv2 + gv3, half)]
    got_message = swap(gq_message, 2)
    vec_out = jax.ShapeDtypeStruct((local_v, dim), F32)
    return pl.pallas_call(
        lambda *refs: finish_kernel(chunks, *refs),
        out_shape=(row_out, vec_out, vec_out),
        in_specs=[VMEM] * (3 + chunks),
        out_specs=(VMEM,) * 3,
        compiler_params=params(16),
        name="finish",
    )(gq_own, got_own, got_message, term, *got_terms)


def solution(mesh):
    placed = P(("groups", "qry"), None)
    return jax.shard_map(
        body,
        mesh=mesh,
        in_specs=(placed,) * 4,
        out_specs=(placed,) * 3,
        check_vma=False,
    )
```

time: 35.8 us -> 34.6 us (0.966)
  Pallas kernels: 7.73 us -> 11.9 us
  waiting for transfers between devices: 10.9 us -> 7.03 us
  local copies, waits for them, and re-layouts: 3.14 us -> 1.8 us
    ppermute x12, waiting for transfers between devices: 10.9 us -> 7.03 us  [swap(): return lax.ppermute(x, 'qry', [(i, i ^ bit) for i in range(n)])]
    pallas_call x4 -> x8, Pallas kernels: 6.63 us -> 9.17 us  [the longest x7 9.02 us: grads(): pl.pallas_call(kernel, out_shape=tuple(outs), in_specs=[VMEM] * len(opera...]
    pallas_call x1, Pallas kernels: 0.12 us -> 1.76 us  [body(): pl.pallas_call(pack_kernel, out_shape=(jax.ShapeDtypeStruct((rows + pad,...]
    unnamed x8, local copies, waits for them, and re-layouts: 3.14 us -> 1.8 us
  transfers between devices with their start and end apart: 12 -> 12, of which waited for: 4 -> 6; matrix products, arithmetic and copies ran while one was open for 0% -> 0% of each run, Pallas kernels for 18% -> 21%
where the time goes in v3:
time: 34.6 us; the launch traced here: 34.4 us
  starting transfers between devices  12.9 us (37%)
  Pallas kernels  11.9 us (34%)
  waiting for transfers between devices  7.03 us (20%)
  local copies, waits for them, and re-layouts  1.8 us (5%)
  between operations  0.74 us (2%)
    ppermute x12, starting transfers between devices, swap(): return lax.ppermute(x, 'qry', [(i, i ^ bit) for i in range(n)])  12.9 us
    pallas_call x7, Pallas kernels, grads(): pl.pallas_call(kernel, out_shape=tuple(outs), in_specs=[VMEM] * len(opera...  9.02 us
    ppermute x12, waiting for transfers between devices, swap(): return lax.ppermute(x, 'qry', [(i, i ^ bit) for i in range(n)])  7.03 us
    unnamed x8, local copies, waits for them, and re-layouts  1.8 us
    pallas_call x1, Pallas kernels, body(): pl.pallas_call(pack_kernel, out_shape=(jax.ShapeDtypeStruct((rows + pad,...  1.76 us
    pallas_call x1, Pallas kernels, body(): pl.pallas_call(lambda *refs: finish_kernel(chunks, *refs), out_shape=(row...  1.02 us
  transfers between devices with their start and end apart: 12, of which 6 were waited for; matrix products, arithmetic and copies ran while one was open for 0% of the time, Pallas kernels for 21%

profile of v3, /device:TPU:0, one launch (start us, length us, event | category | flops | bytes accessed | tf_op | source)
XLA Modules:
  0.0 34.4 jit_solution(662143068535708614)
XLA Ops:
  0.6 1.8 %pack.1 = (bf16[1040,128]{1,0:T(8,128)(2,1)}, bf16[256,128]{1,0:T(8,128)(2,1)}) custom-call(bf16[1024,128]{1,0:T(8,128)(2,1)} %q_hbm.1, bf16[128,128]{1,0:T(8,128)(2,1)} %v_hbm.1, bf16[128,128]{1,0:T(8,128)(2,1)} %d_hbm.1, s32[4,8]{1,0:T(4,128)} %m_hbm.1), custom_call_target="tpu_custom_call" | custom-call | tf_op jit(solution)/shard_map/pack/pallas_call | solution.py:236
  2.4 0.5 %collective-permute-start = (bf16[1040,128]{1,0:T(8,128)(2,1)}, bf16[1040,128]{1,0:T(8,128)(2,1)S(1)}, u32[]{:S(2)}, u32[]{:S(2)}) collective-permute-start(bf16[1040,128]{1,0:T(8,128)(2,1)} %get-tuple-element.37.refs_0_), channel_id=1, source_target_pairs={{0,1},{1,0},{2,3},{3,2},{4,5},{5,4},{6,7},{7,6},{8,9},{9,8},{10,11... | collective-permute-start | bytes 798728 | tf_op jit(solution)/shard_map/ppermute | solution.py:234
  2.9 2.6 %collective-permute-start.1 = (bf16[1040,128]{1,0:T(8,128)(2,1)}, bf16[1040,128]{1,0:T(8,128)(2,1)S(1)}, u32[]{:S(2)}, u32[]{:S(2)}) collective-permute-start(bf16[1040,128]{1,0:T(8,128)(2,1)} %get-tuple-element.37.refs_0_), channel_id=1, source_target_pairs={{0,2},{1,3},{2,0},{3,1},{4,6},{5,7},{6,4},{7,5},{8,10},{9,11},{10,... | collective-permute-start | bytes 798728 | tf_op jit(solution)/shard_map/ppermute | solution.py:234
  5.5 1.6 %collective-permute-start.2 = (bf16[256,128]{1,0:T(8,128)(2,1)}, bf16[256,128]{1,0:T(8,128)(2,1)S(1)}, u32[]{:S(2)}, u32[]{:S(2)}) collective-permute-start(bf16[256,128]{1,0:T(8,128)(2,1)} %get-tuple-element.38.refs_2_.refs_1_), channel_id=1, source_target_pairs={{0,4},{1,5},{2,6},{3,7},{4,0},{5,1},{6,2},{7,3},{8,12},{9,13},{10,... | collective-permute-start | bytes 196616 | tf_op jit(solution)/shard_map/ppermute | solution.py:234
  7.1 2.6 %collective-permute-start.3 = (bf16[256,128]{1,0:T(8,128)(2,1)}, bf16[256,128]{1,0:T(8,128)(2,1)S(1)}, u32[]{:S(2)}, u32[]{:S(2)}) collective-permute-start(bf16[256,128]{1,0:T(8,128)(2,1)} %get-tuple-element.38.refs_2_.refs_1_), channel_id=1, source_target_pairs={{0,8},{1,9},{2,10},{3,11},{4,12},{5,13},{6,14},{7,15},{8,0},{9,1},... | collective-permute-start | bytes 196616 | tf_op jit(solution)/shard_map/ppermute | solution.py:234
  9.7 0.2 collective-permute-start.4
  9.9 0.0 collective-permute-done.refs_1_
  9.9 0.0 copy-start
  9.9 1.0 %copy-done = bf16[1040,128]{1,0:T(8,128)(2,1)S(1)} copy-done((bf16[1040,128]{1,0:T(8,128)(2,1)S(1)}, bf16[1040,128]{1,0:T(8,128)(2,1)}, u32[]{:S(2)}) %copy-start) | copy-done | bytes 266264
  10.9 0.0 copy-start.2
  10.9 0.8 %copy-done.2 = bf16[256,128]{1,0:T(8,128)(2,1)S(1)} copy-done((bf16[256,128]{1,0:T(8,128)(2,1)S(1)}, bf16[256,128]{1,0:T(8,128)(2,1)}, u32[]{:S(2)}) %copy-start.2) | copy-done | bytes 65560
  11.7 1.0 %own_0.1 = (f32[1024,128]{1,0:T(8,128)S(1)}, f32[1024,128]{1,0:T(8,128)S(1)}, f32[128,256]{1,0:T(8,128)S(1)}) custom-call(bf16[1040,128]{1,0:T(8,128)(2,1)S(1)} %copy-done, bf16[1040,128]{1,0:T(8,128)(2,1)S(1)} %collective-permute-done.refs_1_, bf16[256,128]{1,0:T(8,128)(2,1)S(1)} %copy-done.2), custom_call_target="tpu_custom_call" | custom-call | flops 524288 | bytes 1024 | tf_op jit(solution)/shard_map/own_0/pallas_call | solution.py:176
  12.7 0.0 collective-permute-done.2.refs_2_
  12.7 1.3 %own_1.1 = (f32[1024,128]{1,0:T(8,128)S(1)}, f32[1024,128]{1,0:T(8,128)S(1)}, f32[128,256]{1,0:T(8,128)S(1)}) custom-call(bf16[1040,128]{1,0:T(8,128)(2,1)S(1)} %copy-done, bf16[1040,128]{1,0:T(8,128)(2,1)S(1)} %collective-permute-done.refs_1_, bf16[256,128]{1,0:T(8,128)(2,1)S(1)} %collective-permute-done.2.refs_2_, ...), custom_call_target="tpu_custom_call" | custom-call | flops 524288 | bytes 1024 | tf_op jit(solution)/shard_map/own_1/pallas_call | solution.py:176
  14.0 0.0 collective-permute-done.1.refs_0_
  14.0 1.2 %y_01.1 = (f32[1024,128]{1,0:T(8,128)S(1)}, f32[128,256]{1,0:T(8,128)S(1)}, f32[128,256]{1,0:T(8,128)S(1)}) custom-call(bf16[1040,128]{1,0:T(8,128)(2,1)S(1)} %collective-permute-done.1.refs_0_, bf16[256,128]{1,0:T(8,128)(2,1)S(1)} %copy-done.2, bf16[256,128]{1,0:T(8,128)(2,1)S(1)} %collective-permute-done.2.refs_2_, ...), custom_call_target="tpu_custom_call" | custom-call | flops 524288 | bytes 1024 | tf_op jit(solution)/shard_map/y_01/pallas_call | solution.py:176
  15.2 0.0 collective-permute-done.3.refs_1_.refs_3_.refs_2_
  15.2 0.8 %collective-permute-done.4.refs_2_.refs_4_ = bf16[256,128]{1,0:T(8,128)(2,1)S(1)} collective-permute-done((bf16[256,128]{1,0:T(8,128)(2,1)}, bf16[256,128]{1,0:T(8,128)(2,1)S(1)}, u32[]{:S(2)}, u32[]{:S(2)}) %collective-permute-start.4) | collective-permute-done | bytes 65568 | tf_op jit(solution)/shard_map/ppermute | solution.py:234
  16.1 0.0 copy-start.3
  16.1 0.0 collective-permute-start.5
  16.1 1.2 %y_23.1 = (f32[1024,128]{1,0:T(8,128)S(1)}, f32[128,256]{1,0:T(8,128)S(1)}, f32[128,256]{1,0:T(8,128)S(1)}) custom-call(bf16[1040,128]{1,0:T(8,128)(2,1)S(1)} %collective-permute-done.1.refs_0_, bf16[256,128]{1,0:T(8,128)(2,1)S(1)} %collective-permute-done.3.refs_1_.refs_3_.refs_2_, bf16[256,128]{1,0:T(8,128)(2,1)S(1)} %collective-permute-done.4.refs_2_.refs_4_, ...), custom_call_target="tpu_custom_call" | custom-call | flops 524288 | bytes 1024 | tf_op jit(solution)/shard_map/y_23/pallas_call | solution.py:176
  17.3 0.3 collective-permute-done.5.refs_0_
  17.6 0.0 copy-done.3
  17.6 0.0 copy-start.1
  17.6 1.7 %yc.1 = (f32[1024,128]{1,0:T(8,128)S(1)}, f32[128,256]{1,0:T(8,128)S(1)}, s16[144,256]{1,0:T(8,128)(2,1)S(1)}, f32[128,256]{1,0:T(8,128)S(1)}, f32[128,256]{1,0:T(8,128)S(1)}) custom-call(bf16[1040,128]{1,0:T(8,128)(2,1)S(1)} %collective-permute-done.5.refs_0_, bf16[256,128]{1,0:T(8,128)(2,1)S(1)} %copy-done.3, ...), custom_call_target="tpu_custom_call" | custom-call | flops 1048576 | bytes 1024 | tf_op jit(solution)/shard_map/yc/pallas_call | solution.py:176
  19.3 0.3 collective-permute-start.6
  19.5 0.0 copy-done.1
  19.5 1.3 %own_3.1 = (f32[1024,128]{1,0:T(8,128)S(1)}, f32[1024,128]{1,0:T(8,128)S(1)}, s16[144,256]{1,0:T(8,128)(2,1)S(1)}) custom-call(bf16[1040,128]{1,0:T(8,128)(2,1)S(1)} %copy-done.1, bf16[1040,128]{1,0:T(8,128)(2,1)S(1)} %collective-permute-done.refs_1_, bf16[256,128]{1,0:T(8,128)(2,1)S(1)} %collective-permute-done.4.refs_2_.refs_4_, ...), custom_call_target="tpu_custom_call" | custom-call | flops 524288 | bytes 1024 | tf_op jit(solution)/shard_map/own_3/pallas_call | solution.py:176
  20.9 0.4 %collective-permute-done.6.got_y_ref = f32[1024,128]{1,0:T(8,128)S(1)} collective-permute-done((f32[1024,128]{1,0:T(8,128)S(1)}, f32[1024,128]{1,0:T(8,128)S(1)}, u32[]{:S(2)}, u32[]{:S(2)}) %collective-permute-start.6) | collective-permute-done | bytes 524320 | tf_op jit(solution)/shard_map/ppermute | solution.py:234
  21.2 0.2 core_sum.1
  21.4 0.6 %collective-permute-start.8 = (s16[1056,128]{1,0:T(8,128)(2,1)S(1)}, s16[1056,128]{1,0:T(8,128)(2,1)S(1)}, u32[]{:S(2)}, u32[]{:S(2)}) collective-permute-start(s16[1056,128]{1,0:T(8,128)(2,1)S(1)} %core_sum.1), channel_id=1, source_target_pairs={{0,2},{1,3},{2,0},{3,1},{4,6},{5,7},{6,4},{7,5},{8,10},{9,11},{10,... | collective-permute-start | bytes 811016 | tf_op jit(solution)/shard_map/ppermute | solution.py:234
  22.0 1.3 %own_2.1 = (f32[1024,128]{1,0:T(8,128)S(1)}, s16[1040,128]{1,0:T(8,128)(2,1)S(1)}, s16[144,256]{1,0:T(8,128)(2,1)S(1)}) custom-call(bf16[1040,128]{1,0:T(8,128)(2,1)S(1)} %copy-done.1, bf16[1040,128]{1,0:T(8,128)(2,1)S(1)} %collective-permute-done.refs_1_, bf16[256,128]{1,0:T(8,128)(2,1)S(1)} %collective-permute-done.3.refs_1_.refs_3_.refs_2_, ...), custom_call_target="tpu_custom_call" | custom-call | flops 524288 | bytes 1024 | tf_op jit(solution)/shard_map/own_2/pallas_call | solution.py:176
  23.3 0.1 collective-permute-start.7
  23.4 2.9 %collective-permute-start.11 = (s16[144,256]{1,0:T(8,128)(2,1)S(1)}, s16[144,256]{1,0:T(8,128)(2,1)S(1)}, u32[]{:S(2)}, u32[]{:S(2)}) collective-permute-start(s16[144,256]{1,0:T(8,128)(2,1)S(1)} %get-tuple-element.70), channel_id=1, source_target_pairs={{0,12},{1,13},{2,14},{3,15},{4,8},{5,9},{6,10},{7,11},{8,4},{9,5},... | collective-permute-start | bytes 221192 | tf_op jit(solution)/shard_map/ppermute | solution.py:234
  26.3 0.0 collective-permute-start.9
  26.3 1.5 %collective-permute-start.10 = (s16[144,256]{1,0:T(8,128)(2,1)S(1)}, s16[144,256]{1,0:T(8,128)(2,1)S(1)}, u32[]{:S(2)}, u32[]{:S(2)}) collective-permute-start(s16[144,256]{1,0:T(8,128)(2,1)S(1)} %get-tuple-element.69), channel_id=1, source_target_pairs={{0,8},{1,9},{2,10},{3,11},{4,12},{5,13},{6,14},{7,15},{8,0},{9,1},... | collective-permute-start | bytes 221192 | tf_op jit(solution)/shard_map/ppermute | solution.py:234
  27.9 2.6 %collective-permute-done.11.refs_6_ = s16[144,256]{1,0:T(8,128)(2,1)S(1)} collective-permute-done((s16[144,256]{1,0:T(8,128)(2,1)S(1)}, s16[144,256]{1,0:T(8,128)(2,1)S(1)}, u32[]{:S(2)}, u32[]{:S(2)}) %collective-permute-start.11) | collective-permute-done | bytes 73760 | tf_op jit(solution)/shard_map/ppermute | solution.py:234
  30.4 2.6 %collective-permute-done.9.refs_4_ = s16[144,256]{1,0:T(8,128)(2,1)S(1)} collective-permute-done((s16[144,256]{1,0:T(8,128)(2,1)S(1)}, s16[144,256]{1,0:T(8,128)(2,1)S(1)}, u32[]{:S(2)}, u32[]{:S(2)}) %collective-permute-start.9) | collective-permute-done | bytes 73760 | tf_op jit(solution)/shard_map/ppermute | solution.py:234
  33.0 0.4 %collective-permute-done.10.refs_5_ = s16[144,256]{1,0:T(8,128)(2,1)S(1)} collective-permute-done((s16[144,256]{1,0:T(8,128)(2,1)S(1)}, s16[144,256]{1,0:T(8,128)(2,1)S(1)}, u32[]{:S(2)}, u32[]{:S(2)}) %collective-permute-start.10) | collective-permute-done | bytes 73760 | tf_op jit(solution)/shard_map/ppermute | solution.py:234
  33.3 0.0 collective-permute-done.7.refs_1_
  33.4 0.0 collective-permute-done.8.refs_2_
  33.4 1.0 %finish.1 = (f32[1024,128]{1,0:T(8,128)}, f32[128,128]{1,0:T(8,128)}, f32[128,128]{1,0:T(8,128)}) custom-call(f32[1024,128]{1,0:T(8,128)S(1)} %get-tuple-element.64.refs_0_, s16[1040,128]{1,0:T(8,128)(2,1)S(1)} %collective-permute-done.7.refs_1_, s16[1056,128]{1,0:T(8,128)(2,1)S(1)} %collective-permute-done.8.refs_2_, ...), custom_call_target="tpu_custom_call" | custom-call | tf_op jit(solution)/shard_map/finish/pallas_call | solution.py:291
Async XLA Ops:
  2.4 7.5 %collective-permute-start = (bf16[1040,128]{1,0:T(8,128)(2,1)}, bf16[1040,128]{1,0:T(8,128)(2,1)S(1)}, u32[]{:S(2)}, u32[]{:S(2)}) collective-permute-start(bf16[1040,128]{1,0:T(8,128)(2,1)} %get-tuple-element.37.refs_0_), channel_id=1, source_target_pairs={{0,1},{1,0},{2,3},{3,2},{4,5},{5,4},{6,7},{7,6},{8,9},{9,8},{10,11... | collective-permute-start | bytes 798728 | tf_op jit(solution)/shard_map/ppermute | solution.py:234
  2.9 11.1 %collective-permute-start.1 = (bf16[1040,128]{1,0:T(8,128)(2,1)}, bf16[1040,128]{1,0:T(8,128)(2,1)S(1)}, u32[]{:S(2)}, u32[]{:S(2)}) collective-permute-start(bf16[1040,128]{1,0:T(8,128)(2,1)} %get-tuple-element.37.refs_0_), channel_id=1, source_target_pairs={{0,2},{1,3},{2,0},{3,1},{4,6},{5,7},{6,4},{7,5},{8,10},{9,11},{10,... | collective-permute-start | bytes 798728 | tf_op jit(solution)/shard_map/ppermute | solution.py:234
  5.5 7.2 %collective-permute-start.2 = (bf16[256,128]{1,0:T(8,128)(2,1)}, bf16[256,128]{1,0:T(8,128)(2,1)S(1)}, u32[]{:S(2)}, u32[]{:S(2)}) collective-permute-start(bf16[256,128]{1,0:T(8,128)(2,1)} %get-tuple-element.38.refs_2_.refs_1_), channel_id=1, source_target_pairs={{0,4},{1,5},{2,6},{3,7},{4,0},{5,1},{6,2},{7,3},{8,12},{9,13},{10,... | collective-permute-start | bytes 196616 | tf_op jit(solution)/shard_map/ppermute | solution.py:234
  7.1 8.2 %collective-permute-start.3 = (bf16[256,128]{1,0:T(8,128)(2,1)}, bf16[256,128]{1,0:T(8,128)(2,1)S(1)}, u32[]{:S(2)}, u32[]{:S(2)}) collective-permute-start(bf16[256,128]{1,0:T(8,128)(2,1)} %get-tuple-element.38.refs_2_.refs_1_), channel_id=1, source_target_pairs={{0,8},{1,9},{2,10},{3,11},{4,12},{5,13},{6,14},{7,15},{8,0},{9,1},... | collective-permute-start | bytes 196616 | tf_op jit(solution)/shard_map/ppermute | solution.py:234
  9.7 6.4 %collective-permute-start.4 = (bf16[256,128]{1,0:T(8,128)(2,1)}, bf16[256,128]{1,0:T(8,128)(2,1)S(1)}, u32[]{:S(2)}, u32[]{:S(2)}) collective-permute-start(bf16[256,128]{1,0:T(8,128)(2,1)} %get-tuple-element.38.refs_2_.refs_1_), channel_id=1, source_target_pairs={{0,12},{1,13},{2,14},{3,15},{4,8},{5,9},{6,10},{7,11},{8,4},{9,5},... | collective-permute-start | bytes 196616 | tf_op jit(solution)/shard_map/ppermute | solution.py:234
  9.9 1.0 %copy-start = (bf16[1040,128]{1,0:T(8,128)(2,1)S(1)}, bf16[1040,128]{1,0:T(8,128)(2,1)}, u32[]{:S(2)}) copy-start(bf16[1040,128]{1,0:T(8,128)(2,1)} %get-tuple-element.37.refs_0_) | copy-start | bytes 798724
  10.9 0.8 %copy-start.2 = (bf16[256,128]{1,0:T(8,128)(2,1)S(1)}, bf16[256,128]{1,0:T(8,128)(2,1)}, u32[]{:S(2)}) copy-start(bf16[256,128]{1,0:T(8,128)(2,1)} %get-tuple-element.38.refs_2_.refs_1_) | copy-start | bytes 196612
  16.1 1.5 %copy-start.3 = (bf16[256,128]{1,0:T(8,128)(2,1)S(1)}, bf16[256,128]{1,0:T(8,128)(2,1)}, u32[]{:S(2)}) copy-start(bf16[256,128]{1,0:T(8,128)(2,1)} %get-tuple-element.38.refs_2_.refs_1_) | copy-start | bytes 196612
  16.1 1.5 %collective-permute-start.5 = (bf16[1040,128]{1,0:T(8,128)(2,1)S(1)}, bf16[1040,128]{1,0:T(8,128)(2,1)S(1)}, u32[]{:S(2)}, u32[]{:S(2)}) collective-permute-start(bf16[1040,128]{1,0:T(8,128)(2,1)S(1)} %collective-permute-done.1.refs_0_), channel_id=1, source_target_pairs={{0,1},{1,0},{2,3},{3,2},{4,5},{5,4},{6,7},{7,6},{8,9},{9,8},{10,11... | collective-permute-start | bytes 798728 | tf_op jit(solution)/shard_map/ppermute | solution.py:234
  17.6 1.9 %copy-start.1 = (bf16[1040,128]{1,0:T(8,128)(2,1)S(1)}, bf16[1040,128]{1,0:T(8,128)(2,1)}, u32[]{:S(2)}) copy-start(bf16[1040,128]{1,0:T(8,128)(2,1)} %get-tuple-element.37.refs_0_) | copy-start | bytes 798724
  19.3 2.0 %collective-permute-start.6 = (f32[1024,128]{1,0:T(8,128)S(1)}, f32[1024,128]{1,0:T(8,128)S(1)}, u32[]{:S(2)}, u32[]{:S(2)}) collective-permute-start(f32[1024,128]{1,0:T(8,128)S(1)} %get-tuple-element.60), channel_id=1, source_target_pairs={{0,1},{1,0},{2,3},{3,2},{4,5},{5,4},{6,7},{7,6},{8,9},{9,8},{10,11... | collective-permute-start | bytes 1572872 | tf_op jit(solution)/shard_map/ppermute | solution.py:234
  21.4 11.9 %collective-permute-start.8 = (s16[1056,128]{1,0:T(8,128)(2,1)S(1)}, s16[1056,128]{1,0:T(8,128)(2,1)S(1)}, u32[]{:S(2)}, u32[]{:S(2)}) collective-permute-start(s16[1056,128]{1,0:T(8,128)(2,1)S(1)} %core_sum.1), channel_id=1, source_target_pairs={{0,2},{1,3},{2,0},{3,1},{4,6},{5,7},{6,4},{7,5},{8,10},{9,11},{10,... | collective-permute-start | bytes 811016 | tf_op jit(solution)/shard_map/ppermute | solution.py:234
  23.3 10.0 %collective-permute-start.7 = (s16[1040,128]{1,0:T(8,128)(2,1)S(1)}, s16[1040,128]{1,0:T(8,128)(2,1)S(1)}, u32[]{:S(2)}, u32[]{:S(2)}) collective-permute-start(s16[1040,128]{1,0:T(8,128)(2,1)S(1)} %get-tuple-element.65), channel_id=1, source_target_pairs={{0,1},{1,0},{2,3},{3,2},{4,5},{5,4},{6,7},{7,6},{8,9},{9,8},{10,11... | collective-permute-start | bytes 798728 | tf_op jit(solution)/shard_map/ppermute | solution.py:234
  23.4 7.0 %collective-permute-start.11 = (s16[144,256]{1,0:T(8,128)(2,1)S(1)}, s16[144,256]{1,0:T(8,128)(2,1)S(1)}, u32[]{:S(2)}, u32[]{:S(2)}) collective-permute-start(s16[144,256]{1,0:T(8,128)(2,1)S(1)} %get-tuple-element.70), channel_id=1, source_target_pairs={{0,12},{1,13},{2,14},{3,15},{4,8},{5,9},{6,10},{7,11},{8,4},{9,5},... | collective-permute-start | bytes 221192 | tf_op jit(solution)/shard_map/ppermute | solution.py:234
  26.3 6.6 %collective-permute-start.9 = (s16[144,256]{1,0:T(8,128)(2,1)S(1)}, s16[144,256]{1,0:T(8,128)(2,1)S(1)}, u32[]{:S(2)}, u32[]{:S(2)}) collective-permute-start(s16[144,256]{1,0:T(8,128)(2,1)S(1)} %get-tuple-element.68), channel_id=1, source_target_pairs={{0,4},{1,5},{2,6},{3,7},{4,0},{5,1},{6,2},{7,3},{8,12},{9,13},{10,... | collective-permute-start | bytes 221192 | tf_op jit(solution)/shard_map/ppermute | solution.py:234
  26.3 7.0 %collective-permute-start.10 = (s16[144,256]{1,0:T(8,128)(2,1)S(1)}, s16[144,256]{1,0:T(8,128)(2,1)S(1)}, u32[]{:S(2)}, u32[]{:S(2)}) collective-permute-start(s16[144,256]{1,0:T(8,128)(2,1)S(1)} %get-tuple-element.69), channel_id=1, source_target_pairs={{0,8},{1,9},{2,10},{3,11},{4,12},{5,13},{6,14},{7,15},{8,0},{9,1},... | collective-permute-start | bytes 221192 | tf_op jit(solution)/shard_map/ppermute | solution.py:234

commit v4 on v3

v4 whole, which is shorter than its diff:
```python
import math

import jax
import jax.numpy as jnp
from jax import lax
from jax.experimental import pallas as pl
from jax.experimental.pallas import tpu as pltpu
from jax.sharding import PartitionSpec as P

BLK = 256
LOG2E = 1.4426950408889634
LEVELS = 32000.0
TAIL = 16
VMEM = pl.BlockSpec(memory_space=pltpu.VMEM)
HBM = pl.BlockSpec(memory_space=pltpu.HBM)
F32 = jnp.float32
BF16 = jnp.bfloat16
I16 = jnp.int16


def params(mib):
    return pltpu.CompilerParams(vmem_limit_bytes=mib << 20)


def cost(flops, nbytes):
    return pl.CostEstimate(flops=flops, bytes_accessed=nbytes, transcendentals=0)


def encode(x):
    top = jnp.max(jnp.abs(x), axis=0, keepdims=True)
    exponent = jnp.ceil(jnp.log2(jnp.maximum(top, 1e-30)))
    scaled = jnp.round(x * (jnp.exp2(-exponent) * LEVELS))
    return scaled.astype(jnp.int32).astype(I16), exponent


def decode(x, exponent):
    return x.astype(jnp.int32).astype(F32) * (jnp.exp2(exponent) * (1.0 / LEVELS))


def tail_of(exponents):
    rows = jnp.concatenate(exponents, axis=0)
    rest = jnp.zeros((TAIL - rows.shape[0], rows.shape[1]), F32)
    return jnp.concatenate([rows, rest], axis=0).astype(jnp.int32).astype(I16)


def encode_rows(x_ref, out_ref):
    rows = x_ref.shape[0]
    exponents = []
    for r in range(0, rows, BLK):
        code, exponent = encode(x_ref[r : r + BLK, :])
        out_ref[r : r + BLK, :] = code
        exponents.append(exponent)
    out_ref[rows : rows + TAIL, :] = tail_of(exponents)
    if out_ref.shape[0] > rows + TAIL:
        rest = (out_ref.shape[0] - rows - TAIL, out_ref.shape[1])
        out_ref[rows + TAIL :, :] = jnp.zeros(rest, I16)


def pack_kernel(q_hbm, v_hbm, d_hbm, m_hbm, qm_ref, vd_ref, m_ref, sems):
    rows = q_hbm.shape[0]
    local_v = v_hbm.shape[0]
    copies = [
        pltpu.make_async_copy(m_hbm, m_ref, sems.at[0]),
        pltpu.make_async_copy(v_hbm, vd_ref.at[pl.ds(0, local_v)], sems.at[1]),
        pltpu.make_async_copy(d_hbm, vd_ref.at[pl.ds(local_v, local_v)], sems.at[2]),
        pltpu.make_async_copy(q_hbm, qm_ref.at[pl.ds(0, rows)], sems.at[3]),
    ]
    for copy in copies:
        copy.start()
    copies[0].wait()
    blocks, cols = m_ref.shape
    pad, lanes = qm_ref.shape[0] - rows, qm_ref.shape[1]
    flags = jnp.concatenate([m_ref[...].astype(F32), jnp.zeros((blocks, lanes - cols), F32)], axis=1)
    flags = jnp.concatenate([flags, jnp.zeros((pad - blocks, lanes), F32)], axis=0)
    qm_ref[rows:, :] = flags.astype(BF16)
    for copy in copies[1:]:
        copy.wait()


def live_table(flags, chunks, local_v, scale):
    me = lax.axis_index("qry")
    lanes = flags.shape[1]
    rows = lax.broadcasted_iota(jnp.int32, (lanes, 128), 0)
    cols = [(jnp.bitwise_xor(me, 4 * s) * local_v) // BLK for s in range(chunks)]
    onehot = jnp.concatenate([(rows == col).astype(F32) for col in cols], axis=1)
    return jnp.dot(flags, onehot.astype(BF16), preferred_element_type=F32) * (-2.0 * scale)


def tile_weights(q, w, live, chunks, local_v):
    wide = 2 * local_v
    both = lax.dot_general(q, w, (((1,), (1,)), ((), ())), preferred_element_type=F32)
    row_blocks = []
    for b in range(q.shape[0] // BLK):
        weights = []
        for c in range(chunks):
            score = both[b * BLK : (b + 1) * BLK, c * wide : c * wide + local_v]
            error = score - both[b * BLK : (b + 1) * BLK, c * wide + local_v : (c + 1) * wide]
            sig = 1.0 / (1.0 + jnp.exp2(score * (-LOG2E)))
            neg = (error * live(b, c)) * sig
            pos = neg * (error * (0.5 * sig - 0.5) - 1.0)
            weights += [pos.astype(BF16), neg.astype(BF16)]
        row_blocks.append(jnp.concatenate(weights, axis=1))
    return jnp.concatenate(row_blocks, axis=0)


def grads(sets, vds, group, chunks, rows, local_v, scale, table, gqs, gvs, send, code_last, name):
    k, m = len(sets), len(vds)
    dim = sets[0].shape[1]
    pad = sets[0].shape[0] - rows
    wide = 2 * local_v
    part = min(m, 4)
    height = 2 * BLK if rows % (2 * BLK) == 0 else BLK
    fresh = table is None

    def kernel(*refs):
        qm_refs, refs = refs[:k], refs[k:]
        vd_refs, refs = refs[:m], refs[m:]
        gq_ins, gv_ins = None, None
        if not fresh:
            table_ref, refs = refs[0], refs[1:]
        if gqs is not None:
            gq_ins, refs = refs[:k], refs[k:]
        if gvs is not None:
            gv_ins, refs = refs[:m], refs[m:]
        gq_refs, refs = refs[:k], refs[k:]
        gv_outs, refs = refs[:m], refs[m:]
        if fresh:
            table_ref, refs = refs[0], refs[1:]
            for t in range(k):
                table = live_table(qm_refs[t][rows:, :], chunks, local_v, scale)
                for s in range(chunks):
                    table_ref[s, t * pad : (t + 1) * pad, :] = table[:, s * 128 : (s + 1) * 128]
        gv_ref, w_ref, last_ref = refs
        for s in range(m):
            w_ref[s * wide : (s + 1) * wide, :] = vd_refs[s][...]
            gv_ref[:, s * wide : (s + 1) * wide] = (
                jnp.zeros((dim, wide), F32) if gv_ins is None else gv_ins[s][...]
            )
        outs = [*gq_refs[: k - 1], last_ref if code_last else gq_refs[k - 1]]

        def tile(t, r0, first):
            def live(b, c):
                s = group[first + c]
                return table_ref[s, pl.ds(t * pad + r0 // BLK + b, 1), :]

            w = w_ref[first * wide : (first + part) * wide, :]
            weights = tile_weights(qm_refs[t][pl.ds(r0, height), :], w, live, part, local_v)
            gq = jnp.dot(weights, w, preferred_element_type=F32)
            if first > 0:
                gq = gq + outs[t][pl.ds(r0, height), :]
            elif gq_ins is not None:
                gq = gq + gq_ins[t][pl.ds(r0, height), :]
            outs[t][pl.ds(r0, height), :] = gq
            return weights

        if m <= 4:
            weights = [tile(t, r0, 0) for t in range(k) for r0 in range(0, rows, height)]
            q = jnp.concatenate([ref[0:rows, :] for ref in qm_refs], axis=0)
            gv_ref[...] += jnp.dot(
                q.T, jnp.concatenate(weights, axis=0), preferred_element_type=F32
            )
        else:
            for t in range(k):
                for first in range(0, m, part):

                    def step(i, carry, t=t, first=first):
                        r0 = pl.multiple_of(i * height, height)
                        weights = tile(t, r0, first)
                        q = qm_refs[t][pl.ds(r0, height), :]
                        gv_ref[:, first * wide : (first + part) * wide] += jnp.dot(
                            q.T, weights, preferred_element_type=F32
                        )
                        return carry

                    lax.fori_loop(0, rows // height, step, 0)
        if code_last:
            encode_rows(last_ref, gq_refs[k - 1])
        for s in range(m):
            term = gv_ref[:, s * wide : (s + 1) * wide]
            if group[s] in send:
                code, exponent = encode(term)
                gv_outs[s][0:dim, :] = code
                gv_outs[s][dim:, :] = tail_of([exponent])
            else:
                gv_outs[s][...] = term

    operands = [*sets, *vds, *([] if fresh else [table]), *(gqs or []), *(gvs or [])]
    outs = [jax.ShapeDtypeStruct((rows, dim), F32)] * k + [
        jax.ShapeDtypeStruct((dim + TAIL, wide), I16)
        if s in send
        else jax.ShapeDtypeStruct((dim, wide), F32)
        for s in group
    ]
    if code_last:
        outs[k - 1] = jax.ShapeDtypeStruct((rows + TAIL, dim), I16)
    if fresh:
        outs.append(jax.ShapeDtypeStruct((chunks, k * pad, 128), F32))
    res = pl.pallas_call(
        kernel,
        out_shape=tuple(outs),
        in_specs=[VMEM] * len(operands),
        out_specs=(VMEM,) * len(outs),
        scratch_shapes=[
            pltpu.VMEM((dim, m * wide), F32),
            pltpu.VMEM((m * wide, dim), BF16),
            pltpu.VMEM((rows if code_last else 8, dim), F32),
        ],
        compiler_params=params(32),
        cost_estimate=cost(k * rows * m * wide, 1 << 10),
        name=name,
    )(*operands)
    return list(res[:k]), list(res[k : k + m]), res[-1] if fresh else table


def core_sum_kernel(y_ref, got_y_ref, y_out, sum_ref):
    sum_ref[...] = y_ref[...] + got_y_ref[...]
    encode_rows(sum_ref, y_out)


def finish_q_kernel(own_ref, got_own_ref, got_ref, gq_out):
    rows = own_ref.shape[0]
    tail = got_ref[rows : rows + TAIL, :].astype(jnp.int32).astype(F32)
    own_tail = got_own_ref[rows:, :].astype(jnp.int32).astype(F32)
    for b in range(rows // BLK):
        at = slice(b * BLK, (b + 1) * BLK)
        own = own_ref[at, :] + decode(got_own_ref[at, :], own_tail[b : b + 1, :])
        gq_out[at, :] = own + decode(got_ref[at, :], tail[b : b + 1, :])


def finish_v_kernel(term_ref, *refs):
    got_terms, (gv_out, gd_out) = refs[:-2], refs[-2:]
    total = term_ref[...]
    dim = total.shape[0]
    for got in got_terms:
        tail = got[dim:, :].astype(jnp.int32).astype(F32)
        total = total + decode(got[0:dim, :], tail[0:1, :])
    local_v = gv_out.shape[0]
    gv_out[...] = total[:, :local_v].T
    gd_out[...] = total[:, local_v:].T


def body(queries, vectors, decoded, mask):
    rows, dim = queries.shape
    local_v = vectors.shape[0]
    blocks = mask.shape[0]
    n = lax.axis_size("qry")
    chunks = n // 4
    wide = 2 * local_v
    scale = 1.0 / math.sqrt(local_v * n)
    pad = -(-blocks // 16) * 16

    def swap(x, bit):
        return lax.ppermute(x, "qry", [(i, i ^ bit) for i in range(n)])

    qm, vd = pl.pallas_call(
        pack_kernel,
        out_shape=(
            jax.ShapeDtypeStruct((rows + pad, dim), BF16),
            jax.ShapeDtypeStruct((wide, dim), BF16),
        ),
        in_specs=[HBM] * 4,
        out_specs=(VMEM, VMEM),
        scratch_shapes=[pltpu.VMEM(mask.shape, mask.dtype), pltpu.SemaphoreType.DMA((4,))],
        compiler_params=params(8),
        name="pack",
    )(*[pltpu.with_memory_space_constraint(x, pltpu.HBM) for x in (queries, vectors, decoded, mask)])
    row_out = jax.ShapeDtypeStruct((rows, dim), F32)
    quarter = chunks // 4
    groups = [tuple(range(g * quarter, (g + 1) * quarter)) for g in range(4)]
    half = 2 * quarter

    def add(sets, which, table, gqs, gvs, send, code_last, name):
        group = sum((groups[g] for g in which), ())
        return grads(
            sets, [vds[s] for s in group], group, chunks, rows, local_v, scale,
            table, gqs, gvs, send, code_last, name,
        )

    qm_y = swap(qm, 2)
    qm_c = swap(qm, 1)
    vds = [vd] + [swap(vd, 4 * s) for s in range(1, chunks)]
    own = [qm, qm_c]
    gq_o, gv0, table = add(own, [0], None, None, None, (), False, "own_0")
    gq_o, gv1, _ = add(own, [1], table, gq_o, None, (), False, "own_1")
    gq_y, gv01, table_y = add([qm_y], [0, 1], None, None, gv0 + gv1, (), False, "y_01")
    qm_y, gq_y, gv01, vds[half:] = lax.optimization_barrier((qm_y, gq_y, gv01, vds[half:]))
    qm_yc = swap(qm_y, 1)
    gq_y, gv23, _ = add([qm_y], [2, 3], table_y, gq_y, None, (), False, "y_23")
    near = tuple(range(1, half))
    gq_yc, gvs, _ = add([qm_yc], [0, 1, 2, 3], None, None, gv01 + gv23, near, False, "yc")
    got_y = swap(gq_yc[0], 1)
    far = tuple(range(half, chunks))
    gq_o, gv23, _ = add(own, [2, 3], table, gq_o, gvs[half:], far, True, "own_23")
    got_y, gv23 = lax.optimization_barrier((got_y, gv23))
    gq_message = pl.pallas_call(
        core_sum_kernel,
        out_shape=jax.ShapeDtypeStruct((rows + 2 * TAIL, dim), I16),
        in_specs=[VMEM] * 2,
        out_specs=VMEM,
        scratch_shapes=[pltpu.VMEM((rows, dim), F32)],
        compiler_params=params(16),
        name="core_sum",
    )(gq_y[0], got_y)
    gq_own, gq_c = gq_o
    got_own = swap(gq_c, 1)
    term, *messages = gvs[:half] + gv23
    got_message = swap(gq_message, 2)
    got_terms = [swap(x, 4 * s) for s, x in enumerate(messages, 1)]
    grad_q = pl.pallas_call(
        finish_q_kernel,
        out_shape=row_out,
        in_specs=[VMEM] * 3,
        out_specs=VMEM,
        compiler_params=params(16),
        name="finish_q",
    )(gq_own, got_own, got_message)
    grad_q, term = lax.optimization_barrier((grad_q, term))
    vec_out = jax.ShapeDtypeStruct((local_v, dim), F32)
    grad_v, grad_d = pl.pallas_call(
        finish_v_kernel,
        out_shape=(vec_out, vec_out),
        in_specs=[VMEM] * chunks,
        out_specs=(VMEM,) * 2,
        compiler_params=params(16),
        name="finish_v",
    )(term, *got_terms)
    return grad_q, grad_v, grad_d


def solution(mesh):
    placed = P(("groups", "qry"), None)
    return jax.shard_map(
        body,
        mesh=mesh,
        in_specs=(placed,) * 4,
        out_specs=(placed,) * 3,
        check_vma=False,
    )
```

time: 34.6 us -> 31.9 us (0.922)
  local copies, waits for them, and re-layouts: 1.8 us -> 0 us
  Pallas kernels: 11.9 us -> 10.4 us
  waiting for transfers between devices: 7.03 us -> 8.08 us
    unnamed x8 -> x0, local copies, waits for them, and re-layouts: 1.8 us -> none
    pallas_call x7 -> x6, Pallas kernels: 9.02 us -> 7.46 us  [grads(): pl.pallas_call(kernel, out_shape=tuple(outs), in_specs=[VMEM] * len(opera...]
    ppermute x12, waiting for transfers between devices: 7.03 us -> 8.08 us  [swap(): return lax.ppermute(x, 'qry', [(i, i ^ bit) for i in range(n)])]
    pallas_call x1, Pallas kernels: 1.76 us -> 1.04 us  [body(): pl.pallas_call(pack_kernel, out_shape=(jax.ShapeDtypeStruct((rows + pad,...]
    pallas_call x1 -> x2, Pallas kernels: 1.02 us -> 1.72 us  [the longest x1 0.94 us: body(): pl.pallas_call(finish_q_kernel, out_shape=row_out, in_specs=[VMEM] * 3, o...]
where the time goes in v4:
time: 31.9 us; the launch traced here: 31.7 us
  starting transfers between devices  12.6 us (39%)
  Pallas kernels  10.4 us (33%)
  waiting for transfers between devices  8.08 us (25%)
  between operations  0.69 us (2%)
    ppermute x12, starting transfers between devices, swap(): return lax.ppermute(x, 'qry', [(i, i ^ bit) for i in range(n)])  12.6 us
    ppermute x12, waiting for transfers between devices, swap(): return lax.ppermute(x, 'qry', [(i, i ^ bit) for i in range(n)])  8.08 us
    pallas_call x6, Pallas kernels, grads(): pl.pallas_call(kernel, out_shape=tuple(outs), in_specs=[VMEM] * len(opera...  7.46 us
    pallas_call x1, Pallas kernels, body(): pl.pallas_call(pack_kernel, out_shape=(jax.ShapeDtypeStruct((rows + pad,...  1.04 us
    pallas_call x1, Pallas kernels, body(): pl.pallas_call(finish_q_kernel, out_shape=row_out, in_specs=[VMEM] * 3, o...  0.94 us
    pallas_call x1, Pallas kernels, body(): pl.pallas_call(finish_v_kernel, out_shape=(vec_out, vec_out), in_specs=[V...  0.78 us
  transfers between devices with their start and end apart: 12, of which 6 were waited for; matrix products, arithmetic and copies ran while one was open for 0% of the time, Pallas kernels for 21%

profile of v4, /device:TPU:0, one launch (start us, length us, event | category | flops | bytes accessed | tf_op | source)
XLA Modules:
  0.0 31.7 jit_solution(3717687551575742745)
XLA Ops:
  0.6 1.0 %pack.1 = (bf16[1040,128]{1,0:T(8,128)(2,1)S(1)}, bf16[256,128]{1,0:T(8,128)(2,1)S(1)}) custom-call(bf16[1024,128]{1,0:T(8,128)(2,1)} %q_hbm.1, bf16[128,128]{1,0:T(8,128)(2,1)} %v_hbm.1, bf16[128,128]{1,0:T(8,128)(2,1)} %d_hbm.1, s32[4,8]{1,0:T(4,128)} %m_hbm.1), custom_call_target="tpu_custom_call" | custom-call | tf_op jit(solution)/shard_map/pack/pallas_call | solution.py:255
  1.7 0.5 %collective-permute-start = (bf16[1040,128]{1,0:T(8,128)(2,1)S(1)}, bf16[1040,128]{1,0:T(8,128)(2,1)S(1)}, u32[]{:S(2)}, u32[]{:S(2)}) collective-permute-start(bf16[1040,128]{1,0:T(8,128)(2,1)S(1)} %get-tuple-element.41.refs_0_), channel_id=1, source_target_pairs={{0,1},{1,0},{2,3},{3,2},{4,5},{5,4},{6,7},{7,6},{8,9},{9,8},{10,11... | collective-permute-start | bytes 798728 | tf_op jit(solution)/shard_map/ppermute | solution.py:253
  2.2 2.6 %collective-permute-start.1 = (bf16[1040,128]{1,0:T(8,128)(2,1)S(1)}, bf16[1040,128]{1,0:T(8,128)(2,1)S(1)}, u32[]{:S(2)}, u32[]{:S(2)}) collective-permute-start(bf16[1040,128]{1,0:T(8,128)(2,1)S(1)} %get-tuple-element.41.refs_0_), channel_id=1, source_target_pairs={{0,2},{1,3},{2,0},{3,1},{4,6},{5,7},{6,4},{7,5},{8,10},{9,11},{10,... | collective-permute-start | bytes 798728 | tf_op jit(solution)/shard_map/ppermute | solution.py:253
  4.8 1.6 %collective-permute-start.2 = (bf16[256,128]{1,0:T(8,128)(2,1)S(1)}, bf16[256,128]{1,0:T(8,128)(2,1)S(1)}, u32[]{:S(2)}, u32[]{:S(2)}) collective-permute-start(bf16[256,128]{1,0:T(8,128)(2,1)S(1)} %get-tuple-element.42.refs_2_.refs_1_), channel_id=1, source_target_pairs={{0,4},{1,5},{2,6},{3,7},{4,0},{5,1},{6,2},{7,3},{8,12},{9,13},{10,... | collective-permute-start | bytes 196616 | tf_op jit(solution)/shard_map/ppermute | solution.py:253
  6.4 2.5 %collective-permute-start.4 = (bf16[256,128]{1,0:T(8,128)(2,1)S(1)}, bf16[256,128]{1,0:T(8,128)(2,1)S(1)}, u32[]{:S(2)}, u32[]{:S(2)}) collective-permute-start(bf16[256,128]{1,0:T(8,128)(2,1)S(1)} %get-tuple-element.42.refs_2_.refs_1_), channel_id=1, source_target_pairs={{0,12},{1,13},{2,14},{3,15},{4,8},{5,9},{6,10},{7,11},{8,4},{9,5},... | collective-permute-start | bytes 196616 | tf_op jit(solution)/shard_map/ppermute | solution.py:253
  8.8 0.1 collective-permute-start.3
  9.0 0.0 collective-permute-done.refs_1_
  9.0 1.0 %own_0.1 = (f32[1024,128]{1,0:T(8,128)S(1)}, f32[1024,128]{1,0:T(8,128)S(1)}, f32[128,256]{1,0:T(8,128)S(1)}, f32[4,32,128]{2,1,0:T(8,128)S(1)}) custom-call(bf16[1040,128]{1,0:T(8,128)(2,1)S(1)} %get-tuple-element.41.refs_0_, bf16[1040,128]{1,0:T(8,128)(2,1)S(1)} %collective-permute-done.refs_1_, bf16[256,128]{1,0:T(8,128)(2,1)S(1)} %get-tuple-element.42.refs_2_.refs_1_), custom_call_target="tpu_custom_call" | custom-call | flops 524288 | bytes 1024 | tf_op jit(solution)/shard_map/own_0/pallas_call | solution.py:198
  10.0 0.0 collective-permute-done.2.refs_2_
  10.0 1.0 %own_1.1 = (f32[1024,128]{1,0:T(8,128)S(1)}, f32[1024,128]{1,0:T(8,128)S(1)}, f32[128,256]{1,0:T(8,128)S(1)}) custom-call(bf16[1040,128]{1,0:T(8,128)(2,1)S(1)} %get-tuple-element.41.refs_0_, bf16[1040,128]{1,0:T(8,128)(2,1)S(1)} %collective-permute-done.refs_1_, bf16[256,128]{1,0:T(8,128)(2,1)S(1)} %collective-permute-done.2.refs_2_, ...), custom_call_target="tpu_custom_call" | custom-call | flops 524288 | bytes 1024 | tf_op jit(solution)/shard_map/own_1/pallas_call | solution.py:198
  10.9 0.8 %collective-permute-done.1.refs_0_ = bf16[1040,128]{1,0:T(8,128)(2,1)S(1)} collective-permute-done((bf16[1040,128]{1,0:T(8,128)(2,1)S(1)}, bf16[1040,128]{1,0:T(8,128)(2,1)S(1)}, u32[]{:S(2)}, u32[]{:S(2)}) %collective-permute-start.1) | collective-permute-done | bytes 266272 | tf_op jit(solution)/shard_map/ppermute | solution.py:253
  11.8 1.0 %y_01.1 = (f32[1024,128]{1,0:T(8,128)S(1)}, f32[128,256]{1,0:T(8,128)S(1)}, f32[128,256]{1,0:T(8,128)S(1)}, f32[4,16,128]{2,1,0:T(8,128)S(1)}) custom-call(bf16[1040,128]{1,0:T(8,128)(2,1)S(1)} %collective-permute-done.1.refs_0_, bf16[256,128]{1,0:T(8,128)(2,1)S(1)} %get-tuple-element.42.refs_2_.refs_1_, ...), custom_call_target="tpu_custom_call" | custom-call | flops 524288 | bytes 1024 | tf_op jit(solution)/shard_map/y_01/pallas_call | solution.py:198
  12.8 0.3 collective-permute-done.4.refs_2_.refs_4_.refs_3_
  13.0 2.4 %collective-permute-done.3.refs_1_.refs_3_.refs_2_ = bf16[256,128]{1,0:T(8,128)(2,1)S(1)} collective-permute-done((bf16[256,128]{1,0:T(8,128)(2,1)S(1)}, bf16[256,128]{1,0:T(8,128)(2,1)S(1)}, u32[]{:S(2)}, u32[]{:S(2)}) %collective-permute-start.3) | collective-permute-done | bytes 65568 | tf_op jit(solution)/shard_map/ppermute | solution.py:253
  15.4 0.1 collective-permute-start.5
  15.5 1.0 %y_23.1 = (f32[1024,128]{1,0:T(8,128)S(1)}, f32[128,256]{1,0:T(8,128)S(1)}, f32[128,256]{1,0:T(8,128)S(1)}) custom-call(bf16[1040,128]{1,0:T(8,128)(2,1)S(1)} %collective-permute-done.1.refs_0_, bf16[256,128]{1,0:T(8,128)(2,1)S(1)} %collective-permute-done.3.refs_1_.refs_3_.refs_2_, bf16[256,128]{1,0:T(8,128)(2,1)S(1)} %collective-permute-done.4.refs_2_.refs_4_.refs_3_, ...), custom_call_target="tpu_custom_call" | custom-call | flops 524288 | bytes 1024 | tf_op jit(solution)/shard_map/y_23/pallas_call | solution.py:198
  16.4 0.5 %collective-permute-done.5.refs_0_ = bf16[1040,128]{1,0:T(8,128)(2,1)S(1)} collective-permute-done((bf16[1040,128]{1,0:T(8,128)(2,1)S(1)}, bf16[1040,128]{1,0:T(8,128)(2,1)S(1)}, u32[]{:S(2)}, u32[]{:S(2)}) %collective-permute-start.5) | collective-permute-done | bytes 266272 | tf_op jit(solution)/shard_map/ppermute | solution.py:253
  16.9 1.8 %yc.1 = (f32[1024,128]{1,0:T(8,128)S(1)}, f32[128,256]{1,0:T(8,128)S(1)}, s16[144,256]{1,0:T(8,128)(2,1)S(1)}, f32[128,256]{1,0:T(8,128)S(1)}, f32[128,256]{1,0:T(8,128)S(1)}, /*index=5*/f32[4,16,128]{2,1,0:T(8,128)}) custom-call(bf16[1040,128]{1,0:T(8,128)(2,1)S(1)} %collective-permute-done.5.refs_0_, ...), custom_call_target="tpu_custom_call" | custom-call | flops 1048576 | bytes 1024 | tf_op jit(solution)/shard_map/yc/pallas_call | solution.py:198
  18.7 0.1 collective-permute-start.7
  18.9 1.8 %own_23.1 = (f32[1024,128]{1,0:T(8,128)S(1)}, s16[1040,128]{1,0:T(8,128)(2,1)S(1)}, s16[144,256]{1,0:T(8,128)(2,1)S(1)}, s16[144,256]{1,0:T(8,128)(2,1)S(1)}) custom-call(bf16[1040,128]{1,0:T(8,128)(2,1)S(1)} %get-tuple-element.41.refs_0_, bf16[1040,128]{1,0:T(8,128)(2,1)S(1)} %collective-permute-done.refs_1_, ...), custom_call_target="tpu_custom_call" | custom-call | flops 1048576 | bytes 1024 | tf_op jit(solution)/shard_map/own_23/pallas_call | solution.py:198
  20.6 0.0 collective-permute-done.7.got_y_ref
  20.7 0.1 core_sum.1
  20.8 0.6 %collective-permute-start.8 = (s16[1056,128]{1,0:T(8,128)(2,1)S(1)}, s16[1056,128]{1,0:T(8,128)(2,1)S(1)}, u32[]{:S(2)}, u32[]{:S(2)}) collective-permute-start(s16[1056,128]{1,0:T(8,128)(2,1)S(1)} %core_sum.1), channel_id=1, source_target_pairs={{0,2},{1,3},{2,0},{3,1},{4,6},{5,7},{6,4},{7,5},{8,10},{9,11},{10,... | collective-permute-start | bytes 811016 | tf_op jit(solution)/shard_map/ppermute | solution.py:253
  21.4 0.1 collective-permute-start.6
  21.5 0.3 collective-permute-start.9
  21.8 2.9 %collective-permute-start.10 = (s16[144,256]{1,0:T(8,128)(2,1)S(1)}, s16[144,256]{1,0:T(8,128)(2,1)S(1)}, u32[]{:S(2)}, u32[]{:S(2)}) collective-permute-start(s16[144,256]{1,0:T(8,128)(2,1)S(1)} %get-tuple-element.75), channel_id=1, source_target_pairs={{0,8},{1,9},{2,10},{3,11},{4,12},{5,13},{6,14},{7,15},{8,0},{9,1},... | collective-permute-start | bytes 221192 | tf_op jit(solution)/shard_map/ppermute | solution.py:253
  24.7 1.2 %collective-permute-start.11 = (s16[144,256]{1,0:T(8,128)(2,1)S(1)}, s16[144,256]{1,0:T(8,128)(2,1)S(1)}, u32[]{:S(2)}, u32[]{:S(2)}) collective-permute-start(s16[144,256]{1,0:T(8,128)(2,1)S(1)} %get-tuple-element.76), channel_id=1, source_target_pairs={{0,12},{1,13},{2,14},{3,15},{4,8},{5,9},{6,10},{7,11},{8,4},{9,5},... | collective-permute-start | bytes 221192 | tf_op jit(solution)/shard_map/ppermute | solution.py:253
  25.9 0.0 collective-permute-done.6.got_own_ref
  25.9 3.8 %collective-permute-done.8.got_ref = s16[1056,128]{1,0:T(8,128)(2,1)S(1)} collective-permute-done((s16[1056,128]{1,0:T(8,128)(2,1)S(1)}, s16[1056,128]{1,0:T(8,128)(2,1)S(1)}, u32[]{:S(2)}, u32[]{:S(2)}) %collective-permute-start.8) | collective-permute-done | bytes 270368 | tf_op jit(solution)/shard_map/ppermute | solution.py:253
  29.6 0.9 %finish_q.1 = f32[1024,128]{1,0:T(8,128)} custom-call(f32[1024,128]{1,0:T(8,128)S(1)} %get-tuple-element.64.own_ref, s16[1040,128]{1,0:T(8,128)(2,1)S(1)} %collective-permute-done.6.got_own_ref, s16[1056,128]{1,0:T(8,128)(2,1)S(1)} %collective-permute-done.8.got_ref), custom_call_target="tpu_custom_call" | custom-call | tf_op jit(solution)/shard_map/finish_q/pallas_call | solution.py:309
  30.6 0.0 collective-permute-done.9.refs_0_
  30.6 0.4 %collective-permute-done.10.refs_1_ = s16[144,256]{1,0:T(8,128)(2,1)S(1)} collective-permute-done((s16[144,256]{1,0:T(8,128)(2,1)S(1)}, s16[144,256]{1,0:T(8,128)(2,1)S(1)}, u32[]{:S(2)}, u32[]{:S(2)}) %collective-permute-start.10) | collective-permute-done | bytes 73760 | tf_op jit(solution)/shard_map/ppermute | solution.py:253
  30.9 0.0 collective-permute-done.11.refs_2_
  30.9 0.8 %finish_v.1 = (f32[128,128]{1,0:T(8,128)}, f32[128,128]{1,0:T(8,128)}) custom-call(f32[128,256]{1,0:T(8,128)S(1)} %get-tuple-element.73.term_ref, s16[144,256]{1,0:T(8,128)(2,1)S(1)} %collective-permute-done.9.refs_0_, s16[144,256]{1,0:T(8,128)(2,1)S(1)} %collective-permute-done.10.refs_1_, s16[144,256]{1,0:T(8,128)(2,1)S(1)} %collective-permute-done.11.refs_2_), custom_call_target="tpu_custom_call" | custom-call | tf_op jit(solution)/shard_map/finish_v/pallas_call | solution.py:319
Async XLA Ops:
  1.7 7.3 %collective-permute-start = (bf16[1040,128]{1,0:T(8,128)(2,1)S(1)}, bf16[1040,128]{1,0:T(8,128)(2,1)S(1)}, u32[]{:S(2)}, u32[]{:S(2)}) collective-permute-start(bf16[1040,128]{1,0:T(8,128)(2,1)S(1)} %get-tuple-element.41.refs_0_), channel_id=1, source_target_pairs={{0,1},{1,0},{2,3},{3,2},{4,5},{5,4},{6,7},{7,6},{8,9},{9,8},{10,11... | collective-permute-start | bytes 798728 | tf_op jit(solution)/shard_map/ppermute | solution.py:253
  2.2 9.6 %collective-permute-start.1 = (bf16[1040,128]{1,0:T(8,128)(2,1)S(1)}, bf16[1040,128]{1,0:T(8,128)(2,1)S(1)}, u32[]{:S(2)}, u32[]{:S(2)}) collective-permute-start(bf16[1040,128]{1,0:T(8,128)(2,1)S(1)} %get-tuple-element.41.refs_0_), channel_id=1, source_target_pairs={{0,2},{1,3},{2,0},{3,1},{4,6},{5,7},{6,4},{7,5},{8,10},{9,11},{10,... | collective-permute-start | bytes 798728 | tf_op jit(solution)/shard_map/ppermute | solution.py:253
  4.8 5.2 %collective-permute-start.2 = (bf16[256,128]{1,0:T(8,128)(2,1)S(1)}, bf16[256,128]{1,0:T(8,128)(2,1)S(1)}, u32[]{:S(2)}, u32[]{:S(2)}) collective-permute-start(bf16[256,128]{1,0:T(8,128)(2,1)S(1)} %get-tuple-element.42.refs_2_.refs_1_), channel_id=1, source_target_pairs={{0,4},{1,5},{2,6},{3,7},{4,0},{5,1},{6,2},{7,3},{8,12},{9,13},{10,... | collective-permute-start | bytes 196616 | tf_op jit(solution)/shard_map/ppermute | solution.py:253
  6.4 6.6 %collective-permute-start.4 = (bf16[256,128]{1,0:T(8,128)(2,1)S(1)}, bf16[256,128]{1,0:T(8,128)(2,1)S(1)}, u32[]{:S(2)}, u32[]{:S(2)}) collective-permute-start(bf16[256,128]{1,0:T(8,128)(2,1)S(1)} %get-tuple-element.42.refs_2_.refs_1_), channel_id=1, source_target_pairs={{0,12},{1,13},{2,14},{3,15},{4,8},{5,9},{6,10},{7,11},{8,4},{9,5},... | collective-permute-start | bytes 196616 | tf_op jit(solution)/shard_map/ppermute | solution.py:253
  8.8 6.5 %collective-permute-start.3 = (bf16[256,128]{1,0:T(8,128)(2,1)S(1)}, bf16[256,128]{1,0:T(8,128)(2,1)S(1)}, u32[]{:S(2)}, u32[]{:S(2)}) collective-permute-start(bf16[256,128]{1,0:T(8,128)(2,1)S(1)} %get-tuple-element.42.refs_2_.refs_1_), channel_id=1, source_target_pairs={{0,8},{1,9},{2,10},{3,11},{4,12},{5,13},{6,14},{7,15},{8,0},{9,1},... | collective-permute-start | bytes 196616 | tf_op jit(solution)/shard_map/ppermute | solution.py:253
  15.4 1.5 %collective-permute-start.5 = (bf16[1040,128]{1,0:T(8,128)(2,1)S(1)}, bf16[1040,128]{1,0:T(8,128)(2,1)S(1)}, u32[]{:S(2)}, u32[]{:S(2)}) collective-permute-start(bf16[1040,128]{1,0:T(8,128)(2,1)S(1)} %collective-permute-done.1.refs_0_), channel_id=1, source_target_pairs={{0,1},{1,0},{2,3},{3,2},{4,5},{5,4},{6,7},{7,6},{8,9},{9,8},{10,11... | collective-permute-start | bytes 798728 | tf_op jit(solution)/shard_map/ppermute | solution.py:253
  18.7 1.9 %collective-permute-start.7 = (f32[1024,128]{1,0:T(8,128)S(1)}, f32[1024,128]{1,0:T(8,128)S(1)}, u32[]{:S(2)}, u32[]{:S(2)}) collective-permute-start(f32[1024,128]{1,0:T(8,128)S(1)} %get-tuple-element.67), channel_id=1, source_target_pairs={{0,1},{1,0},{2,3},{3,2},{4,5},{5,4},{6,7},{7,6},{8,9},{9,8},{10,11... | collective-permute-start | bytes 1572872 | tf_op jit(solution)/shard_map/ppermute | solution.py:253
  20.8 8.8 %collective-permute-start.8 = (s16[1056,128]{1,0:T(8,128)(2,1)S(1)}, s16[1056,128]{1,0:T(8,128)(2,1)S(1)}, u32[]{:S(2)}, u32[]{:S(2)}) collective-permute-start(s16[1056,128]{1,0:T(8,128)(2,1)S(1)} %core_sum.1), channel_id=1, source_target_pairs={{0,2},{1,3},{2,0},{3,1},{4,6},{5,7},{6,4},{7,5},{8,10},{9,11},{10,... | collective-permute-start | bytes 811016 | tf_op jit(solution)/shard_map/ppermute | solution.py:253
  21.4 4.5 %collective-permute-start.6 = (s16[1040,128]{1,0:T(8,128)(2,1)S(1)}, s16[1040,128]{1,0:T(8,128)(2,1)S(1)}, u32[]{:S(2)}, u32[]{:S(2)}) collective-permute-start(s16[1040,128]{1,0:T(8,128)(2,1)S(1)} %get-tuple-element.65), channel_id=1, source_target_pairs={{0,1},{1,0},{2,3},{3,2},{4,5},{5,4},{6,7},{7,6},{8,9},{9,8},{10,11... | collective-permute-start | bytes 798728 | tf_op jit(solution)/shard_map/ppermute | solution.py:253
  21.5 9.1 %collective-permute-start.9 = (s16[144,256]{1,0:T(8,128)(2,1)S(1)}, s16[144,256]{1,0:T(8,128)(2,1)S(1)}, u32[]{:S(2)}, u32[]{:S(2)}) collective-permute-start(s16[144,256]{1,0:T(8,128)(2,1)S(1)} %get-tuple-element.74), channel_id=1, source_target_pairs={{0,4},{1,5},{2,6},{3,7},{4,0},{5,1},{6,2},{7,3},{8,12},{9,13},{10,... | collective-permute-start | bytes 221192 | tf_op jit(solution)/shard_map/ppermute | solution.py:253
  21.8 9.2 %collective-permute-start.10 = (s16[144,256]{1,0:T(8,128)(2,1)S(1)}, s16[144,256]{1,0:T(8,128)(2,1)S(1)}, u32[]{:S(2)}, u32[]{:S(2)}) collective-permute-start(s16[144,256]{1,0:T(8,128)(2,1)S(1)} %get-tuple-element.75), channel_id=1, source_target_pairs={{0,8},{1,9},{2,10},{3,11},{4,12},{5,13},{6,14},{7,15},{8,0},{9,1},... | collective-permute-start | bytes 221192 | tf_op jit(solution)/shard_map/ppermute | solution.py:253
  24.7 6.3 %collective-permute-start.11 = (s16[144,256]{1,0:T(8,128)(2,1)S(1)}, s16[144,256]{1,0:T(8,128)(2,1)S(1)}, u32[]{:S(2)}, u32[]{:S(2)}) collective-permute-start(s16[144,256]{1,0:T(8,128)(2,1)S(1)} %get-tuple-element.76), channel_id=1, source_target_pairs={{0,12},{1,13},{2,14},{3,15},{4,8},{5,9},{6,10},{7,11},{8,4},{9,5},... | collective-permute-start | bytes 221192 | tf_op jit(solution)/shard_map/ppermute | solution.py:253

commit v5 on v4

--- a/solution.py
+++ b/solution.py
@@ -285,13 +285,12 @@
     gq_y, gv01, table_y = add([qm_y], [0, 1], None, None, gv0 + gv1, (), False, "y_01")
     qm_y, gq_y, gv01, vds[half:] = lax.optimization_barrier((qm_y, gq_y, gv01, vds[half:]))
     qm_yc = swap(qm_y, 1)
-    gq_y, gv23, _ = add([qm_y], [2, 3], table_y, gq_y, None, (), False, "y_23")
-    near = tuple(range(1, half))
+    gq_o, gv23, _ = add(own, [2, 3], table, gq_o, None, (), True, "own_23")
+    near, far = tuple(range(1, half)), tuple(range(half, chunks))
     gq_yc, gvs, _ = add([qm_yc], [0, 1, 2, 3], None, None, gv01 + gv23, near, False, "yc")
     got_y = swap(gq_yc[0], 1)
-    far = tuple(range(half, chunks))
-    gq_o, gv23, _ = add(own, [2, 3], table, gq_o, gvs[half:], far, True, "own_23")
-    got_y, gv23 = lax.optimization_barrier((got_y, gv23))
+    gq_y, gv23, _ = add([qm_y], [2, 3], table_y, gq_y, gvs[half:], far, False, "y_23")
+    got_y, gv01, gv23 = lax.optimization_barrier((got_y, gvs[:half], gv23))
     gq_message = pl.pallas_call(
         core_sum_kernel,
         out_shape=jax.ShapeDtypeStruct((rows + 2 * TAIL, dim), I16),
@@ -303,9 +302,9 @@
     )(gq_y[0], got_y)
     gq_own, gq_c = gq_o
     got_own = swap(gq_c, 1)
-    term, *messages = gvs[:half] + gv23
+    term, *messages = gv01 + gv23
     got_message = swap(gq_message, 2)
-    got_terms = [swap(x, 4 * s) for s, x in enumerate(messages, 1)]
+    got_terms = [swap(x, 4 * s) for s, x in reversed(list(enumerate(messages, 1)))]
     grad_q = pl.pallas_call(
         finish_q_kernel,
         out_shape=row_out,

time: 31.9 us -> 32.3 us (1.013)
  transfers between devices with their start and end apart: 12 -> 12, of which waited for: 6 -> 6; matrix products, arithmetic and copies ran while one was open for 0% -> 0% of each run, Pallas kernels for 21% -> 20%
where the time goes in v5:
time: 32.3 us; the launch traced here: 32.2 us
  starting transfers between devices  12.8 us (40%)
  Pallas kernels  10.4 us (32%)
  waiting for transfers between devices  8.23 us (25%)
  between operations  0.7 us (2%)
    ppermute x12, starting transfers between devices, swap(): return lax.ppermute(x, 'qry', [(i, i ^ bit) for i in range(n)])  12.8 us
    ppermute x12, waiting for transfers between devices, swap(): return lax.ppermute(x, 'qry', [(i, i ^ bit) for i in range(n)])  8.23 us
    pallas_call x6, Pallas kernels, grads(): pl.pallas_call(kernel, out_shape=tuple(outs), in_specs=[VMEM] * len(opera...  7.48 us
    pallas_call x1, Pallas kernels, body(): pl.pallas_call(pack_kernel, out_shape=(jax.ShapeDtypeStruct((rows + pad,...  1.04 us
    pallas_call x1, Pallas kernels, body(): pl.pallas_call(finish_q_kernel, out_shape=row_out, in_specs=[VMEM] * 3, o...  0.94 us
    pallas_call x1, Pallas kernels, body(): pl.pallas_call(finish_v_kernel, out_shape=(vec_out, vec_out), in_specs=[V...  0.78 us
  transfers between devices with their start and end apart: 12, of which 6 were waited for; matrix products, arithmetic and copies ran while one was open for 0% of the time, Pallas kernels for 20%

profile of v5, /device:TPU:0, one launch (start us, length us, event | category | flops | bytes accessed | tf_op | source)
XLA Modules:
  0.0 32.2 jit_solution(3845875410336725774)
XLA Ops:
  0.6 1.0 %pack.1 = (bf16[1040,128]{1,0:T(8,128)(2,1)S(1)}, bf16[256,128]{1,0:T(8,128)(2,1)S(1)}) custom-call(bf16[1024,128]{1,0:T(8,128)(2,1)} %q_hbm.1, bf16[128,128]{1,0:T(8,128)(2,1)} %v_hbm.1, bf16[128,128]{1,0:T(8,128)(2,1)} %d_hbm.1, s32[4,8]{1,0:T(4,128)} %m_hbm.1), custom_call_target="tpu_custom_call" | custom-call | tf_op jit(solution)/shard_map/pack/pallas_call | solution.py:255
  1.7 0.5 %collective-permute-start = (bf16[1040,128]{1,0:T(8,128)(2,1)S(1)}, bf16[1040,128]{1,0:T(8,128)(2,1)S(1)}, u32[]{:S(2)}, u32[]{:S(2)}) collective-permute-start(bf16[1040,128]{1,0:T(8,128)(2,1)S(1)} %get-tuple-element.43.refs_0_), channel_id=1, source_target_pairs={{0,1},{1,0},{2,3},{3,2},{4,5},{5,4},{6,7},{7,6},{8,9},{9,8},{10,11... | collective-permute-start | bytes 798728 | tf_op jit(solution)/shard_map/ppermute | solution.py:253
  2.2 2.6 %collective-permute-start.1 = (bf16[1040,128]{1,0:T(8,128)(2,1)S(1)}, bf16[1040,128]{1,0:T(8,128)(2,1)S(1)}, u32[]{:S(2)}, u32[]{:S(2)}) collective-permute-start(bf16[1040,128]{1,0:T(8,128)(2,1)S(1)} %get-tuple-element.43.refs_0_), channel_id=1, source_target_pairs={{0,2},{1,3},{2,0},{3,1},{4,6},{5,7},{6,4},{7,5},{8,10},{9,11},{10,... | collective-permute-start | bytes 798728 | tf_op jit(solution)/shard_map/ppermute | solution.py:253
  4.8 1.6 %collective-permute-start.2 = (bf16[256,128]{1,0:T(8,128)(2,1)S(1)}, bf16[256,128]{1,0:T(8,128)(2,1)S(1)}, u32[]{:S(2)}, u32[]{:S(2)}) collective-permute-start(bf16[256,128]{1,0:T(8,128)(2,1)S(1)} %get-tuple-element.44.refs_2_.refs_1_), channel_id=1, source_target_pairs={{0,4},{1,5},{2,6},{3,7},{4,0},{5,1},{6,2},{7,3},{8,12},{9,13},{10,... | collective-permute-start | bytes 196616 | tf_op jit(solution)/shard_map/ppermute | solution.py:253
  6.4 2.5 %collective-permute-start.4 = (bf16[256,128]{1,0:T(8,128)(2,1)S(1)}, bf16[256,128]{1,0:T(8,128)(2,1)S(1)}, u32[]{:S(2)}, u32[]{:S(2)}) collective-permute-start(bf16[256,128]{1,0:T(8,128)(2,1)S(1)} %get-tuple-element.44.refs_2_.refs_1_), channel_id=1, source_target_pairs={{0,12},{1,13},{2,14},{3,15},{4,8},{5,9},{6,10},{7,11},{8,4},{9,5},... | collective-permute-start | bytes 196616 | tf_op jit(solution)/shard_map/ppermute | solution.py:253
  8.8 0.1 collective-permute-start.3
  9.0 0.0 collective-permute-done.refs_1_
  9.0 1.0 %own_0.1 = (f32[1024,128]{1,0:T(8,128)S(1)}, f32[1024,128]{1,0:T(8,128)S(1)}, f32[128,256]{1,0:T(8,128)S(1)}, f32[4,32,128]{2,1,0:T(8,128)S(1)}) custom-call(bf16[1040,128]{1,0:T(8,128)(2,1)S(1)} %get-tuple-element.43.refs_0_, bf16[1040,128]{1,0:T(8,128)(2,1)S(1)} %collective-permute-done.refs_1_, bf16[256,128]{1,0:T(8,128)(2,1)S(1)} %get-tuple-element.44.refs_2_.refs_1_), custom_call_target="tpu_custom_call" | custom-call | flops 524288 | bytes 1024 | tf_op jit(solution)/shard_map/own_0/pallas_call | solution.py:198
  10.0 0.0 collective-permute-done.2.refs_2_
  10.0 1.0 %own_1.1 = (f32[1024,128]{1,0:T(8,128)S(1)}, f32[1024,128]{1,0:T(8,128)S(1)}, f32[128,256]{1,0:T(8,128)S(1)}) custom-call(bf16[1040,128]{1,0:T(8,128)(2,1)S(1)} %get-tuple-element.43.refs_0_, bf16[1040,128]{1,0:T(8,128)(2,1)S(1)} %collective-permute-done.refs_1_, bf16[256,128]{1,0:T(8,128)(2,1)S(1)} %collective-permute-done.2.refs_2_, ...), custom_call_target="tpu_custom_call" | custom-call | flops 524288 | bytes 1024 | tf_op jit(solution)/shard_map/own_1/pallas_call | solution.py:198
  11.0 0.8 %collective-permute-done.1.refs_0_ = bf16[1040,128]{1,0:T(8,128)(2,1)S(1)} collective-permute-done((bf16[1040,128]{1,0:T(8,128)(2,1)S(1)}, bf16[1040,128]{1,0:T(8,128)(2,1)S(1)}, u32[]{:S(2)}, u32[]{:S(2)}) %collective-permute-start.1) | collective-permute-done | bytes 266272 | tf_op jit(solution)/shard_map/ppermute | solution.py:253
  11.8 1.0 %y_01.1 = (f32[1024,128]{1,0:T(8,128)S(1)}, f32[128,256]{1,0:T(8,128)S(1)}, f32[128,256]{1,0:T(8,128)S(1)}, f32[4,16,128]{2,1,0:T(8,128)S(1)}) custom-call(bf16[1040,128]{1,0:T(8,128)(2,1)S(1)} %collective-permute-done.1.refs_0_, bf16[256,128]{1,0:T(8,128)(2,1)S(1)} %get-tuple-element.44.refs_2_.refs_1_, ...), custom_call_target="tpu_custom_call" | custom-call | flops 524288 | bytes 1024 | tf_op jit(solution)/shard_map/y_01/pallas_call | solution.py:198
  12.7 0.3 collective-permute-done.4.refs_3_.refs_4_.refs_2_
  13.0 2.4 %collective-permute-done.3.refs_2_.refs_3_.refs_1_ = bf16[256,128]{1,0:T(8,128)(2,1)S(1)} collective-permute-done((bf16[256,128]{1,0:T(8,128)(2,1)S(1)}, bf16[256,128]{1,0:T(8,128)(2,1)S(1)}, u32[]{:S(2)}, u32[]{:S(2)}) %collective-permute-start.3) | collective-permute-done | bytes 65568 | tf_op jit(solution)/shard_map/ppermute | solution.py:253
  15.4 0.1 collective-permute-start.6
  15.5 1.7 %own_23.1 = (f32[1024,128]{1,0:T(8,128)S(1)}, s16[1040,128]{1,0:T(8,128)(2,1)S(1)}, f32[128,256]{1,0:T(8,128)S(1)}, f32[128,256]{1,0:T(8,128)S(1)}) custom-call(bf16[1040,128]{1,0:T(8,128)(2,1)S(1)} %get-tuple-element.43.refs_0_, bf16[1040,128]{1,0:T(8,128)(2,1)S(1)} %collective-permute-done.refs_1_, ...), custom_call_target="tpu_custom_call" | custom-call | flops 1048576 | bytes 1024 | tf_op jit(solution)/shard_map/own_23/pallas_call | solution.py:198
  17.2 0.0 collective-permute-done.6.refs_0_
  17.2 1.8 %yc.1 = (f32[1024,128]{1,0:T(8,128)S(1)}, f32[128,256]{1,0:T(8,128)S(1)}, s16[144,256]{1,0:T(8,128)(2,1)S(1)}, f32[128,256]{1,0:T(8,128)S(1)}, f32[128,256]{1,0:T(8,128)S(1)}, /*index=5*/f32[4,16,128]{2,1,0:T(8,128)}) custom-call(bf16[1040,128]{1,0:T(8,128)(2,1)S(1)} %collective-permute-done.6.refs_0_, ...), custom_call_target="tpu_custom_call" | custom-call | flops 1048576 | bytes 1024 | tf_op jit(solution)/shard_map/yc/pallas_call | solution.py:198
  19.1 0.4 %collective-permute-start.7 = (f32[1024,128]{1,0:T(8,128)S(1)}, f32[1024,128]{1,0:T(8,128)S(1)}, u32[]{:S(2)}, u32[]{:S(2)}) collective-permute-start(f32[1024,128]{1,0:T(8,128)S(1)} %get-tuple-element.69), channel_id=1, source_target_pairs={{0,1},{1,0},{2,3},{3,2},{4,5},{5,4},{6,7},{7,6},{8,9},{9,8},{10,11... | collective-permute-start | bytes 1572872 | tf_op jit(solution)/shard_map/ppermute | solution.py:253
  19.5 1.0 %y_23.1 = (f32[1024,128]{1,0:T(8,128)S(1)}, s16[144,256]{1,0:T(8,128)(2,1)S(1)}, s16[144,256]{1,0:T(8,128)(2,1)S(1)}) custom-call(bf16[1040,128]{1,0:T(8,128)(2,1)S(1)} %collective-permute-done.1.refs_0_, bf16[256,128]{1,0:T(8,128)(2,1)S(1)} %collective-permute-done.3.refs_2_.refs_3_.refs_1_, ...), custom_call_target="tpu_custom_call" | custom-call | flops 524288 | bytes 1024 | tf_op jit(solution)/shard_map/y_23/pallas_call | solution.py:198
  20.4 0.6 %collective-permute-done.7.got_y_ref = f32[1024,128]{1,0:T(8,128)S(1)} collective-permute-done((f32[1024,128]{1,0:T(8,128)S(1)}, f32[1024,128]{1,0:T(8,128)S(1)}, u32[]{:S(2)}, u32[]{:S(2)}) %collective-permute-start.7) | collective-permute-done | bytes 524320 | tf_op jit(solution)/shard_map/ppermute | solution.py:253
  21.0 0.1 core_sum.1
  21.1 0.6 %collective-permute-start.8 = (s16[1056,128]{1,0:T(8,128)(2,1)S(1)}, s16[1056,128]{1,0:T(8,128)(2,1)S(1)}, u32[]{:S(2)}, u32[]{:S(2)}) collective-permute-start(s16[1056,128]{1,0:T(8,128)(2,1)S(1)} %core_sum.1), channel_id=1, source_target_pairs={{0,2},{1,3},{2,0},{3,1},{4,6},{5,7},{6,4},{7,5},{8,10},{9,11},{10,... | collective-permute-start | bytes 811016 | tf_op jit(solution)/shard_map/ppermute | solution.py:253
  21.7 0.1 collective-permute-start.5
  21.8 2.7 %collective-permute-start.9 = (s16[144,256]{1,0:T(8,128)(2,1)S(1)}, s16[144,256]{1,0:T(8,128)(2,1)S(1)}, u32[]{:S(2)}, u32[]{:S(2)}) collective-permute-start(s16[144,256]{1,0:T(8,128)(2,1)S(1)} %get-tuple-element.78), channel_id=1, source_target_pairs={{0,12},{1,13},{2,14},{3,15},{4,8},{5,9},{6,10},{7,11},{8,4},{9,5},... | collective-permute-start | bytes 221192 | tf_op jit(solution)/shard_map/ppermute | solution.py:253
  24.5 0.0 collective-permute-start.10
  24.5 1.7 %collective-permute-start.11 = (s16[144,256]{1,0:T(8,128)(2,1)S(1)}, s16[144,256]{1,0:T(8,128)(2,1)S(1)}, u32[]{:S(2)}, u32[]{:S(2)}) collective-permute-start(s16[144,256]{1,0:T(8,128)(2,1)S(1)} %get-tuple-element.80), channel_id=1, source_target_pairs={{0,4},{1,5},{2,6},{3,7},{4,0},{5,1},{6,2},{7,3},{8,12},{9,13},{10,... | collective-permute-start | bytes 221192 | tf_op jit(solution)/shard_map/ppermute | solution.py:253
  26.2 0.0 collective-permute-done.5.got_own_ref
  26.2 3.8 %collective-permute-done.8.got_ref = s16[1056,128]{1,0:T(8,128)(2,1)S(1)} collective-permute-done((s16[1056,128]{1,0:T(8,128)(2,1)S(1)}, s16[1056,128]{1,0:T(8,128)(2,1)S(1)}, u32[]{:S(2)}, u32[]{:S(2)}) %collective-permute-start.8) | collective-permute-done | bytes 270368 | tf_op jit(solution)/shard_map/ppermute | solution.py:253
  30.0 0.9 %finish_q.1 = f32[1024,128]{1,0:T(8,128)} custom-call(f32[1024,128]{1,0:T(8,128)S(1)} %get-tuple-element.57.own_ref, s16[1040,128]{1,0:T(8,128)(2,1)S(1)} %collective-permute-done.5.got_own_ref, s16[1056,128]{1,0:T(8,128)(2,1)S(1)} %collective-permute-done.8.got_ref), custom_call_target="tpu_custom_call" | custom-call | tf_op jit(solution)/shard_map/finish_q/pallas_call | solution.py:308
  30.9 0.0 collective-permute-done.9.refs_0_
  30.9 0.5 %collective-permute-done.10.refs_1_ = s16[144,256]{1,0:T(8,128)(2,1)S(1)} collective-permute-done((s16[144,256]{1,0:T(8,128)(2,1)S(1)}, s16[144,256]{1,0:T(8,128)(2,1)S(1)}, u32[]{:S(2)}, u32[]{:S(2)}) %collective-permute-start.10) | collective-permute-done | bytes 73760 | tf_op jit(solution)/shard_map/ppermute | solution.py:253
  31.4 0.0 collective-permute-done.11.refs_2_
  31.4 0.8 %finish_v.1 = (f32[128,128]{1,0:T(8,128)}, f32[128,128]{1,0:T(8,128)}) custom-call(f32[128,256]{1,0:T(8,128)S(1)} %get-tuple-element.77.term_ref, s16[144,256]{1,0:T(8,128)(2,1)S(1)} %collective-permute-done.9.refs_0_, s16[144,256]{1,0:T(8,128)(2,1)S(1)} %collective-permute-done.10.refs_1_, s16[144,256]{1,0:T(8,128)(2,1)S(1)} %collective-permute-done.11.refs_2_), custom_call_target="tpu_custom_call" | custom-call | tf_op jit(solution)/shard_map/finish_v/pallas_call | solution.py:318
Async XLA Ops:
  1.7 7.3 %collective-permute-start = (bf16[1040,128]{1,0:T(8,128)(2,1)S(1)}, bf16[1040,128]{1,0:T(8,128)(2,1)S(1)}, u32[]{:S(2)}, u32[]{:S(2)}) collective-permute-start(bf16[1040,128]{1,0:T(8,128)(2,1)S(1)} %get-tuple-element.43.refs_0_), channel_id=1, source_target_pairs={{0,1},{1,0},{2,3},{3,2},{4,5},{5,4},{6,7},{7,6},{8,9},{9,8},{10,11... | collective-permute-start | bytes 798728 | tf_op jit(solution)/shard_map/ppermute | solution.py:253
  2.2 9.6 %collective-permute-start.1 = (bf16[1040,128]{1,0:T(8,128)(2,1)S(1)}, bf16[1040,128]{1,0:T(8,128)(2,1)S(1)}, u32[]{:S(2)}, u32[]{:S(2)}) collective-permute-start(bf16[1040,128]{1,0:T(8,128)(2,1)S(1)} %get-tuple-element.43.refs_0_), channel_id=1, source_target_pairs={{0,2},{1,3},{2,0},{3,1},{4,6},{5,7},{6,4},{7,5},{8,10},{9,11},{10,... | collective-permute-start | bytes 798728 | tf_op jit(solution)/shard_map/ppermute | solution.py:253
  4.8 5.2 %collective-permute-start.2 = (bf16[256,128]{1,0:T(8,128)(2,1)S(1)}, bf16[256,128]{1,0:T(8,128)(2,1)S(1)}, u32[]{:S(2)}, u32[]{:S(2)}) collective-permute-start(bf16[256,128]{1,0:T(8,128)(2,1)S(1)} %get-tuple-element.44.refs_2_.refs_1_), channel_id=1, source_target_pairs={{0,4},{1,5},{2,6},{3,7},{4,0},{5,1},{6,2},{7,3},{8,12},{9,13},{10,... | collective-permute-start | bytes 196616 | tf_op jit(solution)/shard_map/ppermute | solution.py:253
  6.4 6.6 %collective-permute-start.4 = (bf16[256,128]{1,0:T(8,128)(2,1)S(1)}, bf16[256,128]{1,0:T(8,128)(2,1)S(1)}, u32[]{:S(2)}, u32[]{:S(2)}) collective-permute-start(bf16[256,128]{1,0:T(8,128)(2,1)S(1)} %get-tuple-element.44.refs_2_.refs_1_), channel_id=1, source_target_pairs={{0,12},{1,13},{2,14},{3,15},{4,8},{5,9},{6,10},{7,11},{8,4},{9,5},... | collective-permute-start | bytes 196616 | tf_op jit(solution)/shard_map/ppermute | solution.py:253
  8.8 6.5 %collective-permute-start.3 = (bf16[256,128]{1,0:T(8,128)(2,1)S(1)}, bf16[256,128]{1,0:T(8,128)(2,1)S(1)}, u32[]{:S(2)}, u32[]{:S(2)}) collective-permute-start(bf16[256,128]{1,0:T(8,128)(2,1)S(1)} %get-tuple-element.44.refs_2_.refs_1_), channel_id=1, source_target_pairs={{0,8},{1,9},{2,10},{3,11},{4,12},{5,13},{6,14},{7,15},{8,0},{9,1},... | collective-permute-start | bytes 196616 | tf_op jit(solution)/shard_map/ppermute | solution.py:253
  15.4 1.8 %collective-permute-start.6 = (bf16[1040,128]{1,0:T(8,128)(2,1)S(1)}, bf16[1040,128]{1,0:T(8,128)(2,1)S(1)}, u32[]{:S(2)}, u32[]{:S(2)}) collective-permute-start(bf16[1040,128]{1,0:T(8,128)(2,1)S(1)} %collective-permute-done.1.refs_0_), channel_id=1, source_target_pairs={{0,1},{1,0},{2,3},{3,2},{4,5},{5,4},{6,7},{7,6},{8,9},{9,8},{10,11... | collective-permute-start | bytes 798728 | tf_op jit(solution)/shard_map/ppermute | solution.py:253
  19.1 1.9 %collective-permute-start.7 = (f32[1024,128]{1,0:T(8,128)S(1)}, f32[1024,128]{1,0:T(8,128)S(1)}, u32[]{:S(2)}, u32[]{:S(2)}) collective-permute-start(f32[1024,128]{1,0:T(8,128)S(1)} %get-tuple-element.69), channel_id=1, source_target_pairs={{0,1},{1,0},{2,3},{3,2},{4,5},{5,4},{6,7},{7,6},{8,9},{9,8},{10,11... | collective-permute-start | bytes 1572872 | tf_op jit(solution)/shard_map/ppermute | solution.py:253
  21.1 8.8 %collective-permute-start.8 = (s16[1056,128]{1,0:T(8,128)(2,1)S(1)}, s16[1056,128]{1,0:T(8,128)(2,1)S(1)}, u32[]{:S(2)}, u32[]{:S(2)}) collective-permute-start(s16[1056,128]{1,0:T(8,128)(2,1)S(1)} %core_sum.1), channel_id=1, source_target_pairs={{0,2},{1,3},{2,0},{3,1},{4,6},{5,7},{6,4},{7,5},{8,10},{9,11},{10,... | collective-permute-start | bytes 811016 | tf_op jit(solution)/shard_map/ppermute | solution.py:253
  21.7 4.5 %collective-permute-start.5 = (s16[1040,128]{1,0:T(8,128)(2,1)S(1)}, s16[1040,128]{1,0:T(8,128)(2,1)S(1)}, u32[]{:S(2)}, u32[]{:S(2)}) collective-permute-start(s16[1040,128]{1,0:T(8,128)(2,1)S(1)} %get-tuple-element.58), channel_id=1, source_target_pairs={{0,1},{1,0},{2,3},{3,2},{4,5},{5,4},{6,7},{7,6},{8,9},{9,8},{10,11... | collective-permute-start | bytes 798728 | tf_op jit(solution)/shard_map/ppermute | solution.py:253
  21.8 9.1 %collective-permute-start.9 = (s16[144,256]{1,0:T(8,128)(2,1)S(1)}, s16[144,256]{1,0:T(8,128)(2,1)S(1)}, u32[]{:S(2)}, u32[]{:S(2)}) collective-permute-start(s16[144,256]{1,0:T(8,128)(2,1)S(1)} %get-tuple-element.78), channel_id=1, source_target_pairs={{0,12},{1,13},{2,14},{3,15},{4,8},{5,9},{6,10},{7,11},{8,4},{9,5},... | collective-permute-start | bytes 221192 | tf_op jit(solution)/shard_map/ppermute | solution.py:253
  24.5 6.9 %collective-permute-start.10 = (s16[144,256]{1,0:T(8,128)(2,1)S(1)}, s16[144,256]{1,0:T(8,128)(2,1)S(1)}, u32[]{:S(2)}, u32[]{:S(2)}) collective-permute-start(s16[144,256]{1,0:T(8,128)(2,1)S(1)} %get-tuple-element.79), channel_id=1, source_target_pairs={{0,8},{1,9},{2,10},{3,11},{4,12},{5,13},{6,14},{7,15},{8,0},{9,1},... | collective-permute-start | bytes 221192 | tf_op jit(solution)/shard_map/ppermute | solution.py:253
  24.5 6.9 %collective-permute-start.11 = (s16[144,256]{1,0:T(8,128)(2,1)S(1)}, s16[144,256]{1,0:T(8,128)(2,1)S(1)}, u32[]{:S(2)}, u32[]{:S(2)}) collective-permute-start(s16[144,256]{1,0:T(8,128)(2,1)S(1)} %get-tuple-element.80), channel_id=1, source_target_pairs={{0,4},{1,5},{2,6},{3,7},{4,0},{5,1},{6,2},{7,3},{8,12},{9,13},{10,... | collective-permute-start | bytes 221192 | tf_op jit(solution)/shard_map/ppermute | solution.py:253

commit v6 on v5

--- a/solution.py
+++ b/solution.py
@@ -11,6 +11,8 @@
 LOG2E = 1.4426950408889634
 LEVELS = 32000.0
 TAIL = 16
+HEAVY_Y = 1 << 14
+HEAVY_TERMS = 9000
 VMEM = pl.BlockSpec(memory_space=pltpu.VMEM)
 HBM = pl.BlockSpec(memory_space=pltpu.HBM)
 F32 = jnp.float32
@@ -103,7 +105,7 @@
     return jnp.concatenate(row_blocks, axis=0)
 
 
-def grads(sets, vds, group, chunks, rows, local_v, scale, table, gqs, gvs, send, code_last, name):
+def grads(sets, vds, group, chunks, rows, local_v, scale, table, gqs, gvs, send, code_last, name, weight):
     k, m = len(sets), len(vds)
     dim = sets[0].shape[1]
     pad = sets[0].shape[0] - rows
@@ -206,7 +208,7 @@
             pltpu.VMEM((rows if code_last else 8, dim), F32),
         ],
         compiler_params=params(32),
-        cost_estimate=cost(k * rows * m * wide, 1 << 10),
+        cost_estimate=cost(weight * k * rows * m * wide, 1 << 10),
         name=name,
     )(*operands)
     return list(res[:k]), list(res[k : k + m]), res[-1] if fresh else table
@@ -227,13 +229,22 @@
         gq_out[at, :] = own + decode(got_ref[at, :], tail[b : b + 1, :])
 
 
-def finish_v_kernel(term_ref, *refs):
-    got_terms, (gv_out, gd_out) = refs[:-2], refs[-2:]
+def sum_terms(term_ref, got_terms):
     total = term_ref[...]
     dim = total.shape[0]
     for got in got_terms:
         tail = got[dim:, :].astype(jnp.int32).astype(F32)
         total = total + decode(got[0:dim, :], tail[0:1, :])
+    return total
+
+
+def add_terms_kernel(term_ref, *refs):
+    refs[-1][...] = sum_terms(term_ref, refs[:-1])
+
+
+def finish_v_kernel(term_ref, *refs):
+    gv_out, gd_out = refs[-2:]
+    total = sum_terms(term_ref, refs[:-2])
     local_v = gv_out.shape[0]
     gv_out[...] = total[:, :local_v].T
     gd_out[...] = total[:, local_v:].T
@@ -269,28 +280,30 @@
     groups = [tuple(range(g * quarter, (g + 1) * quarter)) for g in range(4)]
     half = 2 * quarter
 
-    def add(sets, which, table, gqs, gvs, send, code_last, name):
+    def add(sets, which, table, gqs, gvs, send, name, code_last=False, weight=1):
         group = sum((groups[g] for g in which), ())
         return grads(
             sets, [vds[s] for s in group], group, chunks, rows, local_v, scale,
-            table, gqs, gvs, send, code_last, name,
+            table, gqs, gvs, send, code_last, name, weight,
         )
 
     qm_y = swap(qm, 2)
     qm_c = swap(qm, 1)
     vds = [vd] + [swap(vd, 4 * s) for s in range(1, chunks)]
     own = [qm, qm_c]
-    gq_o, gv0, table = add(own, [0], None, None, None, (), False, "own_0")
-    gq_o, gv1, _ = add(own, [1], table, gq_o, None, (), False, "own_1")
-    gq_y, gv01, table_y = add([qm_y], [0, 1], None, None, gv0 + gv1, (), False, "y_01")
-    qm_y, gq_y, gv01, vds[half:] = lax.optimization_barrier((qm_y, gq_y, gv01, vds[half:]))
+    near, far = tuple(range(1, half)), tuple(range(half, chunks))
+    gq_o, gv0, table = add(own, [0], None, None, None, (), "own_0")
+    gq_o, gv1, _ = add(own, [1], table, gq_o, None, (), "own_1")
+    qm_y, gv1 = lax.optimization_barrier((qm_y, gv1))
     qm_yc = swap(qm_y, 1)
-    gq_o, gv23, _ = add(own, [2, 3], table, gq_o, None, (), True, "own_23")
-    near, far = tuple(range(1, half)), tuple(range(half, chunks))
-    gq_yc, gvs, _ = add([qm_yc], [0, 1, 2, 3], None, None, gv01 + gv23, near, False, "yc")
+    gq_y, gv01, table_y = add([qm_y], [0, 1], None, None, gv0 + gv1, (), "y_01", weight=HEAVY_Y)
+    gq_yc, gv01, table_yc = add([qm_yc], [0, 1], None, None, gv01, near, "yc_01")
+    gq_yc, gv01, vds[half:] = lax.optimization_barrier((gq_yc, gv01, vds[half:]))
+    gq_yc, gv23, _ = add([qm_yc], [2, 3], table_yc, gq_yc, None, (), "yc_23")
     got_y = swap(gq_yc[0], 1)
-    gq_y, gv23, _ = add([qm_y], [2, 3], table_y, gq_y, gvs[half:], far, False, "y_23")
-    got_y, gv01, gv23 = lax.optimization_barrier((got_y, gvs[:half], gv23))
+    gq_y, gv23, _ = add([qm_y], [2, 3], table_y, gq_y, gv23, (), "y_23")
+    gq_o, gv23, _ = add(own, [2, 3], table, gq_o, gv23, far, "own_23", code_last=True)
+    got_y, gv01, gv23 = lax.optimization_barrier((got_y, gv01, gv23))
     gq_message = pl.pallas_call(
         core_sum_kernel,
         out_shape=jax.ShapeDtypeStruct((rows + 2 * TAIL, dim), I16),
@@ -305,6 +318,17 @@
     term, *messages = gv01 + gv23
     got_message = swap(gq_message, 2)
     got_terms = [swap(x, 4 * s) for s, x in reversed(list(enumerate(messages, 1)))]
+    first, rest = got_terms[:quarter], got_terms[quarter:]
+    term = pl.pallas_call(
+        add_terms_kernel,
+        out_shape=jax.ShapeDtypeStruct((dim, wide), F32),
+        in_specs=[VMEM] * (1 + len(first)),
+        out_specs=VMEM,
+        compiler_params=params(16),
+        cost_estimate=cost(HEAVY_TERMS * rows * wide, 1 << 10),
+        name="add_terms",
+    )(term, *first)
+    gq_own, term = lax.optimization_barrier((gq_own, term))
     grad_q = pl.pallas_call(
         finish_q_kernel,
         out_shape=row_out,
@@ -318,11 +342,11 @@
     grad_v, grad_d = pl.pallas_call(
         finish_v_kernel,
         out_shape=(vec_out, vec_out),
-        in_specs=[VMEM] * chunks,
+        in_specs=[VMEM] * (1 + len(rest)),
         out_specs=(VMEM,) * 2,
         compiler_params=params(16),
         name="finish_v",
-    )(term, *got_terms)
+    )(term, *rest)
     return grad_q, grad_v, grad_d
 
 

time: 32.3 us -> 32.7 us (1.012)
    pallas_call x6 -> x7, Pallas kernels: 7.48 us -> 7.6 us  [grads(): pl.pallas_call(kernel, out_shape=tuple(outs), in_specs=[VMEM] * len(opera...]
  transfers between devices with their start and end apart: 12 -> 12, of which waited for: 6 -> 5; matrix products, arithmetic and copies ran while one was open for 0% -> 0% of each run, Pallas kernels for 20% -> 24%
where the time goes in v6:
time: 32.7 us; the launch traced here: 32.5 us
  starting transfers between devices  12.8 us (39%)
  Pallas kernels  10.5 us (32%)
  waiting for transfers between devices  8.55 us (26%)
  between operations  0.73 us (2%)
    ppermute x12, starting transfers between devices, swap(): return lax.ppermute(x, 'qry', [(i, i ^ bit) for i in range(n)])  12.8 us
    ppermute x12, waiting for transfers between devices, swap(): return lax.ppermute(x, 'qry', [(i, i ^ bit) for i in range(n)])  8.55 us
    pallas_call x7, Pallas kernels, grads(): pl.pallas_call(kernel, out_shape=tuple(outs), in_specs=[VMEM] * len(opera...  7.6 us
    pallas_call x1, Pallas kernels, body(): pl.pallas_call(pack_kernel, out_shape=(jax.ShapeDtypeStruct((rows + pad,...  1.04 us
    pallas_call x1, Pallas kernels, body(): pl.pallas_call(finish_q_kernel, out_shape=row_out, in_specs=[VMEM] * 3, o...  0.94 us
    pallas_call x1, Pallas kernels, body(): pl.pallas_call(finish_v_kernel, out_shape=(vec_out, vec_out), in_specs=[V...  0.77 us
  transfers between devices with their start and end apart: 12, of which 5 were waited for; matrix products, arithmetic and copies ran while one was open for 0% of the time, Pallas kernels for 24%

profile of v6, /device:TPU:0, one launch (start us, length us, event | category | flops | bytes accessed | tf_op | source)
XLA Modules:
  0.0 32.5 jit_solution(257078482741061824)
XLA Ops:
  0.6 1.0 %pack.1 = (bf16[1040,128]{1,0:T(8,128)(2,1)S(1)}, bf16[256,128]{1,0:T(8,128)(2,1)S(1)}) custom-call(bf16[1024,128]{1,0:T(8,128)(2,1)} %q_hbm.1, bf16[128,128]{1,0:T(8,128)(2,1)} %v_hbm.1, bf16[128,128]{1,0:T(8,128)(2,1)} %d_hbm.1, s32[4,8]{1,0:T(4,128)} %m_hbm.1), custom_call_target="tpu_custom_call" | custom-call | tf_op jit(solution)/shard_map/pack/pallas_call | solution.py:266
  1.7 0.5 %collective-permute-start = (bf16[1040,128]{1,0:T(8,128)(2,1)S(1)}, bf16[1040,128]{1,0:T(8,128)(2,1)S(1)}, u32[]{:S(2)}, u32[]{:S(2)}) collective-permute-start(bf16[1040,128]{1,0:T(8,128)(2,1)S(1)} %get-tuple-element.48.refs_0_), channel_id=1, source_target_pairs={{0,1},{1,0},{2,3},{3,2},{4,5},{5,4},{6,7},{7,6},{8,9},{9,8},{10,11... | collective-permute-start | bytes 798728 | tf_op jit(solution)/shard_map/ppermute | solution.py:264
  2.2 2.6 %collective-permute-start.1 = (bf16[1040,128]{1,0:T(8,128)(2,1)S(1)}, bf16[1040,128]{1,0:T(8,128)(2,1)S(1)}, u32[]{:S(2)}, u32[]{:S(2)}) collective-permute-start(bf16[1040,128]{1,0:T(8,128)(2,1)S(1)} %get-tuple-element.48.refs_0_), channel_id=1, source_target_pairs={{0,2},{1,3},{2,0},{3,1},{4,6},{5,7},{6,4},{7,5},{8,10},{9,11},{10,... | collective-permute-start | bytes 798728 | tf_op jit(solution)/shard_map/ppermute | solution.py:264
  4.8 1.6 %collective-permute-start.2 = (bf16[256,128]{1,0:T(8,128)(2,1)S(1)}, bf16[256,128]{1,0:T(8,128)(2,1)S(1)}, u32[]{:S(2)}, u32[]{:S(2)}) collective-permute-start(bf16[256,128]{1,0:T(8,128)(2,1)S(1)} %get-tuple-element.49.refs_2_.refs_1_), channel_id=1, source_target_pairs={{0,4},{1,5},{2,6},{3,7},{4,0},{5,1},{6,2},{7,3},{8,12},{9,13},{10,... | collective-permute-start | bytes 196616 | tf_op jit(solution)/shard_map/ppermute | solution.py:264
  6.4 2.5 %collective-permute-start.5 = (bf16[256,128]{1,0:T(8,128)(2,1)S(1)}, bf16[256,128]{1,0:T(8,128)(2,1)S(1)}, u32[]{:S(2)}, u32[]{:S(2)}) collective-permute-start(bf16[256,128]{1,0:T(8,128)(2,1)S(1)} %get-tuple-element.49.refs_2_.refs_1_), channel_id=1, source_target_pairs={{0,12},{1,13},{2,14},{3,15},{4,8},{5,9},{6,10},{7,11},{8,4},{9,5},... | collective-permute-start | bytes 196616 | tf_op jit(solution)/shard_map/ppermute | solution.py:264
  8.8 0.1 collective-permute-start.4
  9.0 0.0 collective-permute-done.refs_1_
  9.0 1.0 %own_0.1 = (f32[1024,128]{1,0:T(8,128)S(1)}, f32[1024,128]{1,0:T(8,128)S(1)}, f32[128,256]{1,0:T(8,128)S(1)}, f32[4,32,128]{2,1,0:T(8,128)S(1)}) custom-call(bf16[1040,128]{1,0:T(8,128)(2,1)S(1)} %get-tuple-element.48.refs_0_, bf16[1040,128]{1,0:T(8,128)(2,1)S(1)} %collective-permute-done.refs_1_, bf16[256,128]{1,0:T(8,128)(2,1)S(1)} %get-tuple-element.49.refs_2_.refs_1_), custom_call_target="tpu_custom_call" | custom-call | flops 524288 | bytes 1024 | tf_op jit(solution)/shard_map/own_0/pallas_call | solution.py:200
  10.0 0.0 collective-permute-done.2.refs_2_
  10.0 1.0 %own_1.1 = (f32[1024,128]{1,0:T(8,128)S(1)}, f32[1024,128]{1,0:T(8,128)S(1)}, f32[128,256]{1,0:T(8,128)S(1)}) custom-call(bf16[1040,128]{1,0:T(8,128)(2,1)S(1)} %get-tuple-element.48.refs_0_, bf16[1040,128]{1,0:T(8,128)(2,1)S(1)} %collective-permute-done.refs_1_, bf16[256,128]{1,0:T(8,128)(2,1)S(1)} %collective-permute-done.2.refs_2_, ...), custom_call_target="tpu_custom_call" | custom-call | flops 524288 | bytes 1024 | tf_op jit(solution)/shard_map/own_1/pallas_call | solution.py:200
  11.0 0.8 %collective-permute-done.1.refs_0_ = bf16[1040,128]{1,0:T(8,128)(2,1)S(1)} collective-permute-done((bf16[1040,128]{1,0:T(8,128)(2,1)S(1)}, bf16[1040,128]{1,0:T(8,128)(2,1)S(1)}, u32[]{:S(2)}, u32[]{:S(2)}) %collective-permute-start.1) | collective-permute-done | bytes 266272 | tf_op jit(solution)/shard_map/ppermute | solution.py:264
  11.8 0.0 collective-permute-start.3
  11.8 1.0 %y_01.1 = (f32[1024,128]{1,0:T(8,128)S(1)}, f32[128,256]{1,0:T(8,128)S(1)}, f32[128,256]{1,0:T(8,128)S(1)}, f32[4,16,128]{2,1,0:T(8,128)S(1)}) custom-call(bf16[1040,128]{1,0:T(8,128)(2,1)S(1)} %collective-permute-done.1.refs_0_, bf16[256,128]{1,0:T(8,128)(2,1)S(1)} %get-tuple-element.49.refs_2_.refs_1_, ...), custom_call_target="tpu_custom_call" | custom-call | flops 8589934592 | bytes 1024 | tf_op jit(solution)/shard_map/y_01/pallas_call | solution.py:200
  12.8 0.6 %collective-permute-done.3.refs_0_ = bf16[1040,128]{1,0:T(8,128)(2,1)S(1)} collective-permute-done((bf16[1040,128]{1,0:T(8,128)(2,1)S(1)}, bf16[1040,128]{1,0:T(8,128)(2,1)S(1)}, u32[]{:S(2)}, u32[]{:S(2)}) %collective-permute-start.3) | collective-permute-done | bytes 266272 | tf_op jit(solution)/shard_map/ppermute | solution.py:264
  13.3 1.0 %yc_01.1 = (f32[1024,128]{1,0:T(8,128)S(1)}, f32[128,256]{1,0:T(8,128)S(1)}, s16[144,256]{1,0:T(8,128)(2,1)S(1)}, f32[4,16,128]{2,1,0:T(8,128)S(1)}) custom-call(bf16[1040,128]{1,0:T(8,128)(2,1)S(1)} %collective-permute-done.3.refs_0_, bf16[256,128]{1,0:T(8,128)(2,1)S(1)} %get-tuple-element.49.refs_2_.refs_1_, ...), custom_call_target="tpu_custom_call" | custom-call | flops 524288 | bytes 1024 | tf_op jit(solution)/shard_map/yc_01/pallas_call | solution.py:200
  14.3 0.0 collective-permute-done.5.refs_2_.refs_3_
  14.3 1.0 %collective-permute-done.4.refs_1_.refs_2_ = bf16[256,128]{1,0:T(8,128)(2,1)S(1)} collective-permute-done((bf16[256,128]{1,0:T(8,128)(2,1)S(1)}, bf16[256,128]{1,0:T(8,128)(2,1)S(1)}, u32[]{:S(2)}, u32[]{:S(2)}) %collective-permute-start.4) | collective-permute-done | bytes 65568 | tf_op jit(solution)/shard_map/ppermute | solution.py:264
  15.4 1.0 %yc_23.1 = (f32[1024,128]{1,0:T(8,128)S(1)}, f32[128,256]{1,0:T(8,128)S(1)}, f32[128,256]{1,0:T(8,128)S(1)}) custom-call(bf16[1040,128]{1,0:T(8,128)(2,1)S(1)} %collective-permute-done.3.refs_0_, bf16[256,128]{1,0:T(8,128)(2,1)S(1)} %collective-permute-done.4.refs_1_.refs_2_, bf16[256,128]{1,0:T(8,128)(2,1)S(1)} %collective-permute-done.5.refs_2_.refs_3_, ...), custom_call_target="tpu_custom_call" | custom-call | flops 524288 | bytes 1024 | tf_op jit(solution)/shard_map/yc_23/pallas_call | solution.py:200
  16.3 0.2 collective-permute-start.6
  16.5 1.0 %y_23.1 = (f32[1024,128]{1,0:T(8,128)S(1)}, f32[128,256]{1,0:T(8,128)S(1)}, f32[128,256]{1,0:T(8,128)S(1)}) custom-call(bf16[1040,128]{1,0:T(8,128)(2,1)S(1)} %collective-permute-done.1.refs_0_, bf16[256,128]{1,0:T(8,128)(2,1)S(1)} %collective-permute-done.4.refs_1_.refs_2_, bf16[256,128]{1,0:T(8,128)(2,1)S(1)} %collective-permute-done.5.refs_2_.refs_3_, ...), custom_call_target="tpu_custom_call" | custom-call | flops 524288 | bytes 1024 | tf_op jit(solution)/shard_map/y_23/pallas_call | solution.py:200
  17.5 1.8 %own_23.1 = (f32[1024,128]{1,0:T(8,128)S(1)}, s16[1040,128]{1,0:T(8,128)(2,1)S(1)}, s16[144,256]{1,0:T(8,128)(2,1)S(1)}, s16[144,256]{1,0:T(8,128)(2,1)S(1)}) custom-call(bf16[1040,128]{1,0:T(8,128)(2,1)S(1)} %get-tuple-element.48.refs_0_, bf16[1040,128]{1,0:T(8,128)(2,1)S(1)} %collective-permute-done.refs_1_, ...), custom_call_target="tpu_custom_call" | custom-call | flops 1048576 | bytes 1024 | tf_op jit(solution)/shard_map/own_23/pallas_call | solution.py:200
  19.2 0.0 collective-permute-done.6.got_y_ref
  19.2 2.9 %collective-permute-start.7 = (s16[144,256]{1,0:T(8,128)(2,1)S(1)}, s16[144,256]{1,0:T(8,128)(2,1)S(1)}, u32[]{:S(2)}, u32[]{:S(2)}) collective-permute-start(s16[144,256]{1,0:T(8,128)(2,1)S(1)} %get-tuple-element.81), channel_id=1, source_target_pairs={{0,12},{1,13},{2,14},{3,15},{4,8},{5,9},{6,10},{7,11},{8,4},{9,5},... | collective-permute-start | bytes 221192 | tf_op jit(solution)/shard_map/ppermute | solution.py:264
  22.2 0.1 core_sum.1
  22.3 1.6 %collective-permute-start.9 = (s16[1056,128]{1,0:T(8,128)(2,1)S(1)}, s16[1056,128]{1,0:T(8,128)(2,1)S(1)}, u32[]{:S(2)}, u32[]{:S(2)}) collective-permute-start(s16[1056,128]{1,0:T(8,128)(2,1)S(1)} %core_sum.1), channel_id=1, source_target_pairs={{0,2},{1,3},{2,0},{3,1},{4,6},{5,7},{6,4},{7,5},{8,10},{9,11},{10,... | collective-permute-start | bytes 811016 | tf_op jit(solution)/shard_map/ppermute | solution.py:264
  23.9 0.0 collective-permute-start.8
  23.9 0.0 collective-permute-start.10
  23.9 0.8 %collective-permute-start.11 = (s16[144,256]{1,0:T(8,128)(2,1)S(1)}, s16[144,256]{1,0:T(8,128)(2,1)S(1)}, u32[]{:S(2)}, u32[]{:S(2)}) collective-permute-start(s16[144,256]{1,0:T(8,128)(2,1)S(1)} %get-tuple-element.90), channel_id=1, source_target_pairs={{0,4},{1,5},{2,6},{3,7},{4,0},{5,1},{6,2},{7,3},{8,12},{9,13},{10,... | collective-permute-start | bytes 221192 | tf_op jit(solution)/shard_map/ppermute | solution.py:264
  24.7 1.0 %collective-permute-done.7.refs_0_ = s16[144,256]{1,0:T(8,128)(2,1)S(1)} collective-permute-done((s16[144,256]{1,0:T(8,128)(2,1)S(1)}, s16[144,256]{1,0:T(8,128)(2,1)S(1)}, u32[]{:S(2)}, u32[]{:S(2)}) %collective-permute-start.7) | collective-permute-done | bytes 73760 | tf_op jit(solution)/shard_map/ppermute | solution.py:264
  25.7 0.0 collective-permute-done.8.got_own_ref
  25.7 5.1 %collective-permute-done.9.got_ref = s16[1056,128]{1,0:T(8,128)(2,1)S(1)} collective-permute-done((s16[1056,128]{1,0:T(8,128)(2,1)S(1)}, s16[1056,128]{1,0:T(8,128)(2,1)S(1)}, u32[]{:S(2)}, u32[]{:S(2)}) %collective-permute-start.9) | collective-permute-done | bytes 270368 | tf_op jit(solution)/shard_map/ppermute | solution.py:264
  30.8 0.9 %finish_q.1 = f32[1024,128]{1,0:T(8,128)} custom-call(f32[1024,128]{1,0:T(8,128)S(1)} %get-tuple-element.82.own_ref, s16[1040,128]{1,0:T(8,128)(2,1)S(1)} %collective-permute-done.8.got_own_ref, s16[1056,128]{1,0:T(8,128)(2,1)S(1)} %collective-permute-done.9.got_ref), custom_call_target="tpu_custom_call" | custom-call | tf_op jit(solution)/shard_map/finish_q/pallas_call | solution.py:332
  31.8 0.0 collective-permute-done.10.refs_0_
  31.8 0.0 collective-permute-done.11.refs_1_
  31.8 0.8 %finish_v.1 = (f32[128,128]{1,0:T(8,128)}, f32[128,128]{1,0:T(8,128)}) custom-call(f32[128,256]{1,0:T(8,128)S(1)} %add_terms.1.term_ref, s16[144,256]{1,0:T(8,128)(2,1)S(1)} %collective-permute-done.10.refs_0_, s16[144,256]{1,0:T(8,128)(2,1)S(1)} %collective-permute-done.11.refs_1_), custom_call_target="tpu_custom_call" | custom-call | tf_op jit(solution)/shard_map/finish_v/pallas_call | solution.py:342
  (1 shorter events, 0.0 us)
Async XLA Ops:
  1.7 7.3 %collective-permute-start = (bf16[1040,128]{1,0:T(8,128)(2,1)S(1)}, bf16[1040,128]{1,0:T(8,128)(2,1)S(1)}, u32[]{:S(2)}, u32[]{:S(2)}) collective-permute-start(bf16[1040,128]{1,0:T(8,128)(2,1)S(1)} %get-tuple-element.48.refs_0_), channel_id=1, source_target_pairs={{0,1},{1,0},{2,3},{3,2},{4,5},{5,4},{6,7},{7,6},{8,9},{9,8},{10,11... | collective-permute-start | bytes 798728 | tf_op jit(solution)/shard_map/ppermute | solution.py:264
  2.2 9.6 %collective-permute-start.1 = (bf16[1040,128]{1,0:T(8,128)(2,1)S(1)}, bf16[1040,128]{1,0:T(8,128)(2,1)S(1)}, u32[]{:S(2)}, u32[]{:S(2)}) collective-permute-start(bf16[1040,128]{1,0:T(8,128)(2,1)S(1)} %get-tuple-element.48.refs_0_), channel_id=1, source_target_pairs={{0,2},{1,3},{2,0},{3,1},{4,6},{5,7},{6,4},{7,5},{8,10},{9,11},{10,... | collective-permute-start | bytes 798728 | tf_op jit(solution)/shard_map/ppermute | solution.py:264
  4.8 5.2 %collective-permute-start.2 = (bf16[256,128]{1,0:T(8,128)(2,1)S(1)}, bf16[256,128]{1,0:T(8,128)(2,1)S(1)}, u32[]{:S(2)}, u32[]{:S(2)}) collective-permute-start(bf16[256,128]{1,0:T(8,128)(2,1)S(1)} %get-tuple-element.49.refs_2_.refs_1_), channel_id=1, source_target_pairs={{0,4},{1,5},{2,6},{3,7},{4,0},{5,1},{6,2},{7,3},{8,12},{9,13},{10,... | collective-permute-start | bytes 196616 | tf_op jit(solution)/shard_map/ppermute | solution.py:264
  6.4 8.0 %collective-permute-start.5 = (bf16[256,128]{1,0:T(8,128)(2,1)S(1)}, bf16[256,128]{1,0:T(8,128)(2,1)S(1)}, u32[]{:S(2)}, u32[]{:S(2)}) collective-permute-start(bf16[256,128]{1,0:T(8,128)(2,1)S(1)} %get-tuple-element.49.refs_2_.refs_1_), channel_id=1, source_target_pairs={{0,12},{1,13},{2,14},{3,15},{4,8},{5,9},{6,10},{7,11},{8,4},{9,5},... | collective-permute-start | bytes 196616 | tf_op jit(solution)/shard_map/ppermute | solution.py:264
  8.8 6.5 %collective-permute-start.4 = (bf16[256,128]{1,0:T(8,128)(2,1)S(1)}, bf16[256,128]{1,0:T(8,128)(2,1)S(1)}, u32[]{:S(2)}, u32[]{:S(2)}) collective-permute-start(bf16[256,128]{1,0:T(8,128)(2,1)S(1)} %get-tuple-element.49.refs_2_.refs_1_), channel_id=1, source_target_pairs={{0,8},{1,9},{2,10},{3,11},{4,12},{5,13},{6,14},{7,15},{8,0},{9,1},... | collective-permute-start | bytes 196616 | tf_op jit(solution)/shard_map/ppermute | solution.py:264
  11.8 1.5 %collective-permute-start.3 = (bf16[1040,128]{1,0:T(8,128)(2,1)S(1)}, bf16[1040,128]{1,0:T(8,128)(2,1)S(1)}, u32[]{:S(2)}, u32[]{:S(2)}) collective-permute-start(bf16[1040,128]{1,0:T(8,128)(2,1)S(1)} %collective-permute-done.1.refs_0_), channel_id=1, source_target_pairs={{0,1},{1,0},{2,3},{3,2},{4,5},{5,4},{6,7},{7,6},{8,9},{9,8},{10,11... | collective-permute-start | bytes 798728 | tf_op jit(solution)/shard_map/ppermute | solution.py:264
  16.3 2.9 %collective-permute-start.6 = (f32[1024,128]{1,0:T(8,128)S(1)}, f32[1024,128]{1,0:T(8,128)S(1)}, u32[]{:S(2)}, u32[]{:S(2)}) collective-permute-start(f32[1024,128]{1,0:T(8,128)S(1)} %get-tuple-element.75), channel_id=1, source_target_pairs={{0,1},{1,0},{2,3},{3,2},{4,5},{5,4},{6,7},{7,6},{8,9},{9,8},{10,11... | collective-permute-start | bytes 1572872 | tf_op jit(solution)/shard_map/ppermute | solution.py:264
  19.2 6.5 %collective-permute-start.7 = (s16[144,256]{1,0:T(8,128)(2,1)S(1)}, s16[144,256]{1,0:T(8,128)(2,1)S(1)}, u32[]{:S(2)}, u32[]{:S(2)}) collective-permute-start(s16[144,256]{1,0:T(8,128)(2,1)S(1)} %get-tuple-element.81), channel_id=1, source_target_pairs={{0,12},{1,13},{2,14},{3,15},{4,8},{5,9},{6,10},{7,11},{8,4},{9,5},... | collective-permute-start | bytes 221192 | tf_op jit(solution)/shard_map/ppermute | solution.py:264
  22.3 8.5 %collective-permute-start.9 = (s16[1056,128]{1,0:T(8,128)(2,1)S(1)}, s16[1056,128]{1,0:T(8,128)(2,1)S(1)}, u32[]{:S(2)}, u32[]{:S(2)}) collective-permute-start(s16[1056,128]{1,0:T(8,128)(2,1)S(1)} %core_sum.1), channel_id=1, source_target_pairs={{0,2},{1,3},{2,0},{3,1},{4,6},{5,7},{6,4},{7,5},{8,10},{9,11},{10,... | collective-permute-start | bytes 811016 | tf_op jit(solution)/shard_map/ppermute | solution.py:264
  23.9 1.9 %collective-permute-start.8 = (s16[1040,128]{1,0:T(8,128)(2,1)S(1)}, s16[1040,128]{1,0:T(8,128)(2,1)S(1)}, u32[]{:S(2)}, u32[]{:S(2)}) collective-permute-start(s16[1040,128]{1,0:T(8,128)(2,1)S(1)} %get-tuple-element.83), channel_id=1, source_target_pairs={{0,1},{1,0},{2,3},{3,2},{4,5},{5,4},{6,7},{7,6},{8,9},{9,8},{10,11... | collective-permute-start | bytes 798728 | tf_op jit(solution)/shard_map/ppermute | solution.py:264
  23.9 7.9 %collective-permute-start.10 = (s16[144,256]{1,0:T(8,128)(2,1)S(1)}, s16[144,256]{1,0:T(8,128)(2,1)S(1)}, u32[]{:S(2)}, u32[]{:S(2)}) collective-permute-start(s16[144,256]{1,0:T(8,128)(2,1)S(1)} %get-tuple-element.89), channel_id=1, source_target_pairs={{0,8},{1,9},{2,10},{3,11},{4,12},{5,13},{6,14},{7,15},{8,0},{9,1},... | collective-permute-start | bytes 221192 | tf_op jit(solution)/shard_map/ppermute | solution.py:264
  23.9 7.9 %collective-permute-start.11 = (s16[144,256]{1,0:T(8,128)(2,1)S(1)}, s16[144,256]{1,0:T(8,128)(2,1)S(1)}, u32[]{:S(2)}, u32[]{:S(2)}) collective-permute-start(s16[144,256]{1,0:T(8,128)(2,1)S(1)} %get-tuple-element.90), channel_id=1, source_target_pairs={{0,4},{1,5},{2,6},{3,7},{4,0},{5,1},{6,2},{7,3},{8,12},{9,13},{10,... | collective-permute-start | bytes 221192 | tf_op jit(solution)/shard_map/ppermute | solution.py:264

commit v7 on v5

--- a/solution.py
+++ b/solution.py
@@ -11,6 +11,7 @@
 LOG2E = 1.4426950408889634
 LEVELS = 32000.0
 TAIL = 16
+HEAVY = 1 << 14
 VMEM = pl.BlockSpec(memory_space=pltpu.VMEM)
 HBM = pl.BlockSpec(memory_space=pltpu.HBM)
 F32 = jnp.float32
@@ -103,7 +104,7 @@
     return jnp.concatenate(row_blocks, axis=0)
 
 
-def grads(sets, vds, group, chunks, rows, local_v, scale, table, gqs, gvs, send, code_last, name):
+def grads(sets, vds, group, chunks, rows, local_v, scale, table, gqs, gvs, send, code_last, name, weight):
     k, m = len(sets), len(vds)
     dim = sets[0].shape[1]
     pad = sets[0].shape[0] - rows
@@ -206,7 +207,7 @@
             pltpu.VMEM((rows if code_last else 8, dim), F32),
         ],
         compiler_params=params(32),
-        cost_estimate=cost(k * rows * m * wide, 1 << 10),
+        cost_estimate=cost(weight * k * rows * m * wide, 1 << 10),
         name=name,
     )(*operands)
     return list(res[:k]), list(res[k : k + m]), res[-1] if fresh else table
@@ -269,28 +270,31 @@
     groups = [tuple(range(g * quarter, (g + 1) * quarter)) for g in range(4)]
     half = 2 * quarter
 
-    def add(sets, which, table, gqs, gvs, send, code_last, name):
+    def add(sets, which, table, gqs, gvs, send, name, code_last=False, weight=1):
         group = sum((groups[g] for g in which), ())
         return grads(
             sets, [vds[s] for s in group], group, chunks, rows, local_v, scale,
-            table, gqs, gvs, send, code_last, name,
+            table, gqs, gvs, send, code_last, name, weight,
         )
 
     qm_y = swap(qm, 2)
     qm_c = swap(qm, 1)
     vds = [vd] + [swap(vd, 4 * s) for s in range(1, chunks)]
     own = [qm, qm_c]
-    gq_o, gv0, table = add(own, [0], None, None, None, (), False, "own_0")
-    gq_o, gv1, _ = add(own, [1], table, gq_o, None, (), False, "own_1")
-    gq_y, gv01, table_y = add([qm_y], [0, 1], None, None, gv0 + gv1, (), False, "y_01")
-    qm_y, gq_y, gv01, vds[half:] = lax.optimization_barrier((qm_y, gq_y, gv01, vds[half:]))
+    near, far = tuple(range(1, half)), tuple(range(half, chunks))
+    gq_o, gv0, table = add(own, [0], None, None, None, (), "own_0")
+    gq_o, gv1, _ = add(own, [1], table, gq_o, None, (), "own_1")
+    qm_y, gv1 = lax.optimization_barrier((qm_y, gv1))
     qm_yc = swap(qm_y, 1)
-    gq_o, gv23, _ = add(own, [2, 3], table, gq_o, None, (), True, "own_23")
-    near, far = tuple(range(1, half)), tuple(range(half, chunks))
-    gq_yc, gvs, _ = add([qm_yc], [0, 1, 2, 3], None, None, gv01 + gv23, near, False, "yc")
+    gq_y, gv01, table_y = add([qm_y], [0, 1], None, None, gv0 + gv1, (), "y_01", weight=HEAVY)
+    gq_yc, gv01, table_yc = add([qm_yc], [0, 1], None, None, gv01, near, "yc_01")
+    gq_yc, gv01, late = lax.optimization_barrier((gq_yc, gv01, vds[half:][::-1]))
+    vds[half:] = late[::-1]
+    gq_yc, gv23, _ = add([qm_yc], [2, 3], table_yc, gq_yc, None, (), "yc_23")
     got_y = swap(gq_yc[0], 1)
-    gq_y, gv23, _ = add([qm_y], [2, 3], table_y, gq_y, gvs[half:], far, False, "y_23")
-    got_y, gv01, gv23 = lax.optimization_barrier((got_y, gvs[:half], gv23))
+    gq_y, gv23, _ = add([qm_y], [2, 3], table_y, gq_y, gv23, (), "y_23")
+    gq_o, gv23, _ = add(own, [2, 3], table, gq_o, gv23, far, "own_23", code_last=True)
+    got_y, gv01, gv23 = lax.optimization_barrier((got_y, gv01, gv23))
     gq_message = pl.pallas_call(
         core_sum_kernel,
         out_shape=jax.ShapeDtypeStruct((rows + 2 * TAIL, dim), I16),
@@ -304,7 +308,8 @@
     got_own = swap(gq_c, 1)
     term, *messages = gv01 + gv23
     got_message = swap(gq_message, 2)
-    got_terms = [swap(x, 4 * s) for s, x in reversed(list(enumerate(messages, 1)))]
+    order = sorted(range(1, chunks), key=lambda s: (s < half, s))
+    got_terms = [swap(messages[s - 1], 4 * s) for s in order]
     grad_q = pl.pallas_call(
         finish_q_kernel,
         out_shape=row_out,

time: 32.3 us -> 31.3 us (0.969)
  waiting for transfers between devices: 8.23 us -> 6.89 us
    ppermute x12, waiting for transfers between devices: 8.23 us -> 6.89 us  [swap(): return lax.ppermute(x, 'qry', [(i, i ^ bit) for i in range(n)])]
    pallas_call x6 -> x7, Pallas kernels: 7.48 us -> 7.6 us  [grads(): pl.pallas_call(kernel, out_shape=tuple(outs), in_specs=[VMEM] * len(opera...]
  transfers between devices with their start and end apart: 12 -> 12, of which waited for: 6 -> 7; matrix products, arithmetic and copies ran while one was open for 0% -> 0% of each run, Pallas kernels for 20% -> 24%
where the time goes in v7:
time: 31.3 us; the launch traced here: 31.1 us
  starting transfers between devices  13 us (42%)
  Pallas kernels  10.5 us (34%)
  waiting for transfers between devices  6.89 us (22%)
  between operations  0.73 us (2%)
    ppermute x12, starting transfers between devices, swap(): return lax.ppermute(x, 'qry', [(i, i ^ bit) for i in range(n)])  13 us
    pallas_call x7, Pallas kernels, grads(): pl.pallas_call(kernel, out_shape=tuple(outs), in_specs=[VMEM] * len(opera...  7.6 us
    ppermute x12, waiting for transfers between devices, swap(): return lax.ppermute(x, 'qry', [(i, i ^ bit) for i in range(n)])  6.89 us
    pallas_call x1, Pallas kernels, body(): pl.pallas_call(pack_kernel, out_shape=(jax.ShapeDtypeStruct((rows + pad,...  1.04 us
    pallas_call x1, Pallas kernels, body(): pl.pallas_call(finish_q_kernel, out_shape=row_out, in_specs=[VMEM] * 3, o...  0.94 us
    pallas_call x1, Pallas kernels, body(): pl.pallas_call(finish_v_kernel, out_shape=(vec_out, vec_out), in_specs=[V...  0.78 us
  transfers between devices with their start and end apart: 12, of which 7 were waited for; matrix products, arithmetic and copies ran while one was open for 0% of the time, Pallas kernels for 24%

profile of v7, /device:TPU:0, one launch (start us, length us, event | category | flops | bytes accessed | tf_op | source)
XLA Modules:
  0.0 31.1 jit_solution(9182893890515091745)
XLA Ops:
  0.6 1.0 %pack.1 = (bf16[1040,128]{1,0:T(8,128)(2,1)S(1)}, bf16[256,128]{1,0:T(8,128)(2,1)S(1)}) custom-call(bf16[1024,128]{1,0:T(8,128)(2,1)} %q_hbm.1, bf16[128,128]{1,0:T(8,128)(2,1)} %v_hbm.1, bf16[128,128]{1,0:T(8,128)(2,1)} %d_hbm.1, s32[4,8]{1,0:T(4,128)} %m_hbm.1), custom_call_target="tpu_custom_call" | custom-call | tf_op jit(solution)/shard_map/pack/pallas_call | solution.py:256
  1.7 0.5 %collective-permute-start = (bf16[1040,128]{1,0:T(8,128)(2,1)S(1)}, bf16[1040,128]{1,0:T(8,128)(2,1)S(1)}, u32[]{:S(2)}, u32[]{:S(2)}) collective-permute-start(bf16[1040,128]{1,0:T(8,128)(2,1)S(1)} %get-tuple-element.46.refs_0_), channel_id=1, source_target_pairs={{0,1},{1,0},{2,3},{3,2},{4,5},{5,4},{6,7},{7,6},{8,9},{9,8},{10,11... | collective-permute-start | bytes 798728 | tf_op jit(solution)/shard_map/ppermute | solution.py:254
  2.2 2.6 %collective-permute-start.1 = (bf16[1040,128]{1,0:T(8,128)(2,1)S(1)}, bf16[1040,128]{1,0:T(8,128)(2,1)S(1)}, u32[]{:S(2)}, u32[]{:S(2)}) collective-permute-start(bf16[1040,128]{1,0:T(8,128)(2,1)S(1)} %get-tuple-element.46.refs_0_), channel_id=1, source_target_pairs={{0,2},{1,3},{2,0},{3,1},{4,6},{5,7},{6,4},{7,5},{8,10},{9,11},{10,... | collective-permute-start | bytes 798728 | tf_op jit(solution)/shard_map/ppermute | solution.py:254
  4.8 1.6 %collective-permute-start.2 = (bf16[256,128]{1,0:T(8,128)(2,1)S(1)}, bf16[256,128]{1,0:T(8,128)(2,1)S(1)}, u32[]{:S(2)}, u32[]{:S(2)}) collective-permute-start(bf16[256,128]{1,0:T(8,128)(2,1)S(1)} %get-tuple-element.47.refs_2_.refs_1_), channel_id=1, source_target_pairs={{0,4},{1,5},{2,6},{3,7},{4,0},{5,1},{6,2},{7,3},{8,12},{9,13},{10,... | collective-permute-start | bytes 196616 | tf_op jit(solution)/shard_map/ppermute | solution.py:254
  6.4 2.6 %collective-permute-start.5 = (bf16[256,128]{1,0:T(8,128)(2,1)S(1)}, bf16[256,128]{1,0:T(8,128)(2,1)S(1)}, u32[]{:S(2)}, u32[]{:S(2)}) collective-permute-start(bf16[256,128]{1,0:T(8,128)(2,1)S(1)} %get-tuple-element.47.refs_2_.refs_1_), channel_id=1, source_target_pairs={{0,8},{1,9},{2,10},{3,11},{4,12},{5,13},{6,14},{7,15},{8,0},{9,1},... | collective-permute-start | bytes 196616 | tf_op jit(solution)/shard_map/ppermute | solution.py:254
  9.0 0.2 collective-permute-start.4
  9.2 0.0 collective-permute-done.refs_1_
  9.2 1.0 %own_0.1 = (f32[1024,128]{1,0:T(8,128)S(1)}, f32[1024,128]{1,0:T(8,128)S(1)}, f32[128,256]{1,0:T(8,128)S(1)}, f32[4,32,128]{2,1,0:T(8,128)S(1)}) custom-call(bf16[1040,128]{1,0:T(8,128)(2,1)S(1)} %get-tuple-element.46.refs_0_, bf16[1040,128]{1,0:T(8,128)(2,1)S(1)} %collective-permute-done.refs_1_, bf16[256,128]{1,0:T(8,128)(2,1)S(1)} %get-tuple-element.47.refs_2_.refs_1_), custom_call_target="tpu_custom_call" | custom-call | flops 524288 | bytes 1024 | tf_op jit(solution)/shard_map/own_0/pallas_call | solution.py:199
  10.2 0.0 collective-permute-done.2.refs_2_
  10.2 1.0 %own_1.1 = (f32[1024,128]{1,0:T(8,128)S(1)}, f32[1024,128]{1,0:T(8,128)S(1)}, f32[128,256]{1,0:T(8,128)S(1)}) custom-call(bf16[1040,128]{1,0:T(8,128)(2,1)S(1)} %get-tuple-element.46.refs_0_, bf16[1040,128]{1,0:T(8,128)(2,1)S(1)} %collective-permute-done.refs_1_, bf16[256,128]{1,0:T(8,128)(2,1)S(1)} %collective-permute-done.2.refs_2_, ...), custom_call_target="tpu_custom_call" | custom-call | flops 524288 | bytes 1024 | tf_op jit(solution)/shard_map/own_1/pallas_call | solution.py:199
  11.2 0.6 %collective-permute-done.1.refs_0_ = bf16[1040,128]{1,0:T(8,128)(2,1)S(1)} collective-permute-done((bf16[1040,128]{1,0:T(8,128)(2,1)S(1)}, bf16[1040,128]{1,0:T(8,128)(2,1)S(1)}, u32[]{:S(2)}, u32[]{:S(2)}) %collective-permute-start.1) | collective-permute-done | bytes 266272 | tf_op jit(solution)/shard_map/ppermute | solution.py:254
  11.8 0.0 collective-permute-start.3
  11.8 1.0 %y_01.1 = (f32[1024,128]{1,0:T(8,128)S(1)}, f32[128,256]{1,0:T(8,128)S(1)}, f32[128,256]{1,0:T(8,128)S(1)}, f32[4,16,128]{2,1,0:T(8,128)S(1)}) custom-call(bf16[1040,128]{1,0:T(8,128)(2,1)S(1)} %collective-permute-done.1.refs_0_, bf16[256,128]{1,0:T(8,128)(2,1)S(1)} %get-tuple-element.47.refs_2_.refs_1_, ...), custom_call_target="tpu_custom_call" | custom-call | flops 8589934592 | bytes 1024 | tf_op jit(solution)/shard_map/y_01/pallas_call | solution.py:199
  12.8 0.6 %collective-permute-done.3.refs_0_ = bf16[1040,128]{1,0:T(8,128)(2,1)S(1)} collective-permute-done((bf16[1040,128]{1,0:T(8,128)(2,1)S(1)}, bf16[1040,128]{1,0:T(8,128)(2,1)S(1)}, u32[]{:S(2)}, u32[]{:S(2)}) %collective-permute-start.3) | collective-permute-done | bytes 266272 | tf_op jit(solution)/shard_map/ppermute | solution.py:254
  13.3 1.0 %yc_01.1 = (f32[1024,128]{1,0:T(8,128)S(1)}, f32[128,256]{1,0:T(8,128)S(1)}, s16[144,256]{1,0:T(8,128)(2,1)S(1)}, f32[4,16,128]{2,1,0:T(8,128)S(1)}) custom-call(bf16[1040,128]{1,0:T(8,128)(2,1)S(1)} %collective-permute-done.3.refs_0_, bf16[256,128]{1,0:T(8,128)(2,1)S(1)} %get-tuple-element.47.refs_2_.refs_1_, ...), custom_call_target="tpu_custom_call" | custom-call | flops 524288 | bytes 1024 | tf_op jit(solution)/shard_map/yc_01/pallas_call | solution.py:199
  14.3 0.0 collective-permute-done.5.refs_1_.refs_2_
  14.3 0.8 %collective-permute-done.4.refs_2_.refs_3_ = bf16[256,128]{1,0:T(8,128)(2,1)S(1)} collective-permute-done((bf16[256,128]{1,0:T(8,128)(2,1)S(1)}, bf16[256,128]{1,0:T(8,128)(2,1)S(1)}, u32[]{:S(2)}, u32[]{:S(2)}) %collective-permute-start.4) | collective-permute-done | bytes 65568 | tf_op jit(solution)/shard_map/ppermute | solution.py:254
  15.1 1.0 %yc_23.1 = (f32[1024,128]{1,0:T(8,128)S(1)}, f32[128,256]{1,0:T(8,128)S(1)}, f32[128,256]{1,0:T(8,128)S(1)}) custom-call(bf16[1040,128]{1,0:T(8,128)(2,1)S(1)} %collective-permute-done.3.refs_0_, bf16[256,128]{1,0:T(8,128)(2,1)S(1)} %collective-permute-done.5.refs_1_.refs_2_, bf16[256,128]{1,0:T(8,128)(2,1)S(1)} %collective-permute-done.4.refs_2_.refs_3_, ...), custom_call_target="tpu_custom_call" | custom-call | flops 524288 | bytes 1024 | tf_op jit(solution)/shard_map/yc_23/pallas_call | solution.py:199
  16.1 0.1 collective-permute-start.7
  16.2 1.0 %y_23.1 = (f32[1024,128]{1,0:T(8,128)S(1)}, f32[128,256]{1,0:T(8,128)S(1)}, f32[128,256]{1,0:T(8,128)S(1)}) custom-call(bf16[1040,128]{1,0:T(8,128)(2,1)S(1)} %collective-permute-done.1.refs_0_, bf16[256,128]{1,0:T(8,128)(2,1)S(1)} %collective-permute-done.5.refs_1_.refs_2_, bf16[256,128]{1,0:T(8,128)(2,1)S(1)} %collective-permute-done.4.refs_2_.refs_3_, ...), custom_call_target="tpu_custom_call" | custom-call | flops 524288 | bytes 1024 | tf_op jit(solution)/shard_map/y_23/pallas_call | solution.py:199
  17.1 1.8 %own_23.1 = (f32[1024,128]{1,0:T(8,128)S(1)}, s16[1040,128]{1,0:T(8,128)(2,1)S(1)}, s16[144,256]{1,0:T(8,128)(2,1)S(1)}, s16[144,256]{1,0:T(8,128)(2,1)S(1)}) custom-call(bf16[1040,128]{1,0:T(8,128)(2,1)S(1)} %get-tuple-element.46.refs_0_, bf16[1040,128]{1,0:T(8,128)(2,1)S(1)} %collective-permute-done.refs_1_, ...), custom_call_target="tpu_custom_call" | custom-call | flops 1048576 | bytes 1024 | tf_op jit(solution)/shard_map/own_23/pallas_call | solution.py:199
  18.9 0.0 collective-permute-done.7.got_y_ref
  18.9 0.1 core_sum.1
  19.0 1.2 %collective-permute-start.8 = (s16[1056,128]{1,0:T(8,128)(2,1)S(1)}, s16[1056,128]{1,0:T(8,128)(2,1)S(1)}, u32[]{:S(2)}, u32[]{:S(2)}) collective-permute-start(s16[1056,128]{1,0:T(8,128)(2,1)S(1)} %core_sum.1), channel_id=1, source_target_pairs={{0,2},{1,3},{2,0},{3,1},{4,6},{5,7},{6,4},{7,5},{8,10},{9,11},{10,... | collective-permute-start | bytes 811016 | tf_op jit(solution)/shard_map/ppermute | solution.py:254
  20.2 0.1 collective-permute-start.6
  20.3 2.6 %collective-permute-start.9 = (s16[144,256]{1,0:T(8,128)(2,1)S(1)}, s16[144,256]{1,0:T(8,128)(2,1)S(1)}, u32[]{:S(2)}, u32[]{:S(2)}) collective-permute-start(s16[144,256]{1,0:T(8,128)(2,1)S(1)} %get-tuple-element.84), channel_id=1, source_target_pairs={{0,8},{1,9},{2,10},{3,11},{4,12},{5,13},{6,14},{7,15},{8,0},{9,1},... | collective-permute-start | bytes 221192 | tf_op jit(solution)/shard_map/ppermute | solution.py:254
  22.9 1.4 %collective-permute-start.10 = (s16[144,256]{1,0:T(8,128)(2,1)S(1)}, s16[144,256]{1,0:T(8,128)(2,1)S(1)}, u32[]{:S(2)}, u32[]{:S(2)}) collective-permute-start(s16[144,256]{1,0:T(8,128)(2,1)S(1)} %get-tuple-element.85), channel_id=1, source_target_pairs={{0,12},{1,13},{2,14},{3,15},{4,8},{5,9},{6,10},{7,11},{8,4},{9,5},... | collective-permute-start | bytes 221192 | tf_op jit(solution)/shard_map/ppermute | solution.py:254
  24.2 0.2 collective-permute-start.11
  24.5 0.0 collective-permute-done.6.got_own_ref
  24.5 3.5 %collective-permute-done.8.got_ref = s16[1056,128]{1,0:T(8,128)(2,1)S(1)} collective-permute-done((s16[1056,128]{1,0:T(8,128)(2,1)S(1)}, s16[1056,128]{1,0:T(8,128)(2,1)S(1)}, u32[]{:S(2)}, u32[]{:S(2)}) %collective-permute-start.8) | collective-permute-done | bytes 270368 | tf_op jit(solution)/shard_map/ppermute | solution.py:254
  28.0 0.9 %finish_q.1 = f32[1024,128]{1,0:T(8,128)} custom-call(f32[1024,128]{1,0:T(8,128)S(1)} %get-tuple-element.72.own_ref, s16[1040,128]{1,0:T(8,128)(2,1)S(1)} %collective-permute-done.6.got_own_ref, s16[1056,128]{1,0:T(8,128)(2,1)S(1)} %collective-permute-done.8.got_ref), custom_call_target="tpu_custom_call" | custom-call | tf_op jit(solution)/shard_map/finish_q/pallas_call | solution.py:313
  28.9 0.1 collective-permute-done.9.refs_0_
  29.1 0.7 %collective-permute-done.10.refs_1_ = s16[144,256]{1,0:T(8,128)(2,1)S(1)} collective-permute-done((s16[144,256]{1,0:T(8,128)(2,1)S(1)}, s16[144,256]{1,0:T(8,128)(2,1)S(1)}, u32[]{:S(2)}, u32[]{:S(2)}) %collective-permute-start.10) | collective-permute-done | bytes 73760 | tf_op jit(solution)/shard_map/ppermute | solution.py:254
  29.8 0.5 %collective-permute-done.11.refs_2_ = s16[144,256]{1,0:T(8,128)(2,1)S(1)} collective-permute-done((s16[144,256]{1,0:T(8,128)(2,1)S(1)}, s16[144,256]{1,0:T(8,128)(2,1)S(1)}, u32[]{:S(2)}, u32[]{:S(2)}) %collective-permute-start.11) | collective-permute-done | bytes 73760 | tf_op jit(solution)/shard_map/ppermute | solution.py:254
  30.3 0.8 %finish_v.1 = (f32[128,128]{1,0:T(8,128)}, f32[128,128]{1,0:T(8,128)}) custom-call(f32[128,256]{1,0:T(8,128)S(1)} %get-tuple-element.83.term_ref, s16[144,256]{1,0:T(8,128)(2,1)S(1)} %collective-permute-done.9.refs_0_, s16[144,256]{1,0:T(8,128)(2,1)S(1)} %collective-permute-done.10.refs_1_, s16[144,256]{1,0:T(8,128)(2,1)S(1)} %collective-permute-done.11.refs_2_), custom_call_target="tpu_custom_call" | custom-call | tf_op jit(solution)/shard_map/finish_v/pallas_call | solution.py:323
Async XLA Ops:
  1.7 7.5 %collective-permute-start = (bf16[1040,128]{1,0:T(8,128)(2,1)S(1)}, bf16[1040,128]{1,0:T(8,128)(2,1)S(1)}, u32[]{:S(2)}, u32[]{:S(2)}) collective-permute-start(bf16[1040,128]{1,0:T(8,128)(2,1)S(1)} %get-tuple-element.46.refs_0_), channel_id=1, source_target_pairs={{0,1},{1,0},{2,3},{3,2},{4,5},{5,4},{6,7},{7,6},{8,9},{9,8},{10,11... | collective-permute-start | bytes 798728 | tf_op jit(solution)/shard_map/ppermute | solution.py:254
  2.2 9.6 %collective-permute-start.1 = (bf16[1040,128]{1,0:T(8,128)(2,1)S(1)}, bf16[1040,128]{1,0:T(8,128)(2,1)S(1)}, u32[]{:S(2)}, u32[]{:S(2)}) collective-permute-start(bf16[1040,128]{1,0:T(8,128)(2,1)S(1)} %get-tuple-element.46.refs_0_), channel_id=1, source_target_pairs={{0,2},{1,3},{2,0},{3,1},{4,6},{5,7},{6,4},{7,5},{8,10},{9,11},{10,... | collective-permute-start | bytes 798728 | tf_op jit(solution)/shard_map/ppermute | solution.py:254
  4.8 5.4 %collective-permute-start.2 = (bf16[256,128]{1,0:T(8,128)(2,1)S(1)}, bf16[256,128]{1,0:T(8,128)(2,1)S(1)}, u32[]{:S(2)}, u32[]{:S(2)}) collective-permute-start(bf16[256,128]{1,0:T(8,128)(2,1)S(1)} %get-tuple-element.47.refs_2_.refs_1_), channel_id=1, source_target_pairs={{0,4},{1,5},{2,6},{3,7},{4,0},{5,1},{6,2},{7,3},{8,12},{9,13},{10,... | collective-permute-start | bytes 196616 | tf_op jit(solution)/shard_map/ppermute | solution.py:254
  6.4 8.0 %collective-permute-start.5 = (bf16[256,128]{1,0:T(8,128)(2,1)S(1)}, bf16[256,128]{1,0:T(8,128)(2,1)S(1)}, u32[]{:S(2)}, u32[]{:S(2)}) collective-permute-start(bf16[256,128]{1,0:T(8,128)(2,1)S(1)} %get-tuple-element.47.refs_2_.refs_1_), channel_id=1, source_target_pairs={{0,8},{1,9},{2,10},{3,11},{4,12},{5,13},{6,14},{7,15},{8,0},{9,1},... | collective-permute-start | bytes 196616 | tf_op jit(solution)/shard_map/ppermute | solution.py:254
  9.0 6.2 %collective-permute-start.4 = (bf16[256,128]{1,0:T(8,128)(2,1)S(1)}, bf16[256,128]{1,0:T(8,128)(2,1)S(1)}, u32[]{:S(2)}, u32[]{:S(2)}) collective-permute-start(bf16[256,128]{1,0:T(8,128)(2,1)S(1)} %get-tuple-element.47.refs_2_.refs_1_), channel_id=1, source_target_pairs={{0,12},{1,13},{2,14},{3,15},{4,8},{5,9},{6,10},{7,11},{8,4},{9,5},... | collective-permute-start | bytes 196616 | tf_op jit(solution)/shard_map/ppermute | solution.py:254
  11.8 1.5 %collective-permute-start.3 = (bf16[1040,128]{1,0:T(8,128)(2,1)S(1)}, bf16[1040,128]{1,0:T(8,128)(2,1)S(1)}, u32[]{:S(2)}, u32[]{:S(2)}) collective-permute-start(bf16[1040,128]{1,0:T(8,128)(2,1)S(1)} %collective-permute-done.1.refs_0_), channel_id=1, source_target_pairs={{0,1},{1,0},{2,3},{3,2},{4,5},{5,4},{6,7},{7,6},{8,9},{9,8},{10,11... | collective-permute-start | bytes 798728 | tf_op jit(solution)/shard_map/ppermute | solution.py:254
  16.1 2.8 %collective-permute-start.7 = (f32[1024,128]{1,0:T(8,128)S(1)}, f32[1024,128]{1,0:T(8,128)S(1)}, u32[]{:S(2)}, u32[]{:S(2)}) collective-permute-start(f32[1024,128]{1,0:T(8,128)S(1)} %get-tuple-element.75), channel_id=1, source_target_pairs={{0,1},{1,0},{2,3},{3,2},{4,5},{5,4},{6,7},{7,6},{8,9},{9,8},{10,11... | collective-permute-start | bytes 1572872 | tf_op jit(solution)/shard_map/ppermute | solution.py:254
  19.0 8.9 %collective-permute-start.8 = (s16[1056,128]{1,0:T(8,128)(2,1)S(1)}, s16[1056,128]{1,0:T(8,128)(2,1)S(1)}, u32[]{:S(2)}, u32[]{:S(2)}) collective-permute-start(s16[1056,128]{1,0:T(8,128)(2,1)S(1)} %core_sum.1), channel_id=1, source_target_pairs={{0,2},{1,3},{2,0},{3,1},{4,6},{5,7},{6,4},{7,5},{8,10},{9,11},{10,... | collective-permute-start | bytes 811016 | tf_op jit(solution)/shard_map/ppermute | solution.py:254
  20.2 4.3 %collective-permute-start.6 = (s16[1040,128]{1,0:T(8,128)(2,1)S(1)}, s16[1040,128]{1,0:T(8,128)(2,1)S(1)}, u32[]{:S(2)}, u32[]{:S(2)}) collective-permute-start(s16[1040,128]{1,0:T(8,128)(2,1)S(1)} %get-tuple-element.73), channel_id=1, source_target_pairs={{0,1},{1,0},{2,3},{3,2},{4,5},{5,4},{6,7},{7,6},{8,9},{9,8},{10,11... | collective-permute-start | bytes 798728 | tf_op jit(solution)/shard_map/ppermute | solution.py:254
  20.3 8.8 %collective-permute-start.9 = (s16[144,256]{1,0:T(8,128)(2,1)S(1)}, s16[144,256]{1,0:T(8,128)(2,1)S(1)}, u32[]{:S(2)}, u32[]{:S(2)}) collective-permute-start(s16[144,256]{1,0:T(8,128)(2,1)S(1)} %get-tuple-element.84), channel_id=1, source_target_pairs={{0,8},{1,9},{2,10},{3,11},{4,12},{5,13},{6,14},{7,15},{8,0},{9,1},... | collective-permute-start | bytes 221192 | tf_op jit(solution)/shard_map/ppermute | solution.py:254
  22.9 6.9 %collective-permute-start.10 = (s16[144,256]{1,0:T(8,128)(2,1)S(1)}, s16[144,256]{1,0:T(8,128)(2,1)S(1)}, u32[]{:S(2)}, u32[]{:S(2)}) collective-permute-start(s16[144,256]{1,0:T(8,128)(2,1)S(1)} %get-tuple-element.85), channel_id=1, source_target_pairs={{0,12},{1,13},{2,14},{3,15},{4,8},{5,9},{6,10},{7,11},{8,4},{9,5},... | collective-permute-start | bytes 221192 | tf_op jit(solution)/shard_map/ppermute | solution.py:254
  24.2 6.1 %collective-permute-start.11 = (s16[144,256]{1,0:T(8,128)(2,1)S(1)}, s16[144,256]{1,0:T(8,128)(2,1)S(1)}, u32[]{:S(2)}, u32[]{:S(2)}) collective-permute-start(s16[144,256]{1,0:T(8,128)(2,1)S(1)} %get-tuple-element.86), channel_id=1, source_target_pairs={{0,4},{1,5},{2,6},{3,7},{4,0},{5,1},{6,2},{7,3},{8,12},{9,13},{10,... | collective-permute-start | bytes 221192 | tf_op jit(solution)/shard_map/ppermute | solution.py:254

commit v8 on v7

--- a/solution.py
+++ b/solution.py
@@ -12,6 +12,7 @@
 LEVELS = 32000.0
 TAIL = 16
 HEAVY = 1 << 14
+MEDIUM = 1500
 VMEM = pl.BlockSpec(memory_space=pltpu.VMEM)
 HBM = pl.BlockSpec(memory_space=pltpu.HBM)
 F32 = jnp.float32
@@ -57,23 +58,23 @@
         out_ref[rows + TAIL :, :] = jnp.zeros(rest, I16)
 
 
-def pack_kernel(q_hbm, v_hbm, d_hbm, m_hbm, qm_ref, vd_ref, m_ref, sems):
-    rows = q_hbm.shape[0]
+def pack_kernel(q_hbm, v_hbm, d_hbm, m_hbm, q_ref, vd_ref, flags_ref, m_ref, sems):
     local_v = v_hbm.shape[0]
     copies = [
         pltpu.make_async_copy(m_hbm, m_ref, sems.at[0]),
         pltpu.make_async_copy(v_hbm, vd_ref.at[pl.ds(0, local_v)], sems.at[1]),
         pltpu.make_async_copy(d_hbm, vd_ref.at[pl.ds(local_v, local_v)], sems.at[2]),
-        pltpu.make_async_copy(q_hbm, qm_ref.at[pl.ds(0, rows)], sems.at[3]),
+        pltpu.make_async_copy(q_hbm, q_ref, sems.at[3]),
     ]
     for copy in copies:
         copy.start()
     copies[0].wait()
     blocks, cols = m_ref.shape
-    pad, lanes = qm_ref.shape[0] - rows, qm_ref.shape[1]
+    pad, lanes = flags_ref.shape
     flags = jnp.concatenate([m_ref[...].astype(F32), jnp.zeros((blocks, lanes - cols), F32)], axis=1)
-    flags = jnp.concatenate([flags, jnp.zeros((pad - blocks, lanes), F32)], axis=0)
-    qm_ref[rows:, :] = flags.astype(BF16)
+    if pad > blocks:
+        flags = jnp.concatenate([flags, jnp.zeros((pad - blocks, lanes), F32)], axis=0)
+    flags_ref[...] = flags.astype(BF16)
     for copy in copies[1:]:
         copy.wait()
 
@@ -104,14 +105,14 @@
     return jnp.concatenate(row_blocks, axis=0)
 
 
-def grads(sets, vds, group, chunks, rows, local_v, scale, table, gqs, gvs, send, code_last, name, weight):
+def grads(sets, vds, group, chunks, rows, local_v, scale, table, row0, flags, gqs, gvs, send, code_last, name, weight):
     k, m = len(sets), len(vds)
     dim = sets[0].shape[1]
-    pad = sets[0].shape[0] - rows
+    fresh = table is None
+    pad = (sum(x.shape[0] for x in flags) if fresh else table.shape[1]) // 2
     wide = 2 * local_v
     part = min(m, 4)
     height = 2 * BLK if rows % (2 * BLK) == 0 else BLK
-    fresh = table is None
 
     def kernel(*refs):
         qm_refs, refs = refs[:k], refs[k:]
@@ -119,6 +120,8 @@
         gq_ins, gv_ins = None, None
         if not fresh:
             table_ref, refs = refs[0], refs[1:]
+        else:
+            flags_refs, refs = refs[: len(flags)], refs[len(flags) :]
         if gqs is not None:
             gq_ins, refs = refs[:k], refs[k:]
         if gvs is not None:
@@ -127,10 +130,13 @@
         gv_outs, refs = refs[:m], refs[m:]
         if fresh:
             table_ref, refs = refs[0], refs[1:]
-            for t in range(k):
-                table = live_table(qm_refs[t][rows:, :], chunks, local_v, scale)
-                for s in range(chunks):
-                    table_ref[s, t * pad : (t + 1) * pad, :] = table[:, s * 128 : (s + 1) * 128]
+            both = jnp.concatenate([ref[...] for ref in flags_refs], axis=0)
+            if len(flags) == 2:
+                refs[0][...] = both
+                refs = refs[1:]
+            lanes = live_table(both, chunks, local_v, scale)
+            for s in range(chunks):
+                table_ref[s, :, :] = lanes[:, s * 128 : (s + 1) * 128]
         gv_ref, w_ref, last_ref = refs
         for s in range(m):
             w_ref[s * wide : (s + 1) * wide, :] = vd_refs[s][...]
@@ -142,7 +148,7 @@
         def tile(t, r0, first):
             def live(b, c):
                 s = group[first + c]
-                return table_ref[s, pl.ds(t * pad + r0 // BLK + b, 1), :]
+                return table_ref[s, pl.ds(row0 + t * pad + r0 // BLK + b, 1), :]
 
             w = w_ref[first * wide : (first + part) * wide, :]
             weights = tile_weights(qm_refs[t][pl.ds(r0, height), :], w, live, part, local_v)
@@ -185,7 +191,8 @@
             else:
                 gv_outs[s][...] = term
 
-    operands = [*sets, *vds, *([] if fresh else [table]), *(gqs or []), *(gvs or [])]
+    given = flags if fresh else [table]
+    operands = [*sets, *vds, *given, *(gqs or []), *(gvs or [])]
     outs = [jax.ShapeDtypeStruct((rows, dim), F32)] * k + [
         jax.ShapeDtypeStruct((dim + TAIL, wide), I16)
         if s in send
@@ -195,7 +202,9 @@
     if code_last:
         outs[k - 1] = jax.ShapeDtypeStruct((rows + TAIL, dim), I16)
     if fresh:
-        outs.append(jax.ShapeDtypeStruct((chunks, k * pad, 128), F32))
+        outs.append(jax.ShapeDtypeStruct((chunks, 2 * pad, 128), F32))
+        if len(flags) == 2:
+            outs.append(jax.ShapeDtypeStruct((2 * pad, dim), BF16))
     res = pl.pallas_call(
         kernel,
         out_shape=tuple(outs),
@@ -210,7 +219,7 @@
         cost_estimate=cost(weight * k * rows * m * wide, 1 << 10),
         name=name,
     )(*operands)
-    return list(res[:k]), list(res[k : k + m]), res[-1] if fresh else table
+    return list(res[:k]), list(res[k : k + m]), res[k + m :]
 
 
 def core_sum_kernel(y_ref, got_y_ref, y_out, sum_ref):
@@ -253,14 +262,13 @@
     def swap(x, bit):
         return lax.ppermute(x, "qry", [(i, i ^ bit) for i in range(n)])
 
-    qm, vd = pl.pallas_call(
+    q_y = swap(queries, 2)
+    q_c = swap(queries, 1)
+    q, vd, flags = pl.pallas_call(
         pack_kernel,
-        out_shape=(
-            jax.ShapeDtypeStruct((rows + pad, dim), BF16),
-            jax.ShapeDtypeStruct((wide, dim), BF16),
-        ),
+        out_shape=tuple(jax.ShapeDtypeStruct((r, dim), BF16) for r in (rows, wide, pad)),
         in_specs=[HBM] * 4,
-        out_specs=(VMEM, VMEM),
+        out_specs=(VMEM,) * 3,
         scratch_shapes=[pltpu.VMEM(mask.shape, mask.dtype), pltpu.SemaphoreType.DMA((4,))],
         compiler_params=params(8),
         name="pack",
@@ -270,30 +278,31 @@
     groups = [tuple(range(g * quarter, (g + 1) * quarter)) for g in range(4)]
     half = 2 * quarter
 
-    def add(sets, which, table, gqs, gvs, send, name, code_last=False, weight=1):
+    def add(sets, which, gqs, gvs, name, table=None, row0=0, flags=None, send=(), code_last=False,
+            weight=1):
         group = sum((groups[g] for g in which), ())
         return grads(
             sets, [vds[s] for s in group], group, chunks, rows, local_v, scale,
-            table, gqs, gvs, send, code_last, name, weight,
+            table, row0, flags, gqs, gvs, send, code_last, name, weight,
         )
 
-    qm_y = swap(qm, 2)
-    qm_c = swap(qm, 1)
+    flags_c = swap(flags, 1)
     vds = [vd] + [swap(vd, 4 * s) for s in range(1, chunks)]
-    own = [qm, qm_c]
+    own = [q, q_c]
     near, far = tuple(range(1, half)), tuple(range(half, chunks))
-    gq_o, gv0, table = add(own, [0], None, None, None, (), "own_0")
-    gq_o, gv1, _ = add(own, [1], table, gq_o, None, (), "own_1")
-    qm_y, gv1 = lax.optimization_barrier((qm_y, gv1))
-    qm_yc = swap(qm_y, 1)
-    gq_y, gv01, table_y = add([qm_y], [0, 1], None, None, gv0 + gv1, (), "y_01", weight=HEAVY)
-    gq_yc, gv01, table_yc = add([qm_yc], [0, 1], None, None, gv01, near, "yc_01")
+    gq_o, gv0, (table, flags) = add(own, [0], None, None, "own_0", flags=[flags, flags_c])
+    flags = swap(flags, 2)
+    gq_o, gv1, _ = add(own, [1], gq_o, None, "own_1", table, weight=MEDIUM)
+    q_y, gv1 = lax.optimization_barrier((q_y, gv1))
+    q_yc = swap(q_y, 1)
+    gq_y, gv01, (table_y,) = add([q_y], [0, 1], None, gv0 + gv1, "y_01", flags=[flags], weight=HEAVY)
+    gq_yc, gv01, _ = add([q_yc], [0, 1], None, gv01, "yc_01", table_y, pad, send=near)
     gq_yc, gv01, late = lax.optimization_barrier((gq_yc, gv01, vds[half:][::-1]))
     vds[half:] = late[::-1]
-    gq_yc, gv23, _ = add([qm_yc], [2, 3], table_yc, gq_yc, None, (), "yc_23")
+    gq_yc, gv23, _ = add([q_yc], [2, 3], gq_yc, None, "yc_23", table_y, pad)
     got_y = swap(gq_yc[0], 1)
-    gq_y, gv23, _ = add([qm_y], [2, 3], table_y, gq_y, gv23, (), "y_23")
-    gq_o, gv23, _ = add(own, [2, 3], table, gq_o, gv23, far, "own_23", code_last=True)
+    gq_y, gv23, _ = add([q_y], [2, 3], gq_y, gv23, "y_23", table_y)
+    gq_o, gv23, _ = add(own, [2, 3], gq_o, gv23, "own_23", table, send=far, code_last=True)
     got_y, gv01, gv23 = lax.optimization_barrier((got_y, gv01, gv23))
     gq_message = pl.pallas_call(
         core_sum_kernel,

time: 31.3 us -> 32.2 us (1.029)
  waiting for transfers between devices: 6.89 us -> 7.5 us
  starting transfers between devices: 13 us -> 13.4 us
    ppermute x12 -> x14, waiting for transfers between devices: 6.89 us -> 7.5 us  [swap(): return lax.ppermute(x, 'qry', [(i, i ^ bit) for i in range(n)])]
    ppermute x12 -> x14, starting transfers between devices: 13 us -> 13.4 us  [swap(): return lax.ppermute(x, 'qry', [(i, i ^ bit) for i in range(n)])]
  transfers between devices with their start and end apart: 12 -> 14, of which waited for: 7 -> 3; matrix products, arithmetic and copies ran while one was open for 0% -> 0% of each run, Pallas kernels for 24% -> 27%
where the time goes in v8:
time: 32.2 us; the launch traced here: 32.1 us
  starting transfers between devices  13.4 us (42%)
  Pallas kernels  10.5 us (33%)
  waiting for transfers between devices  7.5 us (23%)
  between operations  0.75 us (2%)
    ppermute x14, starting transfers between devices, swap(): return lax.ppermute(x, 'qry', [(i, i ^ bit) for i in range(n)])  13.4 us
    pallas_call x7, Pallas kernels, grads(): pl.pallas_call(kernel, out_shape=tuple(outs), in_specs=[VMEM] * len(opera...  7.54 us
    ppermute x14, waiting for transfers between devices, swap(): return lax.ppermute(x, 'qry', [(i, i ^ bit) for i in range(n)])  7.5 us
    pallas_call x1, Pallas kernels, body(): pl.pallas_call(pack_kernel, out_shape=tuple((jax.ShapeDtypeStruct((r, dim...  1.06 us
    pallas_call x1, Pallas kernels, body(): pl.pallas_call(finish_q_kernel, out_shape=row_out, in_specs=[VMEM] * 3, o...  0.94 us
    pallas_call x1, Pallas kernels, body(): pl.pallas_call(finish_v_kernel, out_shape=(vec_out, vec_out), in_specs=[V...  0.78 us
  transfers between devices with their start and end apart: 14, of which 3 were waited for; matrix products, arithmetic and copies ran while one was open for 0% of the time, Pallas kernels for 27%

profile of v8, /device:TPU:0, one launch (start us, length us, event | category | flops | bytes accessed | tf_op | source)
XLA Modules:
  0.0 32.1 jit_solution(649554864503891489)
XLA Ops:
  0.6 0.5 %collective-permute-start = (bf16[1024,128]{1,0:T(8,128)(2,1)}, bf16[1024,128]{1,0:T(8,128)(2,1)S(1)}, u32[]{:S(2)}, u32[]{:S(2)}) collective-permute-start(bf16[1024,128]{1,0:T(8,128)(2,1)} %q_hbm.1), channel_id=1, source_target_pairs={{0,1},{1,0},{2,3},{3,2},{4,5},{5,4},{6,7},{7,6},{8,9},{9,8},{10,11... | collective-permute-start | bytes 786440 | tf_op jit(solution)/shard_map/ppermute | solution.py:263
  1.1 2.6 %collective-permute-start.1 = (bf16[1024,128]{1,0:T(8,128)(2,1)}, bf16[1024,128]{1,0:T(8,128)(2,1)S(1)}, u32[]{:S(2)}, u32[]{:S(2)}) collective-permute-start(bf16[1024,128]{1,0:T(8,128)(2,1)} %q_hbm.1), channel_id=1, source_target_pairs={{0,2},{1,3},{2,0},{3,1},{4,6},{5,7},{6,4},{7,5},{8,10},{9,11},{10,... | collective-permute-start | bytes 786440 | tf_op jit(solution)/shard_map/ppermute | solution.py:263
  3.7 1.1 %pack.1 = (bf16[1024,128]{1,0:T(8,128)(2,1)S(1)}, bf16[256,128]{1,0:T(8,128)(2,1)S(1)}, bf16[16,128]{1,0:T(8,128)(2,1)S(1)}) custom-call(bf16[1024,128]{1,0:T(8,128)(2,1)} %q_hbm.1, bf16[128,128]{1,0:T(8,128)(2,1)} %v_hbm.1, bf16[128,128]{1,0:T(8,128)(2,1)} %d_hbm.1, s32[4,8]{1,0:T(4,128)} %m_hbm.1), custom_call_target="tpu_custom_call" | custom-call | tf_op jit(solution)/shard_map/pack/pallas_call | solution.py:267
  4.8 1.6 %collective-permute-start.2 = (bf16[256,128]{1,0:T(8,128)(2,1)S(1)}, bf16[256,128]{1,0:T(8,128)(2,1)S(1)}, u32[]{:S(2)}, u32[]{:S(2)}) collective-permute-start(bf16[256,128]{1,0:T(8,128)(2,1)S(1)} %get-tuple-element.48.refs_2_.refs_1_), channel_id=1, source_target_pairs={{0,4},{1,5},{2,6},{3,7},{4,0},{5,1},{6,2},{7,3},{8,12},{9,13},{10,... | collective-permute-start | bytes 196616 | tf_op jit(solution)/shard_map/ppermute | solution.py:263
  6.5 0.0 collective-permute-start.3
  6.5 2.6 %collective-permute-start.7 = (bf16[256,128]{1,0:T(8,128)(2,1)S(1)}, bf16[256,128]{1,0:T(8,128)(2,1)S(1)}, u32[]{:S(2)}, u32[]{:S(2)}) collective-permute-start(bf16[256,128]{1,0:T(8,128)(2,1)S(1)} %get-tuple-element.48.refs_2_.refs_1_), channel_id=1, source_target_pairs={{0,8},{1,9},{2,10},{3,11},{4,12},{5,13},{6,14},{7,15},{8,0},{9,1},... | collective-permute-start | bytes 196616 | tf_op jit(solution)/shard_map/ppermute | solution.py:263
  9.0 0.0 collective-permute-done.3.refs_4_
  9.1 1.0 %collective-permute-start.6 = (bf16[256,128]{1,0:T(8,128)(2,1)S(1)}, bf16[256,128]{1,0:T(8,128)(2,1)S(1)}, u32[]{:S(2)}, u32[]{:S(2)}) collective-permute-start(bf16[256,128]{1,0:T(8,128)(2,1)S(1)} %get-tuple-element.48.refs_2_.refs_1_), channel_id=1, source_target_pairs={{0,12},{1,13},{2,14},{3,15},{4,8},{5,9},{6,10},{7,11},{8,4},{9,5},... | collective-permute-start | bytes 196616 | tf_op jit(solution)/shard_map/ppermute | solution.py:263
  10.1 0.0 collective-permute-done.refs_1_
  10.1 1.0 %own_0.1 = (f32[1024,128]{1,0:T(8,128)S(1)}, f32[1024,128]{1,0:T(8,128)S(1)}, f32[128,256]{1,0:T(8,128)S(1)}, f32[4,32,128]{2,1,0:T(8,128)S(1)}, bf16[32,128]{1,0:T(8,128)(2,1)S(1)}) custom-call(bf16[1024,128]{1,0:T(8,128)(2,1)S(1)} %get-tuple-element.47.refs_0_, bf16[1024,128]{1,0:T(8,128)(2,1)S(1)} %collective-permute-done.refs_1_, ...), custom_call_target="tpu_custom_call" | custom-call | flops 524288 | bytes 1024 | tf_op jit(solution)/shard_map/own_0/pallas_call | solution.py:208
  11.1 0.6 %collective-permute-start.5 = (bf16[32,128]{1,0:T(8,128)(2,1)S(1)}, bf16[32,128]{1,0:T(8,128)(2,1)S(1)}, u32[]{:S(2)}, u32[]{:S(2)}) collective-permute-start(bf16[32,128]{1,0:T(8,128)(2,1)S(1)} %get-tuple-element.55), channel_id=1, source_target_pairs={{0,2},{1,3},{2,0},{3,1},{4,6},{5,7},{6,4},{7,5},{8,10},{9,11},{10,... | collective-permute-start | bytes 24584 | tf_op jit(solution)/shard_map/ppermute | solution.py:263
  11.7 0.0 collective-permute-done.2.refs_2_
  11.7 1.0 %own_1.1 = (f32[1024,128]{1,0:T(8,128)S(1)}, f32[1024,128]{1,0:T(8,128)S(1)}, f32[128,256]{1,0:T(8,128)S(1)}) custom-call(bf16[1024,128]{1,0:T(8,128)(2,1)S(1)} %get-tuple-element.47.refs_0_, bf16[1024,128]{1,0:T(8,128)(2,1)S(1)} %collective-permute-done.refs_1_, bf16[256,128]{1,0:T(8,128)(2,1)S(1)} %collective-permute-done.2.refs_2_, ...), custom_call_target="tpu_custom_call" | custom-call | flops 786432000 | bytes 1024 | tf_op jit(solution)/shard_map/own_1/pallas_call | solution.py:208
  12.7 0.0 collective-permute-done.1.refs_0_
  12.7 0.1 collective-permute-start.4
  12.7 2.1 %collective-permute-done.5.refs_3_ = bf16[32,128]{1,0:T(8,128)(2,1)S(1)} collective-permute-done((bf16[32,128]{1,0:T(8,128)(2,1)S(1)}, bf16[32,128]{1,0:T(8,128)(2,1)S(1)}, u32[]{:S(2)}, u32[]{:S(2)}) %collective-permute-start.5) | collective-permute-done | bytes 8224 | tf_op jit(solution)/shard_map/ppermute | solution.py:263
  14.8 1.0 %y_01.1 = (f32[1024,128]{1,0:T(8,128)S(1)}, f32[128,256]{1,0:T(8,128)S(1)}, f32[128,256]{1,0:T(8,128)S(1)}, f32[4,32,128]{2,1,0:T(8,128)S(1)}) custom-call(bf16[1024,128]{1,0:T(8,128)(2,1)S(1)} %collective-permute-done.1.refs_0_, bf16[256,128]{1,0:T(8,128)(2,1)S(1)} %get-tuple-element.48.refs_2_.refs_1_, ...), custom_call_target="tpu_custom_call" | custom-call | flops 8589934592 | bytes 1024 | tf_op jit(solution)/shard_map/y_01/pallas_call | solution.py:208
  15.8 0.0 collective-permute-done.4.refs_0_
  15.8 1.0 %yc_01.1 = (f32[1024,128]{1,0:T(8,128)S(1)}, f32[128,256]{1,0:T(8,128)S(1)}, s16[144,256]{1,0:T(8,128)(2,1)S(1)}) custom-call(bf16[1024,128]{1,0:T(8,128)(2,1)S(1)} %collective-permute-done.4.refs_0_, bf16[256,128]{1,0:T(8,128)(2,1)S(1)} %get-tuple-element.48.refs_2_.refs_1_, bf16[256,128]{1,0:T(8,128)(2,1)S(1)} %collective-permute-done.2.refs_2_, ...), custom_call_target="tpu_custom_call" | custom-call | flops 524288 | bytes 1024 | tf_op jit(solution)/shard_map/yc_01/pallas_call | solution.py:208
  16.8 0.0 collective-permute-done.7.refs_1_.refs_2_
  16.8 0.0 collective-permute-done.6.refs_2_.refs_3_
  16.8 0.9 %yc_23.1 = (f32[1024,128]{1,0:T(8,128)S(1)}, f32[128,256]{1,0:T(8,128)S(1)}, f32[128,256]{1,0:T(8,128)S(1)}) custom-call(bf16[1024,128]{1,0:T(8,128)(2,1)S(1)} %collective-permute-done.4.refs_0_, bf16[256,128]{1,0:T(8,128)(2,1)S(1)} %collective-permute-done.7.refs_1_.refs_2_, bf16[256,128]{1,0:T(8,128)(2,1)S(1)} %collective-permute-done.6.refs_2_.refs_3_, ...), custom_call_target="tpu_custom_call" | custom-call | flops 524288 | bytes 1024 | tf_op jit(solution)/shard_map/yc_23/pallas_call | solution.py:208
  17.7 0.1 collective-permute-start.9
  17.8 1.0 %y_23.1 = (f32[1024,128]{1,0:T(8,128)S(1)}, f32[128,256]{1,0:T(8,128)S(1)}, f32[128,256]{1,0:T(8,128)S(1)}) custom-call(bf16[1024,128]{1,0:T(8,128)(2,1)S(1)} %collective-permute-done.1.refs_0_, bf16[256,128]{1,0:T(8,128)(2,1)S(1)} %collective-permute-done.7.refs_1_.refs_2_, bf16[256,128]{1,0:T(8,128)(2,1)S(1)} %collective-permute-done.6.refs_2_.refs_3_, ...), custom_call_target="tpu_custom_call" | custom-call | flops 524288 | bytes 1024 | tf_op jit(solution)/shard_map/y_23/pallas_call | solution.py:208
  18.8 1.8 %own_23.1 = (f32[1024,128]{1,0:T(8,128)S(1)}, s16[1040,128]{1,0:T(8,128)(2,1)S(1)}, s16[144,256]{1,0:T(8,128)(2,1)S(1)}, s16[144,256]{1,0:T(8,128)(2,1)S(1)}) custom-call(bf16[1024,128]{1,0:T(8,128)(2,1)S(1)} %get-tuple-element.47.refs_0_, bf16[1024,128]{1,0:T(8,128)(2,1)S(1)} %collective-permute-done.refs_1_, ...), custom_call_target="tpu_custom_call" | custom-call | flops 1048576 | bytes 1024 | tf_op jit(solution)/shard_map/own_23/pallas_call | solution.py:208
  20.5 0.0 collective-permute-done.9.got_y_ref
  20.5 0.1 core_sum.1
  20.7 0.6 %collective-permute-start.10 = (s16[1056,128]{1,0:T(8,128)(2,1)S(1)}, s16[1056,128]{1,0:T(8,128)(2,1)S(1)}, u32[]{:S(2)}, u32[]{:S(2)}) collective-permute-start(s16[1056,128]{1,0:T(8,128)(2,1)S(1)} %core_sum.1), channel_id=1, source_target_pairs={{0,2},{1,3},{2,0},{3,1},{4,6},{5,7},{6,4},{7,5},{8,10},{9,11},{10,... | collective-permute-start | bytes 811016 | tf_op jit(solution)/shard_map/ppermute | solution.py:263
  21.2 0.2 collective-permute-start.8
  21.5 0.9 %collective-permute-start.11 = (s16[144,256]{1,0:T(8,128)(2,1)S(1)}, s16[144,256]{1,0:T(8,128)(2,1)S(1)}, u32[]{:S(2)}, u32[]{:S(2)}) collective-permute-start(s16[144,256]{1,0:T(8,128)(2,1)S(1)} %get-tuple-element.86), channel_id=1, source_target_pairs={{0,8},{1,9},{2,10},{3,11},{4,12},{5,13},{6,14},{7,15},{8,0},{9,1},... | collective-permute-start | bytes 221192 | tf_op jit(solution)/shard_map/ppermute | solution.py:263
  22.3 2.2 %collective-permute-start.12 = (s16[144,256]{1,0:T(8,128)(2,1)S(1)}, s16[144,256]{1,0:T(8,128)(2,1)S(1)}, u32[]{:S(2)}, u32[]{:S(2)}) collective-permute-start(s16[144,256]{1,0:T(8,128)(2,1)S(1)} %get-tuple-element.87), channel_id=1, source_target_pairs={{0,12},{1,13},{2,14},{3,15},{4,8},{5,9},{6,10},{7,11},{8,4},{9,5},... | collective-permute-start | bytes 221192 | tf_op jit(solution)/shard_map/ppermute | solution.py:263
  24.5 0.4 %collective-permute-start.13 = (s16[144,256]{1,0:T(8,128)(2,1)S(1)}, s16[144,256]{1,0:T(8,128)(2,1)S(1)}, u32[]{:S(2)}, u32[]{:S(2)}) collective-permute-start(s16[144,256]{1,0:T(8,128)(2,1)S(1)} %get-tuple-element.88), channel_id=1, source_target_pairs={{0,4},{1,5},{2,6},{3,7},{4,0},{5,1},{6,2},{7,3},{8,12},{9,13},{10,... | collective-permute-start | bytes 221192 | tf_op jit(solution)/shard_map/ppermute | solution.py:263
  24.9 0.0 collective-permute-done.8.got_own_ref
  24.9 4.7 %collective-permute-done.10.got_ref = s16[1056,128]{1,0:T(8,128)(2,1)S(1)} collective-permute-done((s16[1056,128]{1,0:T(8,128)(2,1)S(1)}, s16[1056,128]{1,0:T(8,128)(2,1)S(1)}, u32[]{:S(2)}, u32[]{:S(2)}) %collective-permute-start.10) | collective-permute-done | bytes 270368 | tf_op jit(solution)/shard_map/ppermute | solution.py:263
  29.6 0.9 %finish_q.1 = f32[1024,128]{1,0:T(8,128)} custom-call(f32[1024,128]{1,0:T(8,128)S(1)} %get-tuple-element.74.own_ref, s16[1040,128]{1,0:T(8,128)(2,1)S(1)} %collective-permute-done.8.got_own_ref, s16[1056,128]{1,0:T(8,128)(2,1)S(1)} %collective-permute-done.10.got_ref), custom_call_target="tpu_custom_call" | custom-call | tf_op jit(solution)/shard_map/finish_q/pallas_call | solution.py:322
  30.6 0.0 collective-permute-done.11.refs_0_
  30.6 0.0 collective-permute-done.12.refs_1_
  30.6 0.7 %collective-permute-done.13.refs_2_ = s16[144,256]{1,0:T(8,128)(2,1)S(1)} collective-permute-done((s16[144,256]{1,0:T(8,128)(2,1)S(1)}, s16[144,256]{1,0:T(8,128)(2,1)S(1)}, u32[]{:S(2)}, u32[]{:S(2)}) %collective-permute-start.13) | collective-permute-done | bytes 73760 | tf_op jit(solution)/shard_map/ppermute | solution.py:263
  31.3 0.8 %finish_v.1 = (f32[128,128]{1,0:T(8,128)}, f32[128,128]{1,0:T(8,128)}) custom-call(f32[128,256]{1,0:T(8,128)S(1)} %get-tuple-element.85.term_ref, s16[144,256]{1,0:T(8,128)(2,1)S(1)} %collective-permute-done.11.refs_0_, s16[144,256]{1,0:T(8,128)(2,1)S(1)} %collective-permute-done.12.refs_1_, s16[144,256]{1,0:T(8,128)(2,1)S(1)} %collective-permute-done.13.refs_2_), custom_call_target="tpu_custom_call" | custom-call | tf_op jit(solution)/shard_map/finish_v/pallas_call | solution.py:332
Async XLA Ops:
  0.6 9.5 %collective-permute-start = (bf16[1024,128]{1,0:T(8,128)(2,1)}, bf16[1024,128]{1,0:T(8,128)(2,1)S(1)}, u32[]{:S(2)}, u32[]{:S(2)}) collective-permute-start(bf16[1024,128]{1,0:T(8,128)(2,1)} %q_hbm.1), channel_id=1, source_target_pairs={{0,1},{1,0},{2,3},{3,2},{4,5},{5,4},{6,7},{7,6},{8,9},{9,8},{10,11... | collective-permute-start | bytes 786440 | tf_op jit(solution)/shard_map/ppermute | solution.py:263
  1.1 11.5 %collective-permute-start.1 = (bf16[1024,128]{1,0:T(8,128)(2,1)}, bf16[1024,128]{1,0:T(8,128)(2,1)S(1)}, u32[]{:S(2)}, u32[]{:S(2)}) collective-permute-start(bf16[1024,128]{1,0:T(8,128)(2,1)} %q_hbm.1), channel_id=1, source_target_pairs={{0,2},{1,3},{2,0},{3,1},{4,6},{5,7},{6,4},{7,5},{8,10},{9,11},{10,... | collective-permute-start | bytes 786440 | tf_op jit(solution)/shard_map/ppermute | solution.py:263
  4.8 6.9 %collective-permute-start.2 = (bf16[256,128]{1,0:T(8,128)(2,1)S(1)}, bf16[256,128]{1,0:T(8,128)(2,1)S(1)}, u32[]{:S(2)}, u32[]{:S(2)}) collective-permute-start(bf16[256,128]{1,0:T(8,128)(2,1)S(1)} %get-tuple-element.48.refs_2_.refs_1_), channel_id=1, source_target_pairs={{0,4},{1,5},{2,6},{3,7},{4,0},{5,1},{6,2},{7,3},{8,12},{9,13},{10,... | collective-permute-start | bytes 196616 | tf_op jit(solution)/shard_map/ppermute | solution.py:263
  6.5 2.6 %collective-permute-start.3 = (bf16[16,128]{1,0:T(8,128)(2,1)S(1)}, bf16[16,128]{1,0:T(8,128)(2,1)S(1)}, u32[]{:S(2)}, u32[]{:S(2)}) collective-permute-start(bf16[16,128]{1,0:T(8,128)(2,1)S(1)} %get-tuple-element.49.refs_3_), channel_id=1, source_target_pairs={{0,1},{1,0},{2,3},{3,2},{4,5},{5,4},{6,7},{7,6},{8,9},{9,8},{10,11... | collective-permute-start | bytes 12296 | tf_op jit(solution)/shard_map/ppermute | solution.py:263
  6.5 10.3 %collective-permute-start.7 = (bf16[256,128]{1,0:T(8,128)(2,1)S(1)}, bf16[256,128]{1,0:T(8,128)(2,1)S(1)}, u32[]{:S(2)}, u32[]{:S(2)}) collective-permute-start(bf16[256,128]{1,0:T(8,128)(2,1)S(1)} %get-tuple-element.48.refs_2_.refs_1_), channel_id=1, source_target_pairs={{0,8},{1,9},{2,10},{3,11},{4,12},{5,13},{6,14},{7,15},{8,0},{9,1},... | collective-permute-start | bytes 196616 | tf_op jit(solution)/shard_map/ppermute | solution.py:263
  9.1 7.7 %collective-permute-start.6 = (bf16[256,128]{1,0:T(8,128)(2,1)S(1)}, bf16[256,128]{1,0:T(8,128)(2,1)S(1)}, u32[]{:S(2)}, u32[]{:S(2)}) collective-permute-start(bf16[256,128]{1,0:T(8,128)(2,1)S(1)} %get-tuple-element.48.refs_2_.refs_1_), channel_id=1, source_target_pairs={{0,12},{1,13},{2,14},{3,15},{4,8},{5,9},{6,10},{7,11},{8,4},{9,5},... | collective-permute-start | bytes 196616 | tf_op jit(solution)/shard_map/ppermute | solution.py:263
  11.1 3.7 %collective-permute-start.5 = (bf16[32,128]{1,0:T(8,128)(2,1)S(1)}, bf16[32,128]{1,0:T(8,128)(2,1)S(1)}, u32[]{:S(2)}, u32[]{:S(2)}) collective-permute-start(bf16[32,128]{1,0:T(8,128)(2,1)S(1)} %get-tuple-element.55), channel_id=1, source_target_pairs={{0,2},{1,3},{2,0},{3,1},{4,6},{5,7},{6,4},{7,5},{8,10},{9,11},{10,... | collective-permute-start | bytes 24584 | tf_op jit(solution)/shard_map/ppermute | solution.py:263
  12.7 3.1 %collective-permute-start.4 = (bf16[1024,128]{1,0:T(8,128)(2,1)S(1)}, bf16[1024,128]{1,0:T(8,128)(2,1)S(1)}, u32[]{:S(2)}, u32[]{:S(2)}) collective-permute-start(bf16[1024,128]{1,0:T(8,128)(2,1)S(1)} %collective-permute-done.1.refs_0_), channel_id=1, source_target_pairs={{0,1},{1,0},{2,3},{3,2},{4,5},{5,4},{6,7},{7,6},{8,9},{9,8},{10,11... | collective-permute-start | bytes 786440 | tf_op jit(solution)/shard_map/ppermute | solution.py:263
  17.7 2.8 %collective-permute-start.9 = (f32[1024,128]{1,0:T(8,128)S(1)}, f32[1024,128]{1,0:T(8,128)S(1)}, u32[]{:S(2)}, u32[]{:S(2)}) collective-permute-start(f32[1024,128]{1,0:T(8,128)S(1)} %get-tuple-element.77), channel_id=1, source_target_pairs={{0,1},{1,0},{2,3},{3,2},{4,5},{5,4},{6,7},{7,6},{8,9},{9,8},{10,11... | collective-permute-start | bytes 1572872 | tf_op jit(solution)/shard_map/ppermute | solution.py:263
  20.7 8.9 %collective-permute-start.10 = (s16[1056,128]{1,0:T(8,128)(2,1)S(1)}, s16[1056,128]{1,0:T(8,128)(2,1)S(1)}, u32[]{:S(2)}, u32[]{:S(2)}) collective-permute-start(s16[1056,128]{1,0:T(8,128)(2,1)S(1)} %core_sum.1), channel_id=1, source_target_pairs={{0,2},{1,3},{2,0},{3,1},{4,6},{5,7},{6,4},{7,5},{8,10},{9,11},{10,... | collective-permute-start | bytes 811016 | tf_op jit(solution)/shard_map/ppermute | solution.py:263
  21.2 3.7 %collective-permute-start.8 = (s16[1040,128]{1,0:T(8,128)(2,1)S(1)}, s16[1040,128]{1,0:T(8,128)(2,1)S(1)}, u32[]{:S(2)}, u32[]{:S(2)}) collective-permute-start(s16[1040,128]{1,0:T(8,128)(2,1)S(1)} %get-tuple-element.75), channel_id=1, source_target_pairs={{0,1},{1,0},{2,3},{3,2},{4,5},{5,4},{6,7},{7,6},{8,9},{9,8},{10,11... | collective-permute-start | bytes 798728 | tf_op jit(solution)/shard_map/ppermute | solution.py:263
  21.5 9.1 %collective-permute-start.11 = (s16[144,256]{1,0:T(8,128)(2,1)S(1)}, s16[144,256]{1,0:T(8,128)(2,1)S(1)}, u32[]{:S(2)}, u32[]{:S(2)}) collective-permute-start(s16[144,256]{1,0:T(8,128)(2,1)S(1)} %get-tuple-element.86), channel_id=1, source_target_pairs={{0,8},{1,9},{2,10},{3,11},{4,12},{5,13},{6,14},{7,15},{8,0},{9,1},... | collective-permute-start | bytes 221192 | tf_op jit(solution)/shard_map/ppermute | solution.py:263
  22.3 8.2 %collective-permute-start.12 = (s16[144,256]{1,0:T(8,128)(2,1)S(1)}, s16[144,256]{1,0:T(8,128)(2,1)S(1)}, u32[]{:S(2)}, u32[]{:S(2)}) collective-permute-start(s16[144,256]{1,0:T(8,128)(2,1)S(1)} %get-tuple-element.87), channel_id=1, source_target_pairs={{0,12},{1,13},{2,14},{3,15},{4,8},{5,9},{6,10},{7,11},{8,4},{9,5},... | collective-permute-start | bytes 221192 | tf_op jit(solution)/shard_map/ppermute | solution.py:263
  24.5 6.8 %collective-permute-start.13 = (s16[144,256]{1,0:T(8,128)(2,1)S(1)}, s16[144,256]{1,0:T(8,128)(2,1)S(1)}, u32[]{:S(2)}, u32[]{:S(2)}) collective-permute-start(s16[144,256]{1,0:T(8,128)(2,1)S(1)} %get-tuple-element.88), channel_id=1, source_target_pairs={{0,4},{1,5},{2,6},{3,7},{4,0},{5,1},{6,2},{7,3},{8,12},{9,13},{10,... | collective-permute-start | bytes 221192 | tf_op jit(solution)/shard_map/ppermute | solution.py:263

commit v9 on v7

--- a/solution.py
+++ b/solution.py
@@ -57,14 +57,15 @@
         out_ref[rows + TAIL :, :] = jnp.zeros(rest, I16)
 
 
-def pack_kernel(q_hbm, v_hbm, d_hbm, m_hbm, qm_ref, vd_ref, m_ref, sems):
+def pack_kernel(q_hbm, v_hbm, d_hbm, m_hbm, qm_ref, far_ref, vd_ref, m_ref, sems):
     rows = q_hbm.shape[0]
     local_v = v_hbm.shape[0]
     copies = [
         pltpu.make_async_copy(m_hbm, m_ref, sems.at[0]),
         pltpu.make_async_copy(v_hbm, vd_ref.at[pl.ds(0, local_v)], sems.at[1]),
         pltpu.make_async_copy(d_hbm, vd_ref.at[pl.ds(local_v, local_v)], sems.at[2]),
-        pltpu.make_async_copy(q_hbm, qm_ref.at[pl.ds(0, rows)], sems.at[3]),
+        pltpu.make_async_copy(q_hbm, far_ref.at[pl.ds(0, rows)], sems.at[3]),
+        pltpu.make_async_copy(q_hbm, qm_ref.at[pl.ds(0, rows)], sems.at[4]),
     ]
     for copy in copies:
         copy.start()
@@ -74,6 +75,8 @@
     flags = jnp.concatenate([m_ref[...].astype(F32), jnp.zeros((blocks, lanes - cols), F32)], axis=1)
     flags = jnp.concatenate([flags, jnp.zeros((pad - blocks, lanes), F32)], axis=0)
     qm_ref[rows:, :] = flags.astype(BF16)
+    far_ref[rows : rows + pad, :] = flags.astype(BF16)
+    far_ref[rows + pad :, :] = flags.astype(BF16)
     for copy in copies[1:]:
         copy.wait()
 
@@ -107,7 +110,7 @@
 def grads(sets, vds, group, chunks, rows, local_v, scale, table, gqs, gvs, send, code_last, name, weight):
     k, m = len(sets), len(vds)
     dim = sets[0].shape[1]
-    pad = sets[0].shape[0] - rows
+    pad = -(-(rows // BLK) // 16) * 16
     wide = 2 * local_v
     part = min(m, 4)
     height = 2 * BLK if rows % (2 * BLK) == 0 else BLK
@@ -128,7 +131,7 @@
         if fresh:
             table_ref, refs = refs[0], refs[1:]
             for t in range(k):
-                table = live_table(qm_refs[t][rows:, :], chunks, local_v, scale)
+                table = live_table(qm_refs[t][rows : rows + pad, :], chunks, local_v, scale)
                 for s in range(chunks):
                     table_ref[s, t * pad : (t + 1) * pad, :] = table[:, s * 128 : (s + 1) * 128]
         gv_ref, w_ref, last_ref = refs
@@ -253,15 +256,16 @@
     def swap(x, bit):
         return lax.ppermute(x, "qry", [(i, i ^ bit) for i in range(n)])
 
-    qm, vd = pl.pallas_call(
+    qm, qm_far, vd = pl.pallas_call(
         pack_kernel,
         out_shape=(
             jax.ShapeDtypeStruct((rows + pad, dim), BF16),
+            jax.ShapeDtypeStruct((rows + 2 * pad, dim), BF16),
             jax.ShapeDtypeStruct((wide, dim), BF16),
         ),
         in_specs=[HBM] * 4,
-        out_specs=(VMEM, VMEM),
-        scratch_shapes=[pltpu.VMEM(mask.shape, mask.dtype), pltpu.SemaphoreType.DMA((4,))],
+        out_specs=(VMEM,) * 3,
+        scratch_shapes=[pltpu.VMEM(mask.shape, mask.dtype), pltpu.SemaphoreType.DMA((5,))],
         compiler_params=params(8),
         name="pack",
     )(*[pltpu.with_memory_space_constraint(x, pltpu.HBM) for x in (queries, vectors, decoded, mask)])
@@ -277,13 +281,13 @@
             table, gqs, gvs, send, code_last, name, weight,
         )
 
-    qm_y = swap(qm, 2)
+    qm_y = swap(qm_far, 2)
     qm_c = swap(qm, 1)
     vds = [vd] + [swap(vd, 4 * s) for s in range(1, chunks)]
     own = [qm, qm_c]
     near, far = tuple(range(1, half)), tuple(range(half, chunks))
-    gq_o, gv0, table = add(own, [0], None, None, None, (), "own_0")
-    gq_o, gv1, _ = add(own, [1], table, gq_o, None, (), "own_1")
+    gq_o, gv0, table = add(own, [0], None, None, None, (), "own_0", weight=0)
+    gq_o, gv1, _ = add(own, [1], table, gq_o, None, (), "own_1", weight=0)
     qm_y, gv1 = lax.optimization_barrier((qm_y, gv1))
     qm_yc = swap(qm_y, 1)
     gq_y, gv01, table_y = add([qm_y], [0, 1], None, None, gv0 + gv1, (), "y_01", weight=HEAVY)

time: 31.3 us -> 30.8 us (0.984)
  starting transfers between devices: 13 us -> 12.4 us
    ppermute x12, starting transfers between devices: 13 us -> 12.4 us  [swap(): return lax.ppermute(x, 'qry', [(i, i ^ bit) for i in range(n)])]
  transfers between devices with their start and end apart: 12 -> 12, of which waited for: 7 -> 6; matrix products, arithmetic and copies ran while one was open for 0% -> 0% of each run, Pallas kernels for 24% -> 25%
where the time goes in v9:
time: 30.8 us; the launch traced here: 30.6 us
  starting transfers between devices  12.4 us (40%)
  Pallas kernels  10.6 us (34%)
  waiting for transfers between devices  6.85 us (22%)
  between operations  0.73 us (2%)
    ppermute x12, starting transfers between devices, swap(): return lax.ppermute(x, 'qry', [(i, i ^ bit) for i in range(n)])  12.4 us
    pallas_call x7, Pallas kernels, grads(): pl.pallas_call(kernel, out_shape=tuple(outs), in_specs=[VMEM] * len(opera...  7.6 us
    ppermute x12, waiting for transfers between devices, swap(): return lax.ppermute(x, 'qry', [(i, i ^ bit) for i in range(n)])  6.85 us
    pallas_call x1, Pallas kernels, body(): pl.pallas_call(pack_kernel, out_shape=(jax.ShapeDtypeStruct((rows + pad,...  1.13 us
    pallas_call x1, Pallas kernels, body(): pl.pallas_call(finish_q_kernel, out_shape=row_out, in_specs=[VMEM] * 3, o...  0.94 us
    pallas_call x1, Pallas kernels, body(): pl.pallas_call(finish_v_kernel, out_shape=(vec_out, vec_out), in_specs=[V...  0.78 us
  transfers between devices with their start and end apart: 12, of which 6 were waited for; matrix products, arithmetic and copies ran while one was open for 0% of the time, Pallas kernels for 25%

profile of v9, /device:TPU:0, one launch (start us, length us, event | category | flops | bytes accessed | tf_op | source)
XLA Modules:
  0.0 30.6 jit_solution(8340117486658049365)
XLA Ops:
  0.6 1.1 %pack.1 = (bf16[1040,128]{1,0:T(8,128)(2,1)S(1)}, bf16[1056,128]{1,0:T(8,128)(2,1)S(1)}, bf16[256,128]{1,0:T(8,128)(2,1)S(1)}) custom-call(bf16[1024,128]{1,0:T(8,128)(2,1)} %q_hbm.1, bf16[128,128]{1,0:T(8,128)(2,1)} %v_hbm.1, bf16[128,128]{1,0:T(8,128)(2,1)} %d_hbm.1, s32[4,8]{1,0:T(4,128)} %m_hbm.1), custom_call_target="tpu_custom_call" | custom-call | tf_op jit(solution)/shard_map/pack/pallas_call | solution.py:259
  1.8 3.0 %collective-permute-start.1 = (bf16[1056,128]{1,0:T(8,128)(2,1)S(1)}, bf16[1056,128]{1,0:T(8,128)(2,1)S(1)}, u32[]{:S(2)}, u32[]{:S(2)}) collective-permute-start(bf16[1056,128]{1,0:T(8,128)(2,1)S(1)} %get-tuple-element.48), channel_id=1, source_target_pairs={{0,2},{1,3},{2,0},{3,1},{4,6},{5,7},{6,4},{7,5},{8,10},{9,11},{10,... | collective-permute-start | bytes 811016 | tf_op jit(solution)/shard_map/ppermute | solution.py:257
  4.8 0.0 collective-permute-start
  4.8 1.6 %collective-permute-start.2 = (bf16[256,128]{1,0:T(8,128)(2,1)S(1)}, bf16[256,128]{1,0:T(8,128)(2,1)S(1)}, u32[]{:S(2)}, u32[]{:S(2)}) collective-permute-start(bf16[256,128]{1,0:T(8,128)(2,1)S(1)} %get-tuple-element.49.refs_2_.refs_1_), channel_id=1, source_target_pairs={{0,4},{1,5},{2,6},{3,7},{4,0},{5,1},{6,2},{7,3},{8,12},{9,13},{10,... | collective-permute-start | bytes 196616 | tf_op jit(solution)/shard_map/ppermute | solution.py:257
  6.4 2.6 %collective-permute-start.5 = (bf16[256,128]{1,0:T(8,128)(2,1)S(1)}, bf16[256,128]{1,0:T(8,128)(2,1)S(1)}, u32[]{:S(2)}, u32[]{:S(2)}) collective-permute-start(bf16[256,128]{1,0:T(8,128)(2,1)S(1)} %get-tuple-element.49.refs_2_.refs_1_), channel_id=1, source_target_pairs={{0,8},{1,9},{2,10},{3,11},{4,12},{5,13},{6,14},{7,15},{8,0},{9,1},... | collective-permute-start | bytes 196616 | tf_op jit(solution)/shard_map/ppermute | solution.py:257
  9.0 0.2 collective-permute-start.4
  9.2 0.0 collective-permute-done.refs_1_
  9.2 1.0 %own_0.1 = (f32[1024,128]{1,0:T(8,128)S(1)}, f32[1024,128]{1,0:T(8,128)S(1)}, f32[128,256]{1,0:T(8,128)S(1)}, f32[4,32,128]{2,1,0:T(8,128)S(1)}) custom-call(bf16[1040,128]{1,0:T(8,128)(2,1)S(1)} %get-tuple-element.47.refs_0_, bf16[1040,128]{1,0:T(8,128)(2,1)S(1)} %collective-permute-done.refs_1_, bf16[256,128]{1,0:T(8,128)(2,1)S(1)} %get-tuple-element.49.refs_2_.refs_1_), custom_call_target="tpu_custom_call" | custom-call | bytes 1024 | tf_op jit(solution)/shard_map/own_0/pallas_call | solution.py:202
  10.2 0.0 collective-permute-done.2.refs_2_
  10.2 1.0 %own_1.1 = (f32[1024,128]{1,0:T(8,128)S(1)}, f32[1024,128]{1,0:T(8,128)S(1)}, f32[128,256]{1,0:T(8,128)S(1)}) custom-call(bf16[1040,128]{1,0:T(8,128)(2,1)S(1)} %get-tuple-element.47.refs_0_, bf16[1040,128]{1,0:T(8,128)(2,1)S(1)} %collective-permute-done.refs_1_, bf16[256,128]{1,0:T(8,128)(2,1)S(1)} %collective-permute-done.2.refs_2_, ...), custom_call_target="tpu_custom_call" | custom-call | bytes 1024 | tf_op jit(solution)/shard_map/own_1/pallas_call | solution.py:202
  11.2 0.1 collective-permute-done.1.refs_0_
  11.3 0.0 collective-permute-start.3
  11.3 1.0 %y_01.1 = (f32[1024,128]{1,0:T(8,128)S(1)}, f32[128,256]{1,0:T(8,128)S(1)}, f32[128,256]{1,0:T(8,128)S(1)}, f32[4,16,128]{2,1,0:T(8,128)S(1)}) custom-call(bf16[1056,128]{1,0:T(8,128)(2,1)S(1)} %collective-permute-done.1.refs_0_, bf16[256,128]{1,0:T(8,128)(2,1)S(1)} %get-tuple-element.49.refs_2_.refs_1_, ...), custom_call_target="tpu_custom_call" | custom-call | flops 8589934592 | bytes 1024 | tf_op jit(solution)/shard_map/y_01/pallas_call | solution.py:202
  12.3 0.6 %collective-permute-done.3.refs_0_ = bf16[1056,128]{1,0:T(8,128)(2,1)S(1)} collective-permute-done((bf16[1056,128]{1,0:T(8,128)(2,1)S(1)}, bf16[1056,128]{1,0:T(8,128)(2,1)S(1)}, u32[]{:S(2)}, u32[]{:S(2)}) %collective-permute-start.3) | collective-permute-done | bytes 270368 | tf_op jit(solution)/shard_map/ppermute | solution.py:257
  12.8 1.0 %yc_01.1 = (f32[1024,128]{1,0:T(8,128)S(1)}, f32[128,256]{1,0:T(8,128)S(1)}, s16[144,256]{1,0:T(8,128)(2,1)S(1)}, f32[4,16,128]{2,1,0:T(8,128)S(1)}) custom-call(bf16[1056,128]{1,0:T(8,128)(2,1)S(1)} %collective-permute-done.3.refs_0_, bf16[256,128]{1,0:T(8,128)(2,1)S(1)} %get-tuple-element.49.refs_2_.refs_1_, ...), custom_call_target="tpu_custom_call" | custom-call | flops 524288 | bytes 1024 | tf_op jit(solution)/shard_map/yc_01/pallas_call | solution.py:202
  13.8 0.0 collective-permute-done.5.refs_1_.refs_2_
  13.8 1.2 %collective-permute-done.4.refs_2_.refs_3_ = bf16[256,128]{1,0:T(8,128)(2,1)S(1)} collective-permute-done((bf16[256,128]{1,0:T(8,128)(2,1)S(1)}, bf16[256,128]{1,0:T(8,128)(2,1)S(1)}, u32[]{:S(2)}, u32[]{:S(2)}) %collective-permute-start.4) | collective-permute-done | bytes 65568 | tf_op jit(solution)/shard_map/ppermute | solution.py:257
  15.1 1.0 %yc_23.1 = (f32[1024,128]{1,0:T(8,128)S(1)}, f32[128,256]{1,0:T(8,128)S(1)}, f32[128,256]{1,0:T(8,128)S(1)}) custom-call(bf16[1056,128]{1,0:T(8,128)(2,1)S(1)} %collective-permute-done.3.refs_0_, bf16[256,128]{1,0:T(8,128)(2,1)S(1)} %collective-permute-done.5.refs_1_.refs_2_, bf16[256,128]{1,0:T(8,128)(2,1)S(1)} %collective-permute-done.4.refs_2_.refs_3_, ...), custom_call_target="tpu_custom_call" | custom-call | flops 524288 | bytes 1024 | tf_op jit(solution)/shard_map/yc_23/pallas_call | solution.py:202
  16.0 0.1 collective-permute-start.7
  16.1 0.9 %y_23.1 = (f32[1024,128]{1,0:T(8,128)S(1)}, f32[128,256]{1,0:T(8,128)S(1)}, f32[128,256]{1,0:T(8,128)S(1)}) custom-call(bf16[1056,128]{1,0:T(8,128)(2,1)S(1)} %collective-permute-done.1.refs_0_, bf16[256,128]{1,0:T(8,128)(2,1)S(1)} %collective-permute-done.5.refs_1_.refs_2_, bf16[256,128]{1,0:T(8,128)(2,1)S(1)} %collective-permute-done.4.refs_2_.refs_3_, ...), custom_call_target="tpu_custom_call" | custom-call | flops 524288 | bytes 1024 | tf_op jit(solution)/shard_map/y_23/pallas_call | solution.py:202
  17.1 1.8 %own_23.1 = (f32[1024,128]{1,0:T(8,128)S(1)}, s16[1040,128]{1,0:T(8,128)(2,1)S(1)}, s16[144,256]{1,0:T(8,128)(2,1)S(1)}, s16[144,256]{1,0:T(8,128)(2,1)S(1)}) custom-call(bf16[1040,128]{1,0:T(8,128)(2,1)S(1)} %get-tuple-element.47.refs_0_, bf16[1040,128]{1,0:T(8,128)(2,1)S(1)} %collective-permute-done.refs_1_, ...), custom_call_target="tpu_custom_call" | custom-call | flops 1048576 | bytes 1024 | tf_op jit(solution)/shard_map/own_23/pallas_call | solution.py:202
  18.8 0.0 collective-permute-done.7.got_y_ref
  18.9 0.1 core_sum.1
  19.0 0.7 %collective-permute-start.8 = (s16[1056,128]{1,0:T(8,128)(2,1)S(1)}, s16[1056,128]{1,0:T(8,128)(2,1)S(1)}, u32[]{:S(2)}, u32[]{:S(2)}) collective-permute-start(s16[1056,128]{1,0:T(8,128)(2,1)S(1)} %core_sum.1), channel_id=1, source_target_pairs={{0,2},{1,3},{2,0},{3,1},{4,6},{5,7},{6,4},{7,5},{8,10},{9,11},{10,... | collective-permute-start | bytes 811016 | tf_op jit(solution)/shard_map/ppermute | solution.py:257
  19.7 0.1 collective-permute-start.6
  19.8 2.6 %collective-permute-start.9 = (s16[144,256]{1,0:T(8,128)(2,1)S(1)}, s16[144,256]{1,0:T(8,128)(2,1)S(1)}, u32[]{:S(2)}, u32[]{:S(2)}) collective-permute-start(s16[144,256]{1,0:T(8,128)(2,1)S(1)} %get-tuple-element.86), channel_id=1, source_target_pairs={{0,8},{1,9},{2,10},{3,11},{4,12},{5,13},{6,14},{7,15},{8,0},{9,1},... | collective-permute-start | bytes 221192 | tf_op jit(solution)/shard_map/ppermute | solution.py:257
  22.4 1.3 %collective-permute-start.10 = (s16[144,256]{1,0:T(8,128)(2,1)S(1)}, s16[144,256]{1,0:T(8,128)(2,1)S(1)}, u32[]{:S(2)}, u32[]{:S(2)}) collective-permute-start(s16[144,256]{1,0:T(8,128)(2,1)S(1)} %get-tuple-element.87), channel_id=1, source_target_pairs={{0,12},{1,13},{2,14},{3,15},{4,8},{5,9},{6,10},{7,11},{8,4},{9,5},... | collective-permute-start | bytes 221192 | tf_op jit(solution)/shard_map/ppermute | solution.py:257
  23.7 0.2 collective-permute-start.11
  23.9 0.0 collective-permute-done.6.got_own_ref
  23.9 4.0 %collective-permute-done.8.got_ref = s16[1056,128]{1,0:T(8,128)(2,1)S(1)} collective-permute-done((s16[1056,128]{1,0:T(8,128)(2,1)S(1)}, s16[1056,128]{1,0:T(8,128)(2,1)S(1)}, u32[]{:S(2)}, u32[]{:S(2)}) %collective-permute-start.8) | collective-permute-done | bytes 270368 | tf_op jit(solution)/shard_map/ppermute | solution.py:257
  27.9 0.9 %finish_q.1 = f32[1024,128]{1,0:T(8,128)} custom-call(f32[1024,128]{1,0:T(8,128)S(1)} %get-tuple-element.74.own_ref, s16[1040,128]{1,0:T(8,128)(2,1)S(1)} %collective-permute-done.6.got_own_ref, s16[1056,128]{1,0:T(8,128)(2,1)S(1)} %collective-permute-done.8.got_ref), custom_call_target="tpu_custom_call" | custom-call | tf_op jit(solution)/shard_map/finish_q/pallas_call | solution.py:317
  28.9 0.0 collective-permute-done.9.refs_0_
  28.9 0.4 %collective-permute-done.10.refs_1_ = s16[144,256]{1,0:T(8,128)(2,1)S(1)} collective-permute-done((s16[144,256]{1,0:T(8,128)(2,1)S(1)}, s16[144,256]{1,0:T(8,128)(2,1)S(1)}, u32[]{:S(2)}, u32[]{:S(2)}) %collective-permute-start.10) | collective-permute-done | bytes 73760 | tf_op jit(solution)/shard_map/ppermute | solution.py:257
  29.3 0.5 %collective-permute-done.11.refs_2_ = s16[144,256]{1,0:T(8,128)(2,1)S(1)} collective-permute-done((s16[144,256]{1,0:T(8,128)(2,1)S(1)}, s16[144,256]{1,0:T(8,128)(2,1)S(1)}, u32[]{:S(2)}, u32[]{:S(2)}) %collective-permute-start.11) | collective-permute-done | bytes 73760 | tf_op jit(solution)/shard_map/ppermute | solution.py:257
  29.8 0.8 %finish_v.1 = (f32[128,128]{1,0:T(8,128)}, f32[128,128]{1,0:T(8,128)}) custom-call(f32[128,256]{1,0:T(8,128)S(1)} %get-tuple-element.85.term_ref, s16[144,256]{1,0:T(8,128)(2,1)S(1)} %collective-permute-done.9.refs_0_, s16[144,256]{1,0:T(8,128)(2,1)S(1)} %collective-permute-done.10.refs_1_, s16[144,256]{1,0:T(8,128)(2,1)S(1)} %collective-permute-done.11.refs_2_), custom_call_target="tpu_custom_call" | custom-call | tf_op jit(solution)/shard_map/finish_v/pallas_call | solution.py:327
Async XLA Ops:
  1.8 9.5 %collective-permute-start.1 = (bf16[1056,128]{1,0:T(8,128)(2,1)S(1)}, bf16[1056,128]{1,0:T(8,128)(2,1)S(1)}, u32[]{:S(2)}, u32[]{:S(2)}) collective-permute-start(bf16[1056,128]{1,0:T(8,128)(2,1)S(1)} %get-tuple-element.48), channel_id=1, source_target_pairs={{0,2},{1,3},{2,0},{3,1},{4,6},{5,7},{6,4},{7,5},{8,10},{9,11},{10,... | collective-permute-start | bytes 811016 | tf_op jit(solution)/shard_map/ppermute | solution.py:257
  4.8 4.4 %collective-permute-start = (bf16[1040,128]{1,0:T(8,128)(2,1)S(1)}, bf16[1040,128]{1,0:T(8,128)(2,1)S(1)}, u32[]{:S(2)}, u32[]{:S(2)}) collective-permute-start(bf16[1040,128]{1,0:T(8,128)(2,1)S(1)} %get-tuple-element.47.refs_0_), channel_id=1, source_target_pairs={{0,1},{1,0},{2,3},{3,2},{4,5},{5,4},{6,7},{7,6},{8,9},{9,8},{10,11... | collective-permute-start | bytes 798728 | tf_op jit(solution)/shard_map/ppermute | solution.py:257
  4.8 5.4 %collective-permute-start.2 = (bf16[256,128]{1,0:T(8,128)(2,1)S(1)}, bf16[256,128]{1,0:T(8,128)(2,1)S(1)}, u32[]{:S(2)}, u32[]{:S(2)}) collective-permute-start(bf16[256,128]{1,0:T(8,128)(2,1)S(1)} %get-tuple-element.49.refs_2_.refs_1_), channel_id=1, source_target_pairs={{0,4},{1,5},{2,6},{3,7},{4,0},{5,1},{6,2},{7,3},{8,12},{9,13},{10,... | collective-permute-start | bytes 196616 | tf_op jit(solution)/shard_map/ppermute | solution.py:257
  6.4 7.5 %collective-permute-start.5 = (bf16[256,128]{1,0:T(8,128)(2,1)S(1)}, bf16[256,128]{1,0:T(8,128)(2,1)S(1)}, u32[]{:S(2)}, u32[]{:S(2)}) collective-permute-start(bf16[256,128]{1,0:T(8,128)(2,1)S(1)} %get-tuple-element.49.refs_2_.refs_1_), channel_id=1, source_target_pairs={{0,8},{1,9},{2,10},{3,11},{4,12},{5,13},{6,14},{7,15},{8,0},{9,1},... | collective-permute-start | bytes 196616 | tf_op jit(solution)/shard_map/ppermute | solution.py:257
  9.0 6.1 %collective-permute-start.4 = (bf16[256,128]{1,0:T(8,128)(2,1)S(1)}, bf16[256,128]{1,0:T(8,128)(2,1)S(1)}, u32[]{:S(2)}, u32[]{:S(2)}) collective-permute-start(bf16[256,128]{1,0:T(8,128)(2,1)S(1)} %get-tuple-element.49.refs_2_.refs_1_), channel_id=1, source_target_pairs={{0,12},{1,13},{2,14},{3,15},{4,8},{5,9},{6,10},{7,11},{8,4},{9,5},... | collective-permute-start | bytes 196616 | tf_op jit(solution)/shard_map/ppermute | solution.py:257
  11.3 1.5 %collective-permute-start.3 = (bf16[1056,128]{1,0:T(8,128)(2,1)S(1)}, bf16[1056,128]{1,0:T(8,128)(2,1)S(1)}, u32[]{:S(2)}, u32[]{:S(2)}) collective-permute-start(bf16[1056,128]{1,0:T(8,128)(2,1)S(1)} %collective-permute-done.1.refs_0_), channel_id=1, source_target_pairs={{0,1},{1,0},{2,3},{3,2},{4,5},{5,4},{6,7},{7,6},{8,9},{9,8},{10,11... | collective-permute-start | bytes 811016 | tf_op jit(solution)/shard_map/ppermute | solution.py:257
  16.0 2.8 %collective-permute-start.7 = (f32[1024,128]{1,0:T(8,128)S(1)}, f32[1024,128]{1,0:T(8,128)S(1)}, u32[]{:S(2)}, u32[]{:S(2)}) collective-permute-start(f32[1024,128]{1,0:T(8,128)S(1)} %get-tuple-element.77), channel_id=1, source_target_pairs={{0,1},{1,0},{2,3},{3,2},{4,5},{5,4},{6,7},{7,6},{8,9},{9,8},{10,11... | collective-permute-start | bytes 1572872 | tf_op jit(solution)/shard_map/ppermute | solution.py:257
  19.0 8.9 %collective-permute-start.8 = (s16[1056,128]{1,0:T(8,128)(2,1)S(1)}, s16[1056,128]{1,0:T(8,128)(2,1)S(1)}, u32[]{:S(2)}, u32[]{:S(2)}) collective-permute-start(s16[1056,128]{1,0:T(8,128)(2,1)S(1)} %core_sum.1), channel_id=1, source_target_pairs={{0,2},{1,3},{2,0},{3,1},{4,6},{5,7},{6,4},{7,5},{8,10},{9,11},{10,... | collective-permute-start | bytes 811016 | tf_op jit(solution)/shard_map/ppermute | solution.py:257
  19.7 4.2 %collective-permute-start.6 = (s16[1040,128]{1,0:T(8,128)(2,1)S(1)}, s16[1040,128]{1,0:T(8,128)(2,1)S(1)}, u32[]{:S(2)}, u32[]{:S(2)}) collective-permute-start(s16[1040,128]{1,0:T(8,128)(2,1)S(1)} %get-tuple-element.75), channel_id=1, source_target_pairs={{0,1},{1,0},{2,3},{3,2},{4,5},{5,4},{6,7},{7,6},{8,9},{9,8},{10,11... | collective-permute-start | bytes 798728 | tf_op jit(solution)/shard_map/ppermute | solution.py:257
  19.8 9.1 %collective-permute-start.9 = (s16[144,256]{1,0:T(8,128)(2,1)S(1)}, s16[144,256]{1,0:T(8,128)(2,1)S(1)}, u32[]{:S(2)}, u32[]{:S(2)}) collective-permute-start(s16[144,256]{1,0:T(8,128)(2,1)S(1)} %get-tuple-element.86), channel_id=1, source_target_pairs={{0,8},{1,9},{2,10},{3,11},{4,12},{5,13},{6,14},{7,15},{8,0},{9,1},... | collective-permute-start | bytes 221192 | tf_op jit(solution)/shard_map/ppermute | solution.py:257
  22.4 6.9 %collective-permute-start.10 = (s16[144,256]{1,0:T(8,128)(2,1)S(1)}, s16[144,256]{1,0:T(8,128)(2,1)S(1)}, u32[]{:S(2)}, u32[]{:S(2)}) collective-permute-start(s16[144,256]{1,0:T(8,128)(2,1)S(1)} %get-tuple-element.87), channel_id=1, source_target_pairs={{0,12},{1,13},{2,14},{3,15},{4,8},{5,9},{6,10},{7,11},{8,4},{9,5},... | collective-permute-start | bytes 221192 | tf_op jit(solution)/shard_map/ppermute | solution.py:257
  23.7 6.1 %collective-permute-start.11 = (s16[144,256]{1,0:T(8,128)(2,1)S(1)}, s16[144,256]{1,0:T(8,128)(2,1)S(1)}, u32[]{:S(2)}, u32[]{:S(2)}) collective-permute-start(s16[144,256]{1,0:T(8,128)(2,1)S(1)} %get-tuple-element.88), channel_id=1, source_target_pairs={{0,4},{1,5},{2,6},{3,7},{4,0},{5,1},{6,2},{7,3},{8,12},{9,13},{10,... | collective-permute-start | bytes 221192 | tf_op jit(solution)/shard_map/ppermute | solution.py:257

commit v10 on v9

--- a/solution.py
+++ b/solution.py
@@ -183,14 +183,15 @@
             term = gv_ref[:, s * wide : (s + 1) * wide]
             if group[s] in send:
                 code, exponent = encode(term)
-                gv_outs[s][0:dim, :] = code
-                gv_outs[s][dim:, :] = tail_of([exponent])
+                gv_outs[s][0:dim, :] = code[:, :local_v]
+                gv_outs[s][dim : 2 * dim, :] = code[:, local_v:]
+                gv_outs[s][2 * dim :, :] = tail_of([exponent[:, :local_v], exponent[:, local_v:]])
             else:
                 gv_outs[s][...] = term
 
     operands = [*sets, *vds, *([] if fresh else [table]), *(gqs or []), *(gvs or [])]
     outs = [jax.ShapeDtypeStruct((rows, dim), F32)] * k + [
-        jax.ShapeDtypeStruct((dim + TAIL, wide), I16)
+        jax.ShapeDtypeStruct((2 * dim + TAIL, local_v), I16)
         if s in send
         else jax.ShapeDtypeStruct((dim, wide), F32)
         for s in group
@@ -233,14 +234,15 @@
 
 def finish_v_kernel(term_ref, *refs):
     got_terms, (gv_out, gd_out) = refs[:-2], refs[-2:]
-    total = term_ref[...]
-    dim = total.shape[0]
-    for got in got_terms:
-        tail = got[dim:, :].astype(jnp.int32).astype(F32)
-        total = total + decode(got[0:dim, :], tail[0:1, :])
+    dim = term_ref.shape[0]
     local_v = gv_out.shape[0]
-    gv_out[...] = total[:, :local_v].T
-    gd_out[...] = total[:, local_v:].T
+    tails = [got[2 * dim :, :].astype(jnp.int32).astype(F32) for got in got_terms]
+    for part, out in enumerate((gv_out, gd_out)):
+        total = term_ref[:, part * local_v : (part + 1) * local_v]
+        for got, tail in zip(got_terms, tails):
+            code = got[part * dim : (part + 1) * dim, :]
+            total = total + decode(code, tail[part : part + 1, :])
+        out[...] = total.T
 
 
 def body(queries, vectors, decoded, mask):

time: 30.8 us -> 30.5 us (level)
  waiting for transfers between devices: 6.85 us -> 6.54 us
where the time goes in v10:
time: 30.5 us; the launch traced here: 30.3 us
  starting transfers between devices  12.5 us (41%)
  Pallas kernels  10.6 us (35%)
  waiting for transfers between devices  6.54 us (21%)
  between operations  0.73 us (2%)
    ppermute x12, starting transfers between devices, swap(): return lax.ppermute(x, 'qry', [(i, i ^ bit) for i in range(n)])  12.5 us
    pallas_call x7, Pallas kernels, grads(): pl.pallas_call(kernel, out_shape=tuple(outs), in_specs=[VMEM] * len(opera...  7.63 us
    ppermute x12, waiting for transfers between devices, swap(): return lax.ppermute(x, 'qry', [(i, i ^ bit) for i in range(n)])  6.54 us
    pallas_call x1, Pallas kernels, body(): pl.pallas_call(pack_kernel, out_shape=(jax.ShapeDtypeStruct((rows + pad,...  1.13 us
    pallas_call x1, Pallas kernels, body(): pl.pallas_call(finish_q_kernel, out_shape=row_out, in_specs=[VMEM] * 3, o...  0.94 us
    pallas_call x1, Pallas kernels, body(): pl.pallas_call(finish_v_kernel, out_shape=(vec_out, vec_out), in_specs=[V...  0.78 us
  transfers between devices with their start and end apart: 12, of which 6 were waited for; matrix products, arithmetic and copies ran while one was open for 0% of the time, Pallas kernels for 25%

profile of v10, /device:TPU:0, one launch (start us, length us, event | category | flops | bytes accessed | tf_op | source)
XLA Modules:
  0.0 30.3 jit_solution(10897163048624865569)
XLA Ops:
  0.6 1.1 %pack.1 = (bf16[1040,128]{1,0:T(8,128)(2,1)S(1)}, bf16[1056,128]{1,0:T(8,128)(2,1)S(1)}, bf16[256,128]{1,0:T(8,128)(2,1)S(1)}) custom-call(bf16[1024,128]{1,0:T(8,128)(2,1)} %q_hbm.1, bf16[128,128]{1,0:T(8,128)(2,1)} %v_hbm.1, bf16[128,128]{1,0:T(8,128)(2,1)} %d_hbm.1, s32[4,8]{1,0:T(4,128)} %m_hbm.1), custom_call_target="tpu_custom_call" | custom-call | tf_op jit(solution)/shard_map/pack/pallas_call | solution.py:261
  1.8 3.0 %collective-permute-start.1 = (bf16[1056,128]{1,0:T(8,128)(2,1)S(1)}, bf16[1056,128]{1,0:T(8,128)(2,1)S(1)}, u32[]{:S(2)}, u32[]{:S(2)}) collective-permute-start(bf16[1056,128]{1,0:T(8,128)(2,1)S(1)} %get-tuple-element.48), channel_id=1, source_target_pairs={{0,2},{1,3},{2,0},{3,1},{4,6},{5,7},{6,4},{7,5},{8,10},{9,11},{10,... | collective-permute-start | bytes 811016 | tf_op jit(solution)/shard_map/ppermute | solution.py:259
  4.8 0.0 collective-permute-start
  4.8 1.6 %collective-permute-start.2 = (bf16[256,128]{1,0:T(8,128)(2,1)S(1)}, bf16[256,128]{1,0:T(8,128)(2,1)S(1)}, u32[]{:S(2)}, u32[]{:S(2)}) collective-permute-start(bf16[256,128]{1,0:T(8,128)(2,1)S(1)} %get-tuple-element.49.refs_2_.refs_1_), channel_id=1, source_target_pairs={{0,4},{1,5},{2,6},{3,7},{4,0},{5,1},{6,2},{7,3},{8,12},{9,13},{10,... | collective-permute-start | bytes 196616 | tf_op jit(solution)/shard_map/ppermute | solution.py:259
  6.4 2.6 %collective-permute-start.5 = (bf16[256,128]{1,0:T(8,128)(2,1)S(1)}, bf16[256,128]{1,0:T(8,128)(2,1)S(1)}, u32[]{:S(2)}, u32[]{:S(2)}) collective-permute-start(bf16[256,128]{1,0:T(8,128)(2,1)S(1)} %get-tuple-element.49.refs_2_.refs_1_), channel_id=1, source_target_pairs={{0,8},{1,9},{2,10},{3,11},{4,12},{5,13},{6,14},{7,15},{8,0},{9,1},... | collective-permute-start | bytes 196616 | tf_op jit(solution)/shard_map/ppermute | solution.py:259
  9.0 0.2 collective-permute-start.4
  9.2 0.0 collective-permute-done.refs_1_
  9.2 1.0 %own_0.1 = (f32[1024,128]{1,0:T(8,128)S(1)}, f32[1024,128]{1,0:T(8,128)S(1)}, f32[128,256]{1,0:T(8,128)S(1)}, f32[4,32,128]{2,1,0:T(8,128)S(1)}) custom-call(bf16[1040,128]{1,0:T(8,128)(2,1)S(1)} %get-tuple-element.47.refs_0_, bf16[1040,128]{1,0:T(8,128)(2,1)S(1)} %collective-permute-done.refs_1_, bf16[256,128]{1,0:T(8,128)(2,1)S(1)} %get-tuple-element.49.refs_2_.refs_1_), custom_call_target="tpu_custom_call" | custom-call | bytes 1024 | tf_op jit(solution)/shard_map/own_0/pallas_call | solution.py:203
  10.2 0.0 collective-permute-done.2.refs_2_
  10.2 1.0 %own_1.1 = (f32[1024,128]{1,0:T(8,128)S(1)}, f32[1024,128]{1,0:T(8,128)S(1)}, f32[128,256]{1,0:T(8,128)S(1)}) custom-call(bf16[1040,128]{1,0:T(8,128)(2,1)S(1)} %get-tuple-element.47.refs_0_, bf16[1040,128]{1,0:T(8,128)(2,1)S(1)} %collective-permute-done.refs_1_, bf16[256,128]{1,0:T(8,128)(2,1)S(1)} %collective-permute-done.2.refs_2_, ...), custom_call_target="tpu_custom_call" | custom-call | bytes 1024 | tf_op jit(solution)/shard_map/own_1/pallas_call | solution.py:203
  11.2 0.1 collective-permute-done.1.refs_0_
  11.3 0.0 collective-permute-start.3
  11.3 1.0 %y_01.1 = (f32[1024,128]{1,0:T(8,128)S(1)}, f32[128,256]{1,0:T(8,128)S(1)}, f32[128,256]{1,0:T(8,128)S(1)}, f32[4,16,128]{2,1,0:T(8,128)S(1)}) custom-call(bf16[1056,128]{1,0:T(8,128)(2,1)S(1)} %collective-permute-done.1.refs_0_, bf16[256,128]{1,0:T(8,128)(2,1)S(1)} %get-tuple-element.49.refs_2_.refs_1_, ...), custom_call_target="tpu_custom_call" | custom-call | flops 8589934592 | bytes 1024 | tf_op jit(solution)/shard_map/y_01/pallas_call | solution.py:203
  12.3 0.6 %collective-permute-done.3.refs_0_ = bf16[1056,128]{1,0:T(8,128)(2,1)S(1)} collective-permute-done((bf16[1056,128]{1,0:T(8,128)(2,1)S(1)}, bf16[1056,128]{1,0:T(8,128)(2,1)S(1)}, u32[]{:S(2)}, u32[]{:S(2)}) %collective-permute-start.3) | collective-permute-done | bytes 270368 | tf_op jit(solution)/shard_map/ppermute | solution.py:259
  12.8 1.0 %yc_01.1 = (f32[1024,128]{1,0:T(8,128)S(1)}, f32[128,256]{1,0:T(8,128)S(1)}, s16[272,128]{1,0:T(8,128)(2,1)S(1)}, f32[4,16,128]{2,1,0:T(8,128)S(1)}) custom-call(bf16[1056,128]{1,0:T(8,128)(2,1)S(1)} %collective-permute-done.3.refs_0_, bf16[256,128]{1,0:T(8,128)(2,1)S(1)} %get-tuple-element.49.refs_2_.refs_1_, ...), custom_call_target="tpu_custom_call" | custom-call | flops 524288 | bytes 1024 | tf_op jit(solution)/shard_map/yc_01/pallas_call | solution.py:203
  13.8 0.0 collective-permute-done.5.refs_1_.refs_2_
  13.8 1.2 %collective-permute-done.4.refs_2_.refs_3_ = bf16[256,128]{1,0:T(8,128)(2,1)S(1)} collective-permute-done((bf16[256,128]{1,0:T(8,128)(2,1)S(1)}, bf16[256,128]{1,0:T(8,128)(2,1)S(1)}, u32[]{:S(2)}, u32[]{:S(2)}) %collective-permute-start.4) | collective-permute-done | bytes 65568 | tf_op jit(solution)/shard_map/ppermute | solution.py:259
  15.1 1.0 %yc_23.1 = (f32[1024,128]{1,0:T(8,128)S(1)}, f32[128,256]{1,0:T(8,128)S(1)}, f32[128,256]{1,0:T(8,128)S(1)}) custom-call(bf16[1056,128]{1,0:T(8,128)(2,1)S(1)} %collective-permute-done.3.refs_0_, bf16[256,128]{1,0:T(8,128)(2,1)S(1)} %collective-permute-done.5.refs_1_.refs_2_, bf16[256,128]{1,0:T(8,128)(2,1)S(1)} %collective-permute-done.4.refs_2_.refs_3_, ...), custom_call_target="tpu_custom_call" | custom-call | flops 524288 | bytes 1024 | tf_op jit(solution)/shard_map/yc_23/pallas_call | solution.py:203
  16.0 0.1 collective-permute-start.7
  16.1 0.9 %y_23.1 = (f32[1024,128]{1,0:T(8,128)S(1)}, f32[128,256]{1,0:T(8,128)S(1)}, f32[128,256]{1,0:T(8,128)S(1)}) custom-call(bf16[1056,128]{1,0:T(8,128)(2,1)S(1)} %collective-permute-done.1.refs_0_, bf16[256,128]{1,0:T(8,128)(2,1)S(1)} %collective-permute-done.5.refs_1_.refs_2_, bf16[256,128]{1,0:T(8,128)(2,1)S(1)} %collective-permute-done.4.refs_2_.refs_3_, ...), custom_call_target="tpu_custom_call" | custom-call | flops 524288 | bytes 1024 | tf_op jit(solution)/shard_map/y_23/pallas_call | solution.py:203
  17.1 1.8 %own_23.1 = (f32[1024,128]{1,0:T(8,128)S(1)}, s16[1040,128]{1,0:T(8,128)(2,1)S(1)}, s16[272,128]{1,0:T(8,128)(2,1)S(1)}, s16[272,128]{1,0:T(8,128)(2,1)S(1)}) custom-call(bf16[1040,128]{1,0:T(8,128)(2,1)S(1)} %get-tuple-element.47.refs_0_, bf16[1040,128]{1,0:T(8,128)(2,1)S(1)} %collective-permute-done.refs_1_, ...), custom_call_target="tpu_custom_call" | custom-call | flops 1048576 | bytes 1024 | tf_op jit(solution)/shard_map/own_23/pallas_call | solution.py:203
  18.8 0.0 collective-permute-done.7.got_y_ref
  18.9 0.1 core_sum.1
  19.0 0.7 %collective-permute-start.8 = (s16[1056,128]{1,0:T(8,128)(2,1)S(1)}, s16[1056,128]{1,0:T(8,128)(2,1)S(1)}, u32[]{:S(2)}, u32[]{:S(2)}) collective-permute-start(s16[1056,128]{1,0:T(8,128)(2,1)S(1)} %core_sum.1), channel_id=1, source_target_pairs={{0,2},{1,3},{2,0},{3,1},{4,6},{5,7},{6,4},{7,5},{8,10},{9,11},{10,... | collective-permute-start | bytes 811016 | tf_op jit(solution)/shard_map/ppermute | solution.py:259
  19.7 0.1 collective-permute-start.6
  19.8 2.6 %collective-permute-start.9 = (s16[272,128]{1,0:T(8,128)(2,1)S(1)}, s16[272,128]{1,0:T(8,128)(2,1)S(1)}, u32[]{:S(2)}, u32[]{:S(2)}) collective-permute-start(s16[272,128]{1,0:T(8,128)(2,1)S(1)} %get-tuple-element.86), channel_id=1, source_target_pairs={{0,8},{1,9},{2,10},{3,11},{4,12},{5,13},{6,14},{7,15},{8,0},{9,1},... | collective-permute-start | bytes 208904 | tf_op jit(solution)/shard_map/ppermute | solution.py:259
  22.4 1.3 %collective-permute-start.10 = (s16[272,128]{1,0:T(8,128)(2,1)S(1)}, s16[272,128]{1,0:T(8,128)(2,1)S(1)}, u32[]{:S(2)}, u32[]{:S(2)}) collective-permute-start(s16[272,128]{1,0:T(8,128)(2,1)S(1)} %get-tuple-element.87), channel_id=1, source_target_pairs={{0,12},{1,13},{2,14},{3,15},{4,8},{5,9},{6,10},{7,11},{8,4},{9,5},... | collective-permute-start | bytes 208904 | tf_op jit(solution)/shard_map/ppermute | solution.py:259
  23.7 0.2 collective-permute-start.11
  24.0 0.0 collective-permute-done.6.got_own_ref
  24.0 4.0 %collective-permute-done.8.got_ref = s16[1056,128]{1,0:T(8,128)(2,1)S(1)} collective-permute-done((s16[1056,128]{1,0:T(8,128)(2,1)S(1)}, s16[1056,128]{1,0:T(8,128)(2,1)S(1)}, u32[]{:S(2)}, u32[]{:S(2)}) %collective-permute-start.8) | collective-permute-done | bytes 270368 | tf_op jit(solution)/shard_map/ppermute | solution.py:259
  27.9 0.9 %finish_q.1 = f32[1024,128]{1,0:T(8,128)} custom-call(f32[1024,128]{1,0:T(8,128)S(1)} %get-tuple-element.74.own_ref, s16[1040,128]{1,0:T(8,128)(2,1)S(1)} %collective-permute-done.6.got_own_ref, s16[1056,128]{1,0:T(8,128)(2,1)S(1)} %collective-permute-done.8.got_ref), custom_call_target="tpu_custom_call" | custom-call | tf_op jit(solution)/shard_map/finish_q/pallas_call | solution.py:319
  28.9 0.0 collective-permute-done.9.refs_0_
  28.9 0.3 collective-permute-done.10.refs_1_
  29.2 0.4 %collective-permute-done.11.refs_2_ = s16[272,128]{1,0:T(8,128)(2,1)S(1)} collective-permute-done((s16[272,128]{1,0:T(8,128)(2,1)S(1)}, s16[272,128]{1,0:T(8,128)(2,1)S(1)}, u32[]{:S(2)}, u32[]{:S(2)}) %collective-permute-start.11) | collective-permute-done | bytes 69664 | tf_op jit(solution)/shard_map/ppermute | solution.py:259
  29.6 0.8 %finish_v.1 = (f32[128,128]{1,0:T(8,128)}, f32[128,128]{1,0:T(8,128)}) custom-call(f32[128,256]{1,0:T(8,128)S(1)} %get-tuple-element.85.term_ref, s16[272,128]{1,0:T(8,128)(2,1)S(1)} %collective-permute-done.9.refs_0_, s16[272,128]{1,0:T(8,128)(2,1)S(1)} %collective-permute-done.10.refs_1_, s16[272,128]{1,0:T(8,128)(2,1)S(1)} %collective-permute-done.11.refs_2_), custom_call_target="tpu_custom_call" | custom-call | tf_op jit(solution)/shard_map/finish_v/pallas_call | solution.py:329
Async XLA Ops:
  1.8 9.5 %collective-permute-start.1 = (bf16[1056,128]{1,0:T(8,128)(2,1)S(1)}, bf16[1056,128]{1,0:T(8,128)(2,1)S(1)}, u32[]{:S(2)}, u32[]{:S(2)}) collective-permute-start(bf16[1056,128]{1,0:T(8,128)(2,1)S(1)} %get-tuple-element.48), channel_id=1, source_target_pairs={{0,2},{1,3},{2,0},{3,1},{4,6},{5,7},{6,4},{7,5},{8,10},{9,11},{10,... | collective-permute-start | bytes 811016 | tf_op jit(solution)/shard_map/ppermute | solution.py:259
  4.8 4.4 %collective-permute-start = (bf16[1040,128]{1,0:T(8,128)(2,1)S(1)}, bf16[1040,128]{1,0:T(8,128)(2,1)S(1)}, u32[]{:S(2)}, u32[]{:S(2)}) collective-permute-start(bf16[1040,128]{1,0:T(8,128)(2,1)S(1)} %get-tuple-element.47.refs_0_), channel_id=1, source_target_pairs={{0,1},{1,0},{2,3},{3,2},{4,5},{5,4},{6,7},{7,6},{8,9},{9,8},{10,11... | collective-permute-start | bytes 798728 | tf_op jit(solution)/shard_map/ppermute | solution.py:259
  4.8 5.4 %collective-permute-start.2 = (bf16[256,128]{1,0:T(8,128)(2,1)S(1)}, bf16[256,128]{1,0:T(8,128)(2,1)S(1)}, u32[]{:S(2)}, u32[]{:S(2)}) collective-permute-start(bf16[256,128]{1,0:T(8,128)(2,1)S(1)} %get-tuple-element.49.refs_2_.refs_1_), channel_id=1, source_target_pairs={{0,4},{1,5},{2,6},{3,7},{4,0},{5,1},{6,2},{7,3},{8,12},{9,13},{10,... | collective-permute-start | bytes 196616 | tf_op jit(solution)/shard_map/ppermute | solution.py:259
  6.4 7.5 %collective-permute-start.5 = (bf16[256,128]{1,0:T(8,128)(2,1)S(1)}, bf16[256,128]{1,0:T(8,128)(2,1)S(1)}, u32[]{:S(2)}, u32[]{:S(2)}) collective-permute-start(bf16[256,128]{1,0:T(8,128)(2,1)S(1)} %get-tuple-element.49.refs_2_.refs_1_), channel_id=1, source_target_pairs={{0,8},{1,9},{2,10},{3,11},{4,12},{5,13},{6,14},{7,15},{8,0},{9,1},... | collective-permute-start | bytes 196616 | tf_op jit(solution)/shard_map/ppermute | solution.py:259
  9.0 6.1 %collective-permute-start.4 = (bf16[256,128]{1,0:T(8,128)(2,1)S(1)}, bf16[256,128]{1,0:T(8,128)(2,1)S(1)}, u32[]{:S(2)}, u32[]{:S(2)}) collective-permute-start(bf16[256,128]{1,0:T(8,128)(2,1)S(1)} %get-tuple-element.49.refs_2_.refs_1_), channel_id=1, source_target_pairs={{0,12},{1,13},{2,14},{3,15},{4,8},{5,9},{6,10},{7,11},{8,4},{9,5},... | collective-permute-start | bytes 196616 | tf_op jit(solution)/shard_map/ppermute | solution.py:259
  11.3 1.6 %collective-permute-start.3 = (bf16[1056,128]{1,0:T(8,128)(2,1)S(1)}, bf16[1056,128]{1,0:T(8,128)(2,1)S(1)}, u32[]{:S(2)}, u32[]{:S(2)}) collective-permute-start(bf16[1056,128]{1,0:T(8,128)(2,1)S(1)} %collective-permute-done.1.refs_0_), channel_id=1, source_target_pairs={{0,1},{1,0},{2,3},{3,2},{4,5},{5,4},{6,7},{7,6},{8,9},{9,8},{10,11... | collective-permute-start | bytes 811016 | tf_op jit(solution)/shard_map/ppermute | solution.py:259
  16.0 2.8 %collective-permute-start.7 = (f32[1024,128]{1,0:T(8,128)S(1)}, f32[1024,128]{1,0:T(8,128)S(1)}, u32[]{:S(2)}, u32[]{:S(2)}) collective-permute-start(f32[1024,128]{1,0:T(8,128)S(1)} %get-tuple-element.77), channel_id=1, source_target_pairs={{0,1},{1,0},{2,3},{3,2},{4,5},{5,4},{6,7},{7,6},{8,9},{9,8},{10,11... | collective-permute-start | bytes 1572872 | tf_op jit(solution)/shard_map/ppermute | solution.py:259
  19.0 8.9 %collective-permute-start.8 = (s16[1056,128]{1,0:T(8,128)(2,1)S(1)}, s16[1056,128]{1,0:T(8,128)(2,1)S(1)}, u32[]{:S(2)}, u32[]{:S(2)}) collective-permute-start(s16[1056,128]{1,0:T(8,128)(2,1)S(1)} %core_sum.1), channel_id=1, source_target_pairs={{0,2},{1,3},{2,0},{3,1},{4,6},{5,7},{6,4},{7,5},{8,10},{9,11},{10,... | collective-permute-start | bytes 811016 | tf_op jit(solution)/shard_map/ppermute | solution.py:259
  19.7 4.3 %collective-permute-start.6 = (s16[1040,128]{1,0:T(8,128)(2,1)S(1)}, s16[1040,128]{1,0:T(8,128)(2,1)S(1)}, u32[]{:S(2)}, u32[]{:S(2)}) collective-permute-start(s16[1040,128]{1,0:T(8,128)(2,1)S(1)} %get-tuple-element.75), channel_id=1, source_target_pairs={{0,1},{1,0},{2,3},{3,2},{4,5},{5,4},{6,7},{7,6},{8,9},{9,8},{10,11... | collective-permute-start | bytes 798728 | tf_op jit(solution)/shard_map/ppermute | solution.py:259
  19.8 9.1 %collective-permute-start.9 = (s16[272,128]{1,0:T(8,128)(2,1)S(1)}, s16[272,128]{1,0:T(8,128)(2,1)S(1)}, u32[]{:S(2)}, u32[]{:S(2)}) collective-permute-start(s16[272,128]{1,0:T(8,128)(2,1)S(1)} %get-tuple-element.86), channel_id=1, source_target_pairs={{0,8},{1,9},{2,10},{3,11},{4,12},{5,13},{6,14},{7,15},{8,0},{9,1},... | collective-permute-start | bytes 208904 | tf_op jit(solution)/shard_map/ppermute | solution.py:259
  22.4 6.8 %collective-permute-start.10 = (s16[272,128]{1,0:T(8,128)(2,1)S(1)}, s16[272,128]{1,0:T(8,128)(2,1)S(1)}, u32[]{:S(2)}, u32[]{:S(2)}) collective-permute-start(s16[272,128]{1,0:T(8,128)(2,1)S(1)} %get-tuple-element.87), channel_id=1, source_target_pairs={{0,12},{1,13},{2,14},{3,15},{4,8},{5,9},{6,10},{7,11},{8,4},{9,5},... | collective-permute-start | bytes 208904 | tf_op jit(solution)/shard_map/ppermute | solution.py:259
  23.7 5.8 %collective-permute-start.11 = (s16[272,128]{1,0:T(8,128)(2,1)S(1)}, s16[272,128]{1,0:T(8,128)(2,1)S(1)}, u32[]{:S(2)}, u32[]{:S(2)}) collective-permute-start(s16[272,128]{1,0:T(8,128)(2,1)S(1)} %get-tuple-element.88), channel_id=1, source_target_pairs={{0,4},{1,5},{2,6},{3,7},{4,0},{5,1},{6,2},{7,3},{8,12},{9,13},{10,... | collective-permute-start | bytes 208904 | tf_op jit(solution)/shard_map/ppermute | solution.py:259

commit v11 on v10

--- a/solution.py
+++ b/solution.py
@@ -115,13 +115,15 @@
     part = min(m, 4)
     height = 2 * BLK if rows % (2 * BLK) == 0 else BLK
     fresh = table is None
+    tables = [] if fresh else table
+    place = [(i, j) for i, x in enumerate(tables) for j in range(0, x.shape[1], pad)]
 
     def kernel(*refs):
         qm_refs, refs = refs[:k], refs[k:]
         vd_refs, refs = refs[:m], refs[m:]
         gq_ins, gv_ins = None, None
         if not fresh:
-            table_ref, refs = refs[0], refs[1:]
+            table_refs, refs = refs[: len(tables)], refs[len(tables) :]
         if gqs is not None:
             gq_ins, refs = refs[:k], refs[k:]
         if gvs is not None:
@@ -145,7 +147,8 @@
         def tile(t, r0, first):
             def live(b, c):
                 s = group[first + c]
-                return table_ref[s, pl.ds(t * pad + r0 // BLK + b, 1), :]
+                ref, row = (table_ref, t * pad) if fresh else (table_refs[place[t][0]], place[t][1])
+                return ref[s, pl.ds(row + r0 // BLK + b, 1), :]
 
             w = w_ref[first * wide : (first + part) * wide, :]
             weights = tile_weights(qm_refs[t][pl.ds(r0, height), :], w, live, part, local_v)
@@ -189,7 +192,7 @@
             else:
                 gv_outs[s][...] = term
 
-    operands = [*sets, *vds, *([] if fresh else [table]), *(gqs or []), *(gvs or [])]
+    operands = [*sets, *vds, *tables, *(gqs or []), *(gvs or [])]
     outs = [jax.ShapeDtypeStruct((rows, dim), F32)] * k + [
         jax.ShapeDtypeStruct((2 * dim + TAIL, local_v), I16)
         if s in send
@@ -289,17 +292,19 @@
     own = [qm, qm_c]
     near, far = tuple(range(1, half)), tuple(range(half, chunks))
     gq_o, gv0, table = add(own, [0], None, None, None, (), "own_0", weight=0)
-    gq_o, gv1, _ = add(own, [1], table, gq_o, None, (), "own_1", weight=0)
+    gq_o, gv1, _ = add(own, [1], [table], gq_o, None, (), "own_1", weight=0)
     qm_y, gv1 = lax.optimization_barrier((qm_y, gv1))
     qm_yc = swap(qm_y, 1)
     gq_y, gv01, table_y = add([qm_y], [0, 1], None, None, gv0 + gv1, (), "y_01", weight=HEAVY)
     gq_yc, gv01, table_yc = add([qm_yc], [0, 1], None, None, gv01, near, "yc_01")
     gq_yc, gv01, late = lax.optimization_barrier((gq_yc, gv01, vds[half:][::-1]))
     vds[half:] = late[::-1]
-    gq_yc, gv23, _ = add([qm_yc], [2, 3], table_yc, gq_yc, None, (), "yc_23")
+    gq_yc, gv23, _ = add([qm_yc], [2, 3], [table_yc], gq_yc, None, (), "yc_23")
     got_y = swap(gq_yc[0], 1)
-    gq_y, gv23, _ = add([qm_y], [2, 3], table_y, gq_y, gv23, (), "y_23")
-    gq_o, gv23, _ = add(own, [2, 3], table, gq_o, gv23, far, "own_23", code_last=True)
+    sums, gv23, _ = add(
+        [qm_y, *own], [2, 3], [table_y, table], [gq_y[0], *gq_o], gv23, far, "last_23", code_last=True
+    )
+    gq_y, gq_o = sums[:1], sums[1:]
     got_y, gv01, gv23 = lax.optimization_barrier((got_y, gv01, gv23))
     gq_message = pl.pallas_call(
         core_sum_kernel,

time: 30.5 us -> 30.2 us (level)
    pallas_call x7 -> x6, Pallas kernels: 7.63 us -> 7.33 us  [grads(): pl.pallas_call(kernel, out_shape=tuple(outs), in_specs=[VMEM] * len(opera...]
  transfers between devices with their start and end apart: 12 -> 12, of which waited for: 6 -> 6; matrix products, arithmetic and copies ran while one was open for 0% -> 0% of each run, Pallas kernels for 25% -> 24%
where the time goes in v11:
time: 30.2 us; the launch traced here: 30.1 us
  starting transfers between devices  12.4 us (41%)
  Pallas kernels  10.3 us (34%)
  waiting for transfers between devices  6.58 us (22%)
  between operations  0.72 us (2%)
    ppermute x12, starting transfers between devices, swap(): return lax.ppermute(x, 'qry', [(i, i ^ bit) for i in range(n)])  12.4 us
    pallas_call x6, Pallas kernels, grads(): pl.pallas_call(kernel, out_shape=tuple(outs), in_specs=[VMEM] * len(opera...  7.33 us
    ppermute x12, waiting for transfers between devices, swap(): return lax.ppermute(x, 'qry', [(i, i ^ bit) for i in range(n)])  6.58 us
    pallas_call x1, Pallas kernels, body(): pl.pallas_call(pack_kernel, out_shape=(jax.ShapeDtypeStruct((rows + pad,...  1.13 us
    pallas_call x1, Pallas kernels, body(): pl.pallas_call(finish_q_kernel, out_shape=row_out, in_specs=[VMEM] * 3, o...  0.94 us
    pallas_call x1, Pallas kernels, body(): pl.pallas_call(finish_v_kernel, out_shape=(vec_out, vec_out), in_specs=[V...  0.78 us
  transfers between devices with their start and end apart: 12, of which 6 were waited for; matrix products, arithmetic and copies ran while one was open for 0% of the time, Pallas kernels for 24%

profile of v11, /device:TPU:0, one launch (start us, length us, event | category | flops | bytes accessed | tf_op | source)
XLA Modules:
  0.0 30.1 jit_solution(7734453358349336784)
XLA Ops:
  0.6 1.1 %pack.1 = (bf16[1040,128]{1,0:T(8,128)(2,1)S(1)}, bf16[1056,128]{1,0:T(8,128)(2,1)S(1)}, bf16[256,128]{1,0:T(8,128)(2,1)S(1)}) custom-call(bf16[1024,128]{1,0:T(8,128)(2,1)} %q_hbm.1, bf16[128,128]{1,0:T(8,128)(2,1)} %v_hbm.1, bf16[128,128]{1,0:T(8,128)(2,1)} %d_hbm.1, s32[4,8]{1,0:T(4,128)} %m_hbm.1), custom_call_target="tpu_custom_call" | custom-call | tf_op jit(solution)/shard_map/pack/pallas_call | solution.py:264
  1.8 3.0 %collective-permute-start = (bf16[1056,128]{1,0:T(8,128)(2,1)S(1)}, bf16[1056,128]{1,0:T(8,128)(2,1)S(1)}, u32[]{:S(2)}, u32[]{:S(2)}) collective-permute-start(bf16[1056,128]{1,0:T(8,128)(2,1)S(1)} %get-tuple-element.45), channel_id=1, source_target_pairs={{0,2},{1,3},{2,0},{3,1},{4,6},{5,7},{6,4},{7,5},{8,10},{9,11},{10,... | collective-permute-start | bytes 811016 | tf_op jit(solution)/shard_map/ppermute | solution.py:262
  4.8 0.0 collective-permute-start.1
  4.8 1.6 %collective-permute-start.2 = (bf16[256,128]{1,0:T(8,128)(2,1)S(1)}, bf16[256,128]{1,0:T(8,128)(2,1)S(1)}, u32[]{:S(2)}, u32[]{:S(2)}) collective-permute-start(bf16[256,128]{1,0:T(8,128)(2,1)S(1)} %get-tuple-element.47.refs_2_.refs_1_), channel_id=1, source_target_pairs={{0,4},{1,5},{2,6},{3,7},{4,0},{5,1},{6,2},{7,3},{8,12},{9,13},{10,... | collective-permute-start | bytes 196616 | tf_op jit(solution)/shard_map/ppermute | solution.py:262
  6.4 2.6 %collective-permute-start.5 = (bf16[256,128]{1,0:T(8,128)(2,1)S(1)}, bf16[256,128]{1,0:T(8,128)(2,1)S(1)}, u32[]{:S(2)}, u32[]{:S(2)}) collective-permute-start(bf16[256,128]{1,0:T(8,128)(2,1)S(1)} %get-tuple-element.47.refs_2_.refs_1_), channel_id=1, source_target_pairs={{0,8},{1,9},{2,10},{3,11},{4,12},{5,13},{6,14},{7,15},{8,0},{9,1},... | collective-permute-start | bytes 196616 | tf_op jit(solution)/shard_map/ppermute | solution.py:262
  9.0 0.2 collective-permute-start.4
  9.2 0.0 collective-permute-done.1.refs_1_.refs_2_
  9.2 1.0 %own_0.1 = (f32[1024,128]{1,0:T(8,128)S(1)}, f32[1024,128]{1,0:T(8,128)S(1)}, f32[128,256]{1,0:T(8,128)S(1)}, f32[4,32,128]{2,1,0:T(8,128)S(1)}) custom-call(bf16[1040,128]{1,0:T(8,128)(2,1)S(1)} %get-tuple-element.46.refs_0_.refs_1_, bf16[1040,128]{1,0:T(8,128)(2,1)S(1)} %collective-permute-done.1.refs_1_.refs_2_, ...), custom_call_target="tpu_custom_call" | custom-call | bytes 1024 | tf_op jit(solution)/shard_map/own_0/pallas_call | solution.py:206
  10.2 0.0 collective-permute-done.2.refs_2_
  10.2 1.0 %own_1.1 = (f32[1024,128]{1,0:T(8,128)S(1)}, f32[1024,128]{1,0:T(8,128)S(1)}, f32[128,256]{1,0:T(8,128)S(1)}) custom-call(bf16[1040,128]{1,0:T(8,128)(2,1)S(1)} %get-tuple-element.46.refs_0_.refs_1_, bf16[1040,128]{1,0:T(8,128)(2,1)S(1)} %collective-permute-done.1.refs_1_.refs_2_, bf16[256,128]{1,0:T(8,128)(2,1)S(1)} %collective-permute-done.2.refs_2_, ...), custom_call_target="tpu_custom_call" | custom-call | bytes 1024 | tf_op jit(solution)/shard_map/own_1/pallas_call | solution.py:206
  11.2 0.1 collective-permute-done.refs_0_
  11.3 0.0 collective-permute-start.3
  11.3 1.0 %y_01.1 = (f32[1024,128]{1,0:T(8,128)S(1)}, f32[128,256]{1,0:T(8,128)S(1)}, f32[128,256]{1,0:T(8,128)S(1)}, f32[4,16,128]{2,1,0:T(8,128)S(1)}) custom-call(bf16[1056,128]{1,0:T(8,128)(2,1)S(1)} %collective-permute-done.refs_0_, bf16[256,128]{1,0:T(8,128)(2,1)S(1)} %get-tuple-element.47.refs_2_.refs_1_, bf16[256,128]{1,0:T(8,128)(2,1)S(1)} %collective-permute-done.2.refs_2_, ...), custom_call_target="tpu_custom_call" | custom-call | flops 8589934592 | bytes 1024 | tf_op jit(solution)/shard_map/y_01/pallas_call | solution.py:206
  12.3 0.6 %collective-permute-done.3.refs_0_ = bf16[1056,128]{1,0:T(8,128)(2,1)S(1)} collective-permute-done((bf16[1056,128]{1,0:T(8,128)(2,1)S(1)}, bf16[1056,128]{1,0:T(8,128)(2,1)S(1)}, u32[]{:S(2)}, u32[]{:S(2)}) %collective-permute-start.3) | collective-permute-done | bytes 270368 | tf_op jit(solution)/shard_map/ppermute | solution.py:262
  12.8 1.0 %yc_01.1 = (f32[1024,128]{1,0:T(8,128)S(1)}, f32[128,256]{1,0:T(8,128)S(1)}, s16[272,128]{1,0:T(8,128)(2,1)S(1)}, f32[4,16,128]{2,1,0:T(8,128)S(1)}) custom-call(bf16[1056,128]{1,0:T(8,128)(2,1)S(1)} %collective-permute-done.3.refs_0_, bf16[256,128]{1,0:T(8,128)(2,1)S(1)} %get-tuple-element.47.refs_2_.refs_1_, ...), custom_call_target="tpu_custom_call" | custom-call | flops 524288 | bytes 1024 | tf_op jit(solution)/shard_map/yc_01/pallas_call | solution.py:206
  13.8 0.0 collective-permute-done.5.refs_1_.refs_3_
  13.8 1.2 %collective-permute-done.4.refs_2_.refs_4_ = bf16[256,128]{1,0:T(8,128)(2,1)S(1)} collective-permute-done((bf16[256,128]{1,0:T(8,128)(2,1)S(1)}, bf16[256,128]{1,0:T(8,128)(2,1)S(1)}, u32[]{:S(2)}, u32[]{:S(2)}) %collective-permute-start.4) | collective-permute-done | bytes 65568 | tf_op jit(solution)/shard_map/ppermute | solution.py:262
  15.1 0.9 %yc_23.1 = (f32[1024,128]{1,0:T(8,128)S(1)}, f32[128,256]{1,0:T(8,128)S(1)}, f32[128,256]{1,0:T(8,128)S(1)}) custom-call(bf16[1056,128]{1,0:T(8,128)(2,1)S(1)} %collective-permute-done.3.refs_0_, bf16[256,128]{1,0:T(8,128)(2,1)S(1)} %collective-permute-done.5.refs_1_.refs_3_, bf16[256,128]{1,0:T(8,128)(2,1)S(1)} %collective-permute-done.4.refs_2_.refs_4_, ...), custom_call_target="tpu_custom_call" | custom-call | flops 524288 | bytes 1024 | tf_op jit(solution)/shard_map/yc_23/pallas_call | solution.py:206
  16.0 0.1 collective-permute-start.7
  16.1 2.4 %last_23.1 = (f32[1024,128]{1,0:T(8,128)S(1)}, f32[1024,128]{1,0:T(8,128)S(1)}, s16[1040,128]{1,0:T(8,128)(2,1)S(1)}, s16[272,128]{1,0:T(8,128)(2,1)S(1)}, s16[272,128]{1,0:T(8,128)(2,1)S(1)}) custom-call(bf16[1056,128]{1,0:T(8,128)(2,1)S(1)} %collective-permute-done.refs_0_, bf16[1040,128]{1,0:T(8,128)(2,1)S(1)} %get-tuple-element.46.refs_0_.refs_1_, ...), custom_call_target="tpu_custom_call" | custom-call | flops 1572864 | bytes 1024 | tf_op jit(solution)/shard_map/last_23/pallas_call | solution.py:206
  18.6 0.0 collective-permute-done.7.got_y_ref
  18.6 0.1 core_sum.1
  18.7 0.7 %collective-permute-start.8 = (s16[1056,128]{1,0:T(8,128)(2,1)S(1)}, s16[1056,128]{1,0:T(8,128)(2,1)S(1)}, u32[]{:S(2)}, u32[]{:S(2)}) collective-permute-start(s16[1056,128]{1,0:T(8,128)(2,1)S(1)} %core_sum.1), channel_id=1, source_target_pairs={{0,2},{1,3},{2,0},{3,1},{4,6},{5,7},{6,4},{7,5},{8,10},{9,11},{10,... | collective-permute-start | bytes 811016 | tf_op jit(solution)/shard_map/ppermute | solution.py:262
  19.4 0.1 collective-permute-start.6
  19.5 2.6 %collective-permute-start.9 = (s16[272,128]{1,0:T(8,128)(2,1)S(1)}, s16[272,128]{1,0:T(8,128)(2,1)S(1)}, u32[]{:S(2)}, u32[]{:S(2)}) collective-permute-start(s16[272,128]{1,0:T(8,128)(2,1)S(1)} %get-tuple-element.82), channel_id=1, source_target_pairs={{0,8},{1,9},{2,10},{3,11},{4,12},{5,13},{6,14},{7,15},{8,0},{9,1},... | collective-permute-start | bytes 208904 | tf_op jit(solution)/shard_map/ppermute | solution.py:262
  22.1 1.3 %collective-permute-start.10 = (s16[272,128]{1,0:T(8,128)(2,1)S(1)}, s16[272,128]{1,0:T(8,128)(2,1)S(1)}, u32[]{:S(2)}, u32[]{:S(2)}) collective-permute-start(s16[272,128]{1,0:T(8,128)(2,1)S(1)} %get-tuple-element.83), channel_id=1, source_target_pairs={{0,12},{1,13},{2,14},{3,15},{4,8},{5,9},{6,10},{7,11},{8,4},{9,5},... | collective-permute-start | bytes 208904 | tf_op jit(solution)/shard_map/ppermute | solution.py:262
  23.4 0.2 collective-permute-start.11
  23.7 0.0 collective-permute-done.6.got_own_ref
  23.7 4.0 %collective-permute-done.8.got_ref = s16[1056,128]{1,0:T(8,128)(2,1)S(1)} collective-permute-done((s16[1056,128]{1,0:T(8,128)(2,1)S(1)}, s16[1056,128]{1,0:T(8,128)(2,1)S(1)}, u32[]{:S(2)}, u32[]{:S(2)}) %collective-permute-start.8) | collective-permute-done | bytes 270368 | tf_op jit(solution)/shard_map/ppermute | solution.py:262
  27.7 0.9 %finish_q.1 = f32[1024,128]{1,0:T(8,128)} custom-call(f32[1024,128]{1,0:T(8,128)S(1)} %get-tuple-element.70.own_ref, s16[1040,128]{1,0:T(8,128)(2,1)S(1)} %collective-permute-done.6.got_own_ref, s16[1056,128]{1,0:T(8,128)(2,1)S(1)} %collective-permute-done.8.got_ref), custom_call_target="tpu_custom_call" | custom-call | tf_op jit(solution)/shard_map/finish_q/pallas_call | solution.py:324
  28.6 0.0 collective-permute-done.9.refs_0_
  28.6 0.3 collective-permute-done.10.refs_1_
  28.9 0.4 %collective-permute-done.11.refs_2_ = s16[272,128]{1,0:T(8,128)(2,1)S(1)} collective-permute-done((s16[272,128]{1,0:T(8,128)(2,1)S(1)}, s16[272,128]{1,0:T(8,128)(2,1)S(1)}, u32[]{:S(2)}, u32[]{:S(2)}) %collective-permute-start.11) | collective-permute-done | bytes 69664 | tf_op jit(solution)/shard_map/ppermute | solution.py:262
  29.3 0.8 %finish_v.1 = (f32[128,128]{1,0:T(8,128)}, f32[128,128]{1,0:T(8,128)}) custom-call(f32[128,256]{1,0:T(8,128)S(1)} %get-tuple-element.81.term_ref, s16[272,128]{1,0:T(8,128)(2,1)S(1)} %collective-permute-done.9.refs_0_, s16[272,128]{1,0:T(8,128)(2,1)S(1)} %collective-permute-done.10.refs_1_, s16[272,128]{1,0:T(8,128)(2,1)S(1)} %collective-permute-done.11.refs_2_), custom_call_target="tpu_custom_call" | custom-call | tf_op jit(solution)/shard_map/finish_v/pallas_call | solution.py:334
Async XLA Ops:
  1.8 9.5 %collective-permute-start = (bf16[1056,128]{1,0:T(8,128)(2,1)S(1)}, bf16[1056,128]{1,0:T(8,128)(2,1)S(1)}, u32[]{:S(2)}, u32[]{:S(2)}) collective-permute-start(bf16[1056,128]{1,0:T(8,128)(2,1)S(1)} %get-tuple-element.45), channel_id=1, source_target_pairs={{0,2},{1,3},{2,0},{3,1},{4,6},{5,7},{6,4},{7,5},{8,10},{9,11},{10,... | collective-permute-start | bytes 811016 | tf_op jit(solution)/shard_map/ppermute | solution.py:262
  4.8 4.4 %collective-permute-start.1 = (bf16[1040,128]{1,0:T(8,128)(2,1)S(1)}, bf16[1040,128]{1,0:T(8,128)(2,1)S(1)}, u32[]{:S(2)}, u32[]{:S(2)}) collective-permute-start(bf16[1040,128]{1,0:T(8,128)(2,1)S(1)} %get-tuple-element.46.refs_0_.refs_1_), channel_id=1, source_target_pairs={{0,1},{1,0},{2,3},{3,2},{4,5},{5,4},{6,7},{7,6},{8,9},{9,8},{10,11... | collective-permute-start | bytes 798728 | tf_op jit(solution)/shard_map/ppermute | solution.py:262
  4.8 5.4 %collective-permute-start.2 = (bf16[256,128]{1,0:T(8,128)(2,1)S(1)}, bf16[256,128]{1,0:T(8,128)(2,1)S(1)}, u32[]{:S(2)}, u32[]{:S(2)}) collective-permute-start(bf16[256,128]{1,0:T(8,128)(2,1)S(1)} %get-tuple-element.47.refs_2_.refs_1_), channel_id=1, source_target_pairs={{0,4},{1,5},{2,6},{3,7},{4,0},{5,1},{6,2},{7,3},{8,12},{9,13},{10,... | collective-permute-start | bytes 196616 | tf_op jit(solution)/shard_map/ppermute | solution.py:262
  6.4 7.5 %collective-permute-start.5 = (bf16[256,128]{1,0:T(8,128)(2,1)S(1)}, bf16[256,128]{1,0:T(8,128)(2,1)S(1)}, u32[]{:S(2)}, u32[]{:S(2)}) collective-permute-start(bf16[256,128]{1,0:T(8,128)(2,1)S(1)} %get-tuple-element.47.refs_2_.refs_1_), channel_id=1, source_target_pairs={{0,8},{1,9},{2,10},{3,11},{4,12},{5,13},{6,14},{7,15},{8,0},{9,1},... | collective-permute-start | bytes 196616 | tf_op jit(solution)/shard_map/ppermute | solution.py:262
  9.0 6.1 %collective-permute-start.4 = (bf16[256,128]{1,0:T(8,128)(2,1)S(1)}, bf16[256,128]{1,0:T(8,128)(2,1)S(1)}, u32[]{:S(2)}, u32[]{:S(2)}) collective-permute-start(bf16[256,128]{1,0:T(8,128)(2,1)S(1)} %get-tuple-element.47.refs_2_.refs_1_), channel_id=1, source_target_pairs={{0,12},{1,13},{2,14},{3,15},{4,8},{5,9},{6,10},{7,11},{8,4},{9,5},... | collective-permute-start | bytes 196616 | tf_op jit(solution)/shard_map/ppermute | solution.py:262
  11.3 1.5 %collective-permute-start.3 = (bf16[1056,128]{1,0:T(8,128)(2,1)S(1)}, bf16[1056,128]{1,0:T(8,128)(2,1)S(1)}, u32[]{:S(2)}, u32[]{:S(2)}) collective-permute-start(bf16[1056,128]{1,0:T(8,128)(2,1)S(1)} %collective-permute-done.refs_0_), channel_id=1, source_target_pairs={{0,1},{1,0},{2,3},{3,2},{4,5},{5,4},{6,7},{7,6},{8,9},{9,8},{10,11... | collective-permute-start | bytes 811016 | tf_op jit(solution)/shard_map/ppermute | solution.py:262
  16.0 2.5 %collective-permute-start.7 = (f32[1024,128]{1,0:T(8,128)S(1)}, f32[1024,128]{1,0:T(8,128)S(1)}, u32[]{:S(2)}, u32[]{:S(2)}) collective-permute-start(f32[1024,128]{1,0:T(8,128)S(1)} %get-tuple-element.73), channel_id=1, source_target_pairs={{0,1},{1,0},{2,3},{3,2},{4,5},{5,4},{6,7},{7,6},{8,9},{9,8},{10,11... | collective-permute-start | bytes 1572872 | tf_op jit(solution)/shard_map/ppermute | solution.py:262
  18.7 8.9 %collective-permute-start.8 = (s16[1056,128]{1,0:T(8,128)(2,1)S(1)}, s16[1056,128]{1,0:T(8,128)(2,1)S(1)}, u32[]{:S(2)}, u32[]{:S(2)}) collective-permute-start(s16[1056,128]{1,0:T(8,128)(2,1)S(1)} %core_sum.1), channel_id=1, source_target_pairs={{0,2},{1,3},{2,0},{3,1},{4,6},{5,7},{6,4},{7,5},{8,10},{9,11},{10,... | collective-permute-start | bytes 811016 | tf_op jit(solution)/shard_map/ppermute | solution.py:262
  19.4 4.3 %collective-permute-start.6 = (s16[1040,128]{1,0:T(8,128)(2,1)S(1)}, s16[1040,128]{1,0:T(8,128)(2,1)S(1)}, u32[]{:S(2)}, u32[]{:S(2)}) collective-permute-start(s16[1040,128]{1,0:T(8,128)(2,1)S(1)} %get-tuple-element.71), channel_id=1, source_target_pairs={{0,1},{1,0},{2,3},{3,2},{4,5},{5,4},{6,7},{7,6},{8,9},{9,8},{10,11... | collective-permute-start | bytes 798728 | tf_op jit(solution)/shard_map/ppermute | solution.py:262
  19.5 9.1 %collective-permute-start.9 = (s16[272,128]{1,0:T(8,128)(2,1)S(1)}, s16[272,128]{1,0:T(8,128)(2,1)S(1)}, u32[]{:S(2)}, u32[]{:S(2)}) collective-permute-start(s16[272,128]{1,0:T(8,128)(2,1)S(1)} %get-tuple-element.82), channel_id=1, source_target_pairs={{0,8},{1,9},{2,10},{3,11},{4,12},{5,13},{6,14},{7,15},{8,0},{9,1},... | collective-permute-start | bytes 208904 | tf_op jit(solution)/shard_map/ppermute | solution.py:262
  22.1 6.8 %collective-permute-start.10 = (s16[272,128]{1,0:T(8,128)(2,1)S(1)}, s16[272,128]{1,0:T(8,128)(2,1)S(1)}, u32[]{:S(2)}, u32[]{:S(2)}) collective-permute-start(s16[272,128]{1,0:T(8,128)(2,1)S(1)} %get-tuple-element.83), channel_id=1, source_target_pairs={{0,12},{1,13},{2,14},{3,15},{4,8},{5,9},{6,10},{7,11},{8,4},{9,5},... | collective-permute-start | bytes 208904 | tf_op jit(solution)/shard_map/ppermute | solution.py:262
  23.4 5.8 %collective-permute-start.11 = (s16[272,128]{1,0:T(8,128)(2,1)S(1)}, s16[272,128]{1,0:T(8,128)(2,1)S(1)}, u32[]{:S(2)}, u32[]{:S(2)}) collective-permute-start(s16[272,128]{1,0:T(8,128)(2,1)S(1)} %get-tuple-element.84), channel_id=1, source_target_pairs={{0,4},{1,5},{2,6},{3,7},{4,0},{5,1},{6,2},{7,3},{8,12},{9,13},{10,... | collective-permute-start | bytes 208904 | tf_op jit(solution)/shard_map/ppermute | solution.py:262

commit v12 on v11

--- a/solution.py
+++ b/solution.py
@@ -296,10 +296,11 @@
     qm_y, gv1 = lax.optimization_barrier((qm_y, gv1))
     qm_yc = swap(qm_y, 1)
     gq_y, gv01, table_y = add([qm_y], [0, 1], None, None, gv0 + gv1, (), "y_01", weight=HEAVY)
-    gq_yc, gv01, table_yc = add([qm_yc], [0, 1], None, None, gv01, near, "yc_01")
-    gq_yc, gv01, late = lax.optimization_barrier((gq_yc, gv01, vds[half:][::-1]))
-    vds[half:] = late[::-1]
-    gq_yc, gv23, _ = add([qm_yc], [2, 3], [table_yc], gq_yc, None, (), "yc_23")
+    empty = jnp.zeros((dim, wide), F32)
+    gq_yc, gvs, _ = add(
+        [qm_yc], [0, 1, 2, 3], None, None, gv01 + [empty] * (chunks - half), near, "yc"
+    )
+    gv01, gv23 = gvs[:half], gvs[half:]
     got_y = swap(gq_yc[0], 1)
     sums, gv23, _ = add(
         [qm_y, *own], [2, 3], [table_y, table], [gq_y[0], *gq_o], gv23, far, "last_23", code_last=True

time: 30.2 us -> 31.5 us (1.043)
  waiting for transfers between devices: 6.58 us -> 8.91 us
  starting transfers between devices: 12.4 us -> 11.5 us
    ppermute x12, waiting for transfers between devices: 6.58 us -> 8.91 us  [swap(): return lax.ppermute(x, 'qry', [(i, i ^ bit) for i in range(n)])]
    ppermute x12, starting transfers between devices: 12.4 us -> 11.5 us  [swap(): return lax.ppermute(x, 'qry', [(i, i ^ bit) for i in range(n)])]
    pallas_call x6 -> x5, Pallas kernels: 7.33 us -> 7.22 us  [grads(): pl.pallas_call(kernel, out_shape=tuple(outs), in_specs=[VMEM] * len(opera...]
  transfers between devices with their start and end apart: 12 -> 12, of which waited for: 6 -> 5; matrix products, arithmetic and copies ran while one was open for 0% -> 0% of each run, Pallas kernels for 24% -> 20%
where the time goes in v12:
time: 31.5 us; the launch traced here: 31.4 us
  starting transfers between devices  11.5 us (37%)
  Pallas kernels  10.2 us (32%)
  waiting for transfers between devices  8.91 us (28%)
  between operations  0.7 us (2%)
    ppermute x12, starting transfers between devices, swap(): return lax.ppermute(x, 'qry', [(i, i ^ bit) for i in range(n)])  11.5 us
    ppermute x12, waiting for transfers between devices, swap(): return lax.ppermute(x, 'qry', [(i, i ^ bit) for i in range(n)])  8.91 us
    pallas_call x5, Pallas kernels, grads(): pl.pallas_call(kernel, out_shape=tuple(outs), in_specs=[VMEM] * len(opera...  7.22 us
    pallas_call x1, Pallas kernels, body(): pl.pallas_call(pack_kernel, out_shape=(jax.ShapeDtypeStruct((rows + pad,...  1.13 us
    pallas_call x1, Pallas kernels, body(): pl.pallas_call(finish_q_kernel, out_shape=row_out, in_specs=[VMEM] * 3, o...  0.94 us
    pallas_call x1, Pallas kernels, body(): pl.pallas_call(finish_v_kernel, out_shape=(vec_out, vec_out), in_specs=[V...  0.78 us
  transfers between devices with their start and end apart: 12, of which 5 were waited for; matrix products, arithmetic and copies ran while one was open for 0% of the time, Pallas kernels for 20%

profile of v12, /device:TPU:0, one launch (start us, length us, event | category | flops | bytes accessed | tf_op | source)
XLA Modules:
  0.0 31.4 jit_solution(9697815997198601053)
XLA Ops:
  0.6 1.1 %pack.1 = (bf16[1040,128]{1,0:T(8,128)(2,1)S(1)}, bf16[1056,128]{1,0:T(8,128)(2,1)S(1)}, bf16[256,128]{1,0:T(8,128)(2,1)S(1)}) custom-call(bf16[1024,128]{1,0:T(8,128)(2,1)} %q_hbm.1, bf16[128,128]{1,0:T(8,128)(2,1)} %v_hbm.1, bf16[128,128]{1,0:T(8,128)(2,1)} %d_hbm.1, s32[4,8]{1,0:T(4,128)} %m_hbm.1), custom_call_target="tpu_custom_call" | custom-call | tf_op jit(solution)/shard_map/pack/pallas_call | solution.py:264
  1.8 3.0 %collective-permute-start = (bf16[1056,128]{1,0:T(8,128)(2,1)S(1)}, bf16[1056,128]{1,0:T(8,128)(2,1)S(1)}, u32[]{:S(2)}, u32[]{:S(2)}) collective-permute-start(bf16[1056,128]{1,0:T(8,128)(2,1)S(1)} %get-tuple-element.38), channel_id=1, source_target_pairs={{0,2},{1,3},{2,0},{3,1},{4,6},{5,7},{6,4},{7,5},{8,10},{9,11},{10,... | collective-permute-start | bytes 811016 | tf_op jit(solution)/shard_map/ppermute | solution.py:262
  4.8 0.0 collective-permute-start.1
  4.8 1.6 %collective-permute-start.2 = (bf16[256,128]{1,0:T(8,128)(2,1)S(1)}, bf16[256,128]{1,0:T(8,128)(2,1)S(1)}, u32[]{:S(2)}, u32[]{:S(2)}) collective-permute-start(bf16[256,128]{1,0:T(8,128)(2,1)S(1)} %get-tuple-element.40.refs_2_.refs_1_), channel_id=1, source_target_pairs={{0,4},{1,5},{2,6},{3,7},{4,0},{5,1},{6,2},{7,3},{8,12},{9,13},{10,... | collective-permute-start | bytes 196616 | tf_op jit(solution)/shard_map/ppermute | solution.py:262
  6.4 2.5 %collective-permute-start.4 = (bf16[256,128]{1,0:T(8,128)(2,1)S(1)}, bf16[256,128]{1,0:T(8,128)(2,1)S(1)}, u32[]{:S(2)}, u32[]{:S(2)}) collective-permute-start(bf16[256,128]{1,0:T(8,128)(2,1)S(1)} %get-tuple-element.40.refs_2_.refs_1_), channel_id=1, source_target_pairs={{0,12},{1,13},{2,14},{3,15},{4,8},{5,9},{6,10},{7,11},{8,4},{9,5},... | collective-permute-start | bytes 196616 | tf_op jit(solution)/shard_map/ppermute | solution.py:262
  8.9 0.1 collective-permute-start.3
  9.0 0.0 collective-permute-done.1.refs_1_.refs_2_
  9.0 1.0 %own_0.1 = (f32[1024,128]{1,0:T(8,128)S(1)}, f32[1024,128]{1,0:T(8,128)S(1)}, f32[128,256]{1,0:T(8,128)S(1)}, f32[4,32,128]{2,1,0:T(8,128)S(1)}) custom-call(bf16[1040,128]{1,0:T(8,128)(2,1)S(1)} %get-tuple-element.39.refs_0_.refs_1_, bf16[1040,128]{1,0:T(8,128)(2,1)S(1)} %collective-permute-done.1.refs_1_.refs_2_, ...), custom_call_target="tpu_custom_call" | custom-call | bytes 1024 | tf_op jit(solution)/shard_map/own_0/pallas_call | solution.py:206
  10.0 0.0 collective-permute-done.2.refs_2_
  10.0 1.0 %own_1.1 = (f32[1024,128]{1,0:T(8,128)S(1)}, f32[1024,128]{1,0:T(8,128)S(1)}, f32[128,256]{1,0:T(8,128)S(1)}) custom-call(bf16[1040,128]{1,0:T(8,128)(2,1)S(1)} %get-tuple-element.39.refs_0_.refs_1_, bf16[1040,128]{1,0:T(8,128)(2,1)S(1)} %collective-permute-done.1.refs_1_.refs_2_, bf16[256,128]{1,0:T(8,128)(2,1)S(1)} %collective-permute-done.2.refs_2_, ...), custom_call_target="tpu_custom_call" | custom-call | bytes 1024 | tf_op jit(solution)/shard_map/own_1/pallas_call | solution.py:206
  11.0 0.3 collective-permute-done.refs_0_
  11.3 0.0 collective-permute-start.5
  11.3 1.0 %y_01.1 = (f32[1024,128]{1,0:T(8,128)S(1)}, f32[128,256]{1,0:T(8,128)S(1)}, f32[128,256]{1,0:T(8,128)S(1)}, f32[4,16,128]{2,1,0:T(8,128)S(1)}) custom-call(bf16[1056,128]{1,0:T(8,128)(2,1)S(1)} %collective-permute-done.refs_0_, bf16[256,128]{1,0:T(8,128)(2,1)S(1)} %get-tuple-element.40.refs_2_.refs_1_, bf16[256,128]{1,0:T(8,128)(2,1)S(1)} %collective-permute-done.2.refs_2_, ...), custom_call_target="tpu_custom_call" | custom-call | flops 8589934592 | bytes 1024 | tf_op jit(solution)/shard_map/y_01/pallas_call | solution.py:206
  12.3 0.9 %collective-permute-done.4.refs_4_ = bf16[256,128]{1,0:T(8,128)(2,1)S(1)} collective-permute-done((bf16[256,128]{1,0:T(8,128)(2,1)S(1)}, bf16[256,128]{1,0:T(8,128)(2,1)S(1)}, u32[]{:S(2)}, u32[]{:S(2)}) %collective-permute-start.4) | collective-permute-done | bytes 65568 | tf_op jit(solution)/shard_map/ppermute | solution.py:262
  13.2 2.5 %collective-permute-done.3.refs_3_ = bf16[256,128]{1,0:T(8,128)(2,1)S(1)} collective-permute-done((bf16[256,128]{1,0:T(8,128)(2,1)S(1)}, bf16[256,128]{1,0:T(8,128)(2,1)S(1)}, u32[]{:S(2)}, u32[]{:S(2)}) %collective-permute-start.3) | collective-permute-done | bytes 65568 | tf_op jit(solution)/shard_map/ppermute | solution.py:262
  15.7 0.0 collective-permute-done.5.refs_0_
  15.7 1.8 %yc.1 = (f32[1024,128]{1,0:T(8,128)S(1)}, f32[128,256]{1,0:T(8,128)S(1)}, s16[272,128]{1,0:T(8,128)(2,1)S(1)}, f32[128,256]{1,0:T(8,128)S(1)}, f32[128,256]{1,0:T(8,128)S(1)}, /*index=5*/f32[4,16,128]{2,1,0:T(8,128)}) custom-call(bf16[1056,128]{1,0:T(8,128)(2,1)S(1)} %collective-permute-done.5.refs_0_, ...), custom_call_target="tpu_custom_call" | custom-call | flops 1048576 | bytes 1024 | tf_op jit(solution)/shard_map/yc/pallas_call | solution.py:206
  17.5 0.1 collective-permute-start.7
  17.6 2.4 %last_23.1 = (f32[1024,128]{1,0:T(8,128)S(1)}, f32[1024,128]{1,0:T(8,128)S(1)}, s16[1040,128]{1,0:T(8,128)(2,1)S(1)}, s16[272,128]{1,0:T(8,128)(2,1)S(1)}, s16[272,128]{1,0:T(8,128)(2,1)S(1)}) custom-call(bf16[1056,128]{1,0:T(8,128)(2,1)S(1)} %collective-permute-done.refs_0_, bf16[1040,128]{1,0:T(8,128)(2,1)S(1)} %get-tuple-element.39.refs_0_.refs_1_, ...), custom_call_target="tpu_custom_call" | custom-call | flops 1572864 | bytes 1024 | tf_op jit(solution)/shard_map/last_23/pallas_call | solution.py:206
  20.1 0.0 collective-permute-done.7.got_y_ref
  20.1 0.1 core_sum.1
  20.2 0.6 %collective-permute-start.8 = (s16[1056,128]{1,0:T(8,128)(2,1)S(1)}, s16[1056,128]{1,0:T(8,128)(2,1)S(1)}, u32[]{:S(2)}, u32[]{:S(2)}) collective-permute-start(s16[1056,128]{1,0:T(8,128)(2,1)S(1)} %core_sum.1), channel_id=1, source_target_pairs={{0,2},{1,3},{2,0},{3,1},{4,6},{5,7},{6,4},{7,5},{8,10},{9,11},{10,... | collective-permute-start | bytes 811016 | tf_op jit(solution)/shard_map/ppermute | solution.py:262
  20.8 0.1 collective-permute-start.6
  20.9 1.0 %collective-permute-start.9 = (s16[272,128]{1,0:T(8,128)(2,1)S(1)}, s16[272,128]{1,0:T(8,128)(2,1)S(1)}, u32[]{:S(2)}, u32[]{:S(2)}) collective-permute-start(s16[272,128]{1,0:T(8,128)(2,1)S(1)} %get-tuple-element.68), channel_id=1, source_target_pairs={{0,8},{1,9},{2,10},{3,11},{4,12},{5,13},{6,14},{7,15},{8,0},{9,1},... | collective-permute-start | bytes 208904 | tf_op jit(solution)/shard_map/ppermute | solution.py:262
  21.9 1.7 %collective-permute-start.10 = (s16[272,128]{1,0:T(8,128)(2,1)S(1)}, s16[272,128]{1,0:T(8,128)(2,1)S(1)}, u32[]{:S(2)}, u32[]{:S(2)}) collective-permute-start(s16[272,128]{1,0:T(8,128)(2,1)S(1)} %get-tuple-element.69), channel_id=1, source_target_pairs={{0,12},{1,13},{2,14},{3,15},{4,8},{5,9},{6,10},{7,11},{8,4},{9,5},... | collective-permute-start | bytes 208904 | tf_op jit(solution)/shard_map/ppermute | solution.py:262
  23.6 0.8 %collective-permute-start.11 = (s16[272,128]{1,0:T(8,128)(2,1)S(1)}, s16[272,128]{1,0:T(8,128)(2,1)S(1)}, u32[]{:S(2)}, u32[]{:S(2)}) collective-permute-start(s16[272,128]{1,0:T(8,128)(2,1)S(1)} %get-tuple-element.70), channel_id=1, source_target_pairs={{0,4},{1,5},{2,6},{3,7},{4,0},{5,1},{6,2},{7,3},{8,12},{9,13},{10,... | collective-permute-start | bytes 208904 | tf_op jit(solution)/shard_map/ppermute | solution.py:262
  24.5 0.0 collective-permute-done.6.got_own_ref
  24.5 4.7 %collective-permute-done.8.got_ref = s16[1056,128]{1,0:T(8,128)(2,1)S(1)} collective-permute-done((s16[1056,128]{1,0:T(8,128)(2,1)S(1)}, s16[1056,128]{1,0:T(8,128)(2,1)S(1)}, u32[]{:S(2)}, u32[]{:S(2)}) %collective-permute-start.8) | collective-permute-done | bytes 270368 | tf_op jit(solution)/shard_map/ppermute | solution.py:262
  29.1 0.9 %finish_q.1 = f32[1024,128]{1,0:T(8,128)} custom-call(f32[1024,128]{1,0:T(8,128)S(1)} %get-tuple-element.56.own_ref, s16[1040,128]{1,0:T(8,128)(2,1)S(1)} %collective-permute-done.6.got_own_ref, s16[1056,128]{1,0:T(8,128)(2,1)S(1)} %collective-permute-done.8.got_ref), custom_call_target="tpu_custom_call" | custom-call | tf_op jit(solution)/shard_map/finish_q/pallas_call | solution.py:325
  30.0 0.0 collective-permute-done.9.refs_0_
  30.0 0.0 collective-permute-done.10.refs_1_
  30.1 0.5 %collective-permute-done.11.refs_2_ = s16[272,128]{1,0:T(8,128)(2,1)S(1)} collective-permute-done((s16[272,128]{1,0:T(8,128)(2,1)S(1)}, s16[272,128]{1,0:T(8,128)(2,1)S(1)}, u32[]{:S(2)}, u32[]{:S(2)}) %collective-permute-start.11) | collective-permute-done | bytes 69664 | tf_op jit(solution)/shard_map/ppermute | solution.py:262
  30.6 0.8 %finish_v.1 = (f32[128,128]{1,0:T(8,128)}, f32[128,128]{1,0:T(8,128)}) custom-call(f32[128,256]{1,0:T(8,128)S(1)} %get-tuple-element.67.term_ref, s16[272,128]{1,0:T(8,128)(2,1)S(1)} %collective-permute-done.9.refs_0_, s16[272,128]{1,0:T(8,128)(2,1)S(1)} %collective-permute-done.10.refs_1_, s16[272,128]{1,0:T(8,128)(2,1)S(1)} %collective-permute-done.11.refs_2_), custom_call_target="tpu_custom_call" | custom-call | tf_op jit(solution)/shard_map/finish_v/pallas_call | solution.py:335
  (1 shorter events, 0.0 us)
Async XLA Ops:
  1.8 9.5 %collective-permute-start = (bf16[1056,128]{1,0:T(8,128)(2,1)S(1)}, bf16[1056,128]{1,0:T(8,128)(2,1)S(1)}, u32[]{:S(2)}, u32[]{:S(2)}) collective-permute-start(bf16[1056,128]{1,0:T(8,128)(2,1)S(1)} %get-tuple-element.38), channel_id=1, source_target_pairs={{0,2},{1,3},{2,0},{3,1},{4,6},{5,7},{6,4},{7,5},{8,10},{9,11},{10,... | collective-permute-start | bytes 811016 | tf_op jit(solution)/shard_map/ppermute | solution.py:262
  4.8 4.2 %collective-permute-start.1 = (bf16[1040,128]{1,0:T(8,128)(2,1)S(1)}, bf16[1040,128]{1,0:T(8,128)(2,1)S(1)}, u32[]{:S(2)}, u32[]{:S(2)}) collective-permute-start(bf16[1040,128]{1,0:T(8,128)(2,1)S(1)} %get-tuple-element.39.refs_0_.refs_1_), channel_id=1, source_target_pairs={{0,1},{1,0},{2,3},{3,2},{4,5},{5,4},{6,7},{7,6},{8,9},{9,8},{10,11... | collective-permute-start | bytes 798728 | tf_op jit(solution)/shard_map/ppermute | solution.py:262
  4.8 5.2 %collective-permute-start.2 = (bf16[256,128]{1,0:T(8,128)(2,1)S(1)}, bf16[256,128]{1,0:T(8,128)(2,1)S(1)}, u32[]{:S(2)}, u32[]{:S(2)}) collective-permute-start(bf16[256,128]{1,0:T(8,128)(2,1)S(1)} %get-tuple-element.40.refs_2_.refs_1_), channel_id=1, source_target_pairs={{0,4},{1,5},{2,6},{3,7},{4,0},{5,1},{6,2},{7,3},{8,12},{9,13},{10,... | collective-permute-start | bytes 196616 | tf_op jit(solution)/shard_map/ppermute | solution.py:262
  6.4 6.8 %collective-permute-start.4 = (bf16[256,128]{1,0:T(8,128)(2,1)S(1)}, bf16[256,128]{1,0:T(8,128)(2,1)S(1)}, u32[]{:S(2)}, u32[]{:S(2)}) collective-permute-start(bf16[256,128]{1,0:T(8,128)(2,1)S(1)} %get-tuple-element.40.refs_2_.refs_1_), channel_id=1, source_target_pairs={{0,12},{1,13},{2,14},{3,15},{4,8},{5,9},{6,10},{7,11},{8,4},{9,5},... | collective-permute-start | bytes 196616 | tf_op jit(solution)/shard_map/ppermute | solution.py:262
  8.9 6.8 %collective-permute-start.3 = (bf16[256,128]{1,0:T(8,128)(2,1)S(1)}, bf16[256,128]{1,0:T(8,128)(2,1)S(1)}, u32[]{:S(2)}, u32[]{:S(2)}) collective-permute-start(bf16[256,128]{1,0:T(8,128)(2,1)S(1)} %get-tuple-element.40.refs_2_.refs_1_), channel_id=1, source_target_pairs={{0,8},{1,9},{2,10},{3,11},{4,12},{5,13},{6,14},{7,15},{8,0},{9,1},... | collective-permute-start | bytes 196616 | tf_op jit(solution)/shard_map/ppermute | solution.py:262
  11.3 4.4 %collective-permute-start.5 = (bf16[1056,128]{1,0:T(8,128)(2,1)S(1)}, bf16[1056,128]{1,0:T(8,128)(2,1)S(1)}, u32[]{:S(2)}, u32[]{:S(2)}) collective-permute-start(bf16[1056,128]{1,0:T(8,128)(2,1)S(1)} %collective-permute-done.refs_0_), channel_id=1, source_target_pairs={{0,1},{1,0},{2,3},{3,2},{4,5},{5,4},{6,7},{7,6},{8,9},{9,8},{10,11... | collective-permute-start | bytes 811016 | tf_op jit(solution)/shard_map/ppermute | solution.py:262
  17.5 2.6 %collective-permute-start.7 = (f32[1024,128]{1,0:T(8,128)S(1)}, f32[1024,128]{1,0:T(8,128)S(1)}, u32[]{:S(2)}, u32[]{:S(2)}) collective-permute-start(f32[1024,128]{1,0:T(8,128)S(1)} %get-tuple-element.59), channel_id=1, source_target_pairs={{0,1},{1,0},{2,3},{3,2},{4,5},{5,4},{6,7},{7,6},{8,9},{9,8},{10,11... | collective-permute-start | bytes 1572872 | tf_op jit(solution)/shard_map/ppermute | solution.py:262
  20.2 8.9 %collective-permute-start.8 = (s16[1056,128]{1,0:T(8,128)(2,1)S(1)}, s16[1056,128]{1,0:T(8,128)(2,1)S(1)}, u32[]{:S(2)}, u32[]{:S(2)}) collective-permute-start(s16[1056,128]{1,0:T(8,128)(2,1)S(1)} %core_sum.1), channel_id=1, source_target_pairs={{0,2},{1,3},{2,0},{3,1},{4,6},{5,7},{6,4},{7,5},{8,10},{9,11},{10,... | collective-permute-start | bytes 811016 | tf_op jit(solution)/shard_map/ppermute | solution.py:262
  20.8 3.7 %collective-permute-start.6 = (s16[1040,128]{1,0:T(8,128)(2,1)S(1)}, s16[1040,128]{1,0:T(8,128)(2,1)S(1)}, u32[]{:S(2)}, u32[]{:S(2)}) collective-permute-start(s16[1040,128]{1,0:T(8,128)(2,1)S(1)} %get-tuple-element.57), channel_id=1, source_target_pairs={{0,1},{1,0},{2,3},{3,2},{4,5},{5,4},{6,7},{7,6},{8,9},{9,8},{10,11... | collective-permute-start | bytes 798728 | tf_op jit(solution)/shard_map/ppermute | solution.py:262
  20.9 9.1 %collective-permute-start.9 = (s16[272,128]{1,0:T(8,128)(2,1)S(1)}, s16[272,128]{1,0:T(8,128)(2,1)S(1)}, u32[]{:S(2)}, u32[]{:S(2)}) collective-permute-start(s16[272,128]{1,0:T(8,128)(2,1)S(1)} %get-tuple-element.68), channel_id=1, source_target_pairs={{0,8},{1,9},{2,10},{3,11},{4,12},{5,13},{6,14},{7,15},{8,0},{9,1},... | collective-permute-start | bytes 208904 | tf_op jit(solution)/shard_map/ppermute | solution.py:262
  21.9 8.1 %collective-permute-start.10 = (s16[272,128]{1,0:T(8,128)(2,1)S(1)}, s16[272,128]{1,0:T(8,128)(2,1)S(1)}, u32[]{:S(2)}, u32[]{:S(2)}) collective-permute-start(s16[272,128]{1,0:T(8,128)(2,1)S(1)} %get-tuple-element.69), channel_id=1, source_target_pairs={{0,12},{1,13},{2,14},{3,15},{4,8},{5,9},{6,10},{7,11},{8,4},{9,5},... | collective-permute-start | bytes 208904 | tf_op jit(solution)/shard_map/ppermute | solution.py:262
  23.6 7.0 %collective-permute-start.11 = (s16[272,128]{1,0:T(8,128)(2,1)S(1)}, s16[272,128]{1,0:T(8,128)(2,1)S(1)}, u32[]{:S(2)}, u32[]{:S(2)}) collective-permute-start(s16[272,128]{1,0:T(8,128)(2,1)S(1)} %get-tuple-element.70), channel_id=1, source_target_pairs={{0,4},{1,5},{2,6},{3,7},{4,0},{5,1},{6,2},{7,3},{8,12},{9,13},{10,... | collective-permute-start | bytes 208904 | tf_op jit(solution)/shard_map/ppermute | solution.py:262
